TPU v7x, 32 devices: a whole 2x2x4 slice. The times are simulated.
32 devices in a mesh: pipe: 8 (over z, x), tensor: 4 (over y, core).
Axes of the slice: x: 2, y: 2, z: 4, core: 2. Of those that a mesh axis runs over, the one named last changes fastest.
Arguments:
- inputs: bfloat16 [2, 4, 32, 3584], replicated
- cotangent: bfloat16 [2, 4, 32, 3584], replicated, may hold values from -0.59765625 to 0.59765625
- section_weights: bfloat16 [8, 2, 3, 3584, 1024], P('pipe', None, None, None, 'tensor'), as said below
- section_gains: float32 [8, 2, 3584], P('pipe'), as said below
Outputs:
- section_grads: bfloat16 [8, 3, 3584, 1024], P('pipe', None, None, 'tensor')
Inputs may be any that keep to these rules, and one draw needn't show every extreme that they name: section_weights[r * 4 + k, 1] is an exact copy of section_weights[r * 4 + 3 - k, 0] for every r and k, and section_weights[r * 4 + k] is the same for every r. section_gains[r * 4 + k, 1] is an exact copy of section_gains[r * 4 + 3 - k, 0] for every r and k, and section_gains[r * 4 + k] is the same for every r.
All inputs are finite; a program needn't handle non-finite values.
Results may differ from a plain program's by a relative error of at most 0.035.
Values may be sent and summed in bfloat16 or wider, within the bound.
No kernel may reach another device: no remote copies, remote signals or barrier semaphores. Data moves between devices by JAX's collectives and lax.ppermute only.
A program may use at most 128 MiB of HBM per device.

v0:
```python
import functools

import jax
import jax.numpy as jnp
from jax import lax
from jax.experimental import pallas as pl
from jax.experimental.pallas import tpu as pltpu
from jax.sharding import PartitionSpec as P

REPL = 2
EPS = 1e-06
BF = jnp.bfloat16
F32 = jnp.float32
SMEM_SPEC = pl.BlockSpec(memory_space=pltpu.SMEM)
VMEM_SPEC = pl.BlockSpec(memory_space=pltpu.VMEM)
HBM_SPEC = pl.BlockSpec(memory_space=pltpu.HBM)
MIB = 1024 * 1024
NEAR, OUTER, FIRST_CHIP, KIND, OWN, TOP, BOTTOM = 1, 2, 3, 4, 5, 13, 21


def chunk_of(features):
    for size in (512, 256, 128):
        if features % size == 0:
            return size
    return features


def norm_rows(rows, gain_row):
    widened = rows.astype(F32)
    root = jnp.sqrt(jnp.mean(widened * widened, axis=-1, keepdims=True) + EPS)
    unit = widened / root
    return unit, root, (unit * gain_row).astype(BF)


def dot(left, right):
    return jnp.dot(left, right, preferred_element_type=F32)


def dot_last(left, right):
    return lax.dot_general(left, right, (((1,), (1,)), ((), ())), preferred_element_type=F32)


def dot_first(left, right):
    return lax.dot_general(left, right, (((0,), (0,)), ((), ())), preferred_element_type=F32)


def is_set(flags_ref, index, value=1):
    if len(flags_ref.shape) == 1:
        return flags_ref[index] == value
    return flags_ref[index : index + 1, 0:1] == value


def gain_at(flags_ref, gains_ref, part):
    return jnp.where(is_set(flags_ref, NEAR, 1 - part), gains_ref[0:1], gains_ref[1:2])


def own_index(flags_ref, part):
    return jnp.where(flags_ref[NEAR] == 1 - part, 0, 1)


def choose(condition, first, second):
    kept = first.dtype
    return jnp.where(condition, first.astype(F32), second.astype(F32)).astype(kept)


def weight_copies(which, w_ref, w_buf, sems, size):
    features = w_buf.shape[1]
    copies = {}
    for matrix in range(3):
        for k in range(features // size):
            rows = pl.ds(k * size, size)
            copies[matrix, k] = pltpu.make_async_copy(
                w_ref.at[which, matrix, rows], w_buf.at[matrix, rows], sems.at[matrix, k]
            )
    return copies


def fill_normed(xm_ref, xo_ref, gain, normed):
    half = xm_ref.shape[0]
    normed[:half] = norm_rows(xm_ref[...], gain)[2]
    normed[half:] = norm_rows(xo_ref[...], gain)[2]


def gate_upper(copies, w_buf, normed, size):
    gate = upper = None
    for k in range(w_buf.shape[1] // size):
        cols = pl.ds(k * size, size)
        if copies:
            copies[0, k].wait()
            copies[1, k].wait()
        block = normed[:, cols]
        gate_k = dot(block, w_buf[0, cols])
        upper_k = dot(block, w_buf[1, cols])
        gate = gate_k if gate is None else gate + gate_k
        upper = upper_k if upper is None else upper + upper_k
    return gate, upper


def forward_math(copies, xm_ref, xo_ref, gain, w_buf, pm_ref, po_ref, normed):
    size = chunk_of(w_buf.shape[1])
    half = xm_ref.shape[0]
    fill_normed(xm_ref, xo_ref, gain, normed)
    gate, upper = gate_upper(copies, w_buf, normed, size)
    active = (gate * jax.nn.sigmoid(gate) * upper).astype(BF)
    for k in range(w_buf.shape[1] // size):
        cols = pl.ds(k * size, size)
        if copies:
            copies[2, k].wait()
        part = dot_last(active, w_buf[2, cols]).astype(BF)
        pm_ref[:, cols] = part[:half]
        po_ref[:, cols] = part[half:]
    return gate, upper


def first_kernel(
    flags_ref, rows_ref, gains_ref, w_ref,
    pm_ref, po_ref, gate_ref, upper_ref, w_buf, xm_ref, xo_ref, marks_ref, normed, gains_buf, sems, row_sems
):
    size = chunk_of(w_buf.shape[1])
    moves = [
        pltpu.make_async_copy(rows_ref.at[flags_ref[OWN + i]], ref, row_sems.at[i])
        for i, ref in enumerate((xm_ref, xo_ref))
    ]
    moves.append(pltpu.make_async_copy(gains_ref, gains_buf, row_sems.at[2]))
    for move in moves:
        move.start()
    for i in range(marks_ref.shape[0]):
        marks_ref[i : i + 1] = jnp.full((1, marks_ref.shape[1]), flags_ref[i], jnp.int32)
    for move in moves:
        move.wait()
    copies = weight_copies(own_index(flags_ref, 0), w_ref, w_buf, sems, size)
    for group in ((0, 1), (2,)):
        for k in range(w_buf.shape[1] // size):
            for matrix in group:
                copies[matrix, k].start()
    gain = gain_at(flags_ref, gains_buf, 0)
    gate_ref[...], upper_ref[...] = forward_math(copies, xm_ref, xo_ref, gain, w_buf, pm_ref, po_ref, normed)


def load_kernel(flags_ref, rows_ref, cot_ref, w_ref, w_buf, xs_ref, us_ref, um_ref, uo_ref, sems, row_sems):
    copies = list(weight_copies(own_index(flags_ref, 1), w_ref, w_buf, sems, w_buf.shape[1]).values())
    pieces, rows = xs_ref.shape[:2]
    group = rows // 2
    for i in range(pieces):
        copies.append(pltpu.make_async_copy(cot_ref.at[flags_ref[OWN + i]], us_ref.at[i], row_sems.at[0, i]))
        for half, base in enumerate((TOP, BOTTOM)):
            part = pl.ds(half * group, group)
            copies.append(
                pltpu.make_async_copy(
                    rows_ref.at[flags_ref[base + i], part], xs_ref.at[i, part], row_sems.at[1 + half, i]
                )
            )
    for i, ref in enumerate((um_ref, uo_ref)):
        copies.append(pltpu.make_async_copy(cot_ref.at[flags_ref[OWN + i]], ref, row_sems.at[3, i]))
    for copy in copies:
        copy.start()
    for copy in copies:
        copy.wait()


def forward_kernel(part, live, flags_ref, xm_ref, xo_ref, gains_ref, w_buf, *refs):
    *old, pm_ref, po_ref, gate_ref, upper_ref, xms_ref, xos_ref, normed = refs
    gain = gain_at(flags_ref, gains_ref, part)
    gate, upper = forward_math(None, xm_ref, xo_ref, gain, w_buf, pm_ref, po_ref, normed)
    found = (gate, upper, xm_ref[...], xo_ref[...])
    outs = (gate_ref, upper_ref, xms_ref, xos_ref)
    if old:
        is_live = is_set(flags_ref, KIND, live)
        found = [choose(is_live, a, b[...]) for a, b in zip(found, old)]
    for out, value in zip(outs, found):
        out[...] = value


def active_gradient(um_ref, uo_ref, w_buf):
    size = chunk_of(w_buf.shape[1])
    d_active = None
    for k in range(w_buf.shape[1] // size):
        cols = pl.ds(k * size, size)
        block = jnp.concatenate([um_ref[:, cols], uo_ref[:, cols]], axis=0)
        part = dot(block, w_buf[2, cols])
        d_active = part if d_active is None else d_active + part
    return d_active


def backward_math(d_active, gate, upper, w_buf, pm_ref, po_ref):
    size = chunk_of(w_buf.shape[1])
    half = pm_ref.shape[0]
    sig = jax.nn.sigmoid(gate)
    d_gate = (d_active * upper * (sig * (1.0 + gate * (1.0 - sig)))).astype(BF)
    d_upper = (d_active * (gate * sig)).astype(BF)
    for k in range(w_buf.shape[1] // size):
        cols = pl.ds(k * size, size)
        part = (dot_last(d_gate, w_buf[0, cols]) + dot_last(d_upper, w_buf[1, cols])).astype(BF)
        pm_ref[:, cols] = part[:half]
        po_ref[:, cols] = part[half:]


def cotangent_kernel(um_ref, uo_ref, w_buf, d_ref):
    d_ref[...] = active_gradient(um_ref, uo_ref, w_buf)


def turn_kernel(
    flags_ref, d_ref, xm_ref, xo_ref, oldm_ref, oldo_ref, gains_ref, w_buf, pm_ref, po_ref, latem_ref, lateo_ref, normed
):
    fill_normed(xm_ref, xo_ref, gain_at(flags_ref, gains_ref, 1), normed)
    gate, upper = gate_upper(None, w_buf, normed, chunk_of(w_buf.shape[1]))
    backward_math(d_ref[...], gate, upper, w_buf, pm_ref, po_ref)
    is_outer = is_set(flags_ref, OUTER)
    latem_ref[...] = choose(is_outer, xm_ref[...], oldm_ref[...])
    lateo_ref[...] = choose(is_outer, xo_ref[...], oldo_ref[...])


def backward_kernel(live, has_old, has_late, flags_ref, um_ref, uo_ref, gate_ref, upper_ref, w_buf, *refs):
    refs = list(refs)
    old = [refs.pop(0) for _ in range(2)] if has_old else []
    late = refs.pop(0) if has_late else None
    pm_ref, po_ref, ums_ref, uos_ref = refs[:4]
    backward_math(active_gradient(um_ref, uo_ref, w_buf), gate_ref[...], upper_ref[...], w_buf, pm_ref, po_ref)
    found = [um_ref[...], uo_ref[...]]
    if old:
        is_live = is_set(flags_ref, KIND, live)
        found = [choose(is_live, a, b[...]) for a, b in zip(found, old)]
    ums_ref[...], uos_ref[...] = found
    if has_late:
        refs[4][...] = choose(is_set(flags_ref, OUTER), late[...], found[0])


def hold_kernel(part, backward, flags_ref, pm_ref, recv_ref, base_ref, *refs):
    summed = pm_ref[...].astype(F32) + recv_ref[...].astype(F32)
    if backward:
        state_ref, gains_ref, *outs = refs
        gain = gain_at(flags_ref, gains_ref, part)
        unit, root, _ = norm_rows(state_ref[...], gain)
        d_unit = summed * gain
        summed = (d_unit - unit * jnp.mean(d_unit * unit, axis=-1, keepdims=True)) / root
    else:
        outs = refs
    base = jnp.where(is_set(flags_ref, FIRST_CHIP), base_ref[...].astype(F32), 0.0)
    value = (summed + base).astype(BF)
    rows = value.shape[0] // len(outs)
    for i, out in enumerate(outs):
        out[...] = value[i * rows : (i + 1) * rows]


def sides_kernel(marks_ref, early_ref, late_ref, same_ref, opposite_ref):
    is_near = is_set(marks_ref, NEAR)
    same_ref[...] = choose(is_near, early_ref[...], late_ref[...])
    opposite_ref[...] = choose(is_near, late_ref[...], early_ref[...])


def stack_kernel(*refs):
    *sources, out_ref = refs
    rows = sources[0].shape[0]
    for i, source in enumerate(sources):
        out_ref[i * rows : (i + 1) * rows] = source[...]


def fill_rows(target, sources, change=None):
    start = 0
    for source in sources:
        rows = source[...]
        target[start : start + rows.shape[0]] = change(rows) if change else rows
        start += rows.shape[0]


def last_kernel(marks_ref, mine_ref, early_ref, first_ref, second_ref):
    is_near = is_set(marks_ref, NEAR)
    mine, early = mine_ref[...], early_ref[...]
    first_ref[...] = choose(is_near, mine, early)
    second_ref[...] = choose(is_near, early, mine)


def sum_kernel(*refs):
    *terms, out = refs
    count = len(terms) // 2
    rows = out.shape[0] // count
    for i in range(count):
        total = terms[i][...].astype(F32) + terms[count + i][...].astype(F32)
        out[i * rows : (i + 1) * rows] = total.astype(BF)


def own_first_kernel(
    flags_ref, xs_ref, em_ref, eo_ref, lm_ref, lo_ref, p0, p1, p2, p3, q0, q1, q2, q3, gains_ref, w_ref,
    turned_ref, left_ref, right_ref, active_ref, w_buf, normed, sems
):
    features = w_buf.shape[1]
    size = chunk_of(features)
    count = features // size
    copies = {}
    for k in range(count):
        rows = pl.ds(k * size, size)
        for matrix in range(2):
            copies[matrix, k] = pltpu.make_async_copy(
                w_ref.at[0, matrix, rows], w_buf.at[matrix, rows], sems.at[matrix, k]
            )
            copies[matrix, k].start()
    gain = gains_ref[0:1]
    pieces, half = xs_ref.shape[:2]
    is_near = flags_ref[NEAR] == 1
    is_outer = flags_ref[OUTER] == 1
    inputs_used = jnp.logical_and(is_near, is_outer)

    def put(piece, rows):
        normed[piece * half : (piece + 1) * half] = norm_rows(rows, gain)[2]

    @pl.when(inputs_used)
    def _():
        for piece in range(pieces):
            put(piece, xs_ref[piece])

    cases = (
        (False, True, (em_ref, eo_ref, p0, p1, p2, p3)),
        (False, False, (lm_ref, lo_ref, p0, p1, p2, p3)),
        (True, False, (lm_ref, lo_ref, q0, q1, q2, q3)),
    )
    for outer, near, sources in cases:

        @pl.when(jnp.logical_and(is_outer == outer, is_near == near))
        def _(sources=sources):
            fill_rows(normed, sources, lambda rows: norm_rows(rows, gain)[2])

    gate, upper = gate_upper(copies, w_buf, normed, size)
    sig = jax.nn.sigmoid(gate)
    smooth = gate * sig
    left_ref[...] = upper * (sig * (1.0 + gate * (1.0 - sig)))
    right_ref[...] = smooth
    active_ref[...] = (smooth * upper).astype(BF)
    for k in range(count):
        cols = pl.ds(k * size, size)
        turned_ref[cols] = normed[:, cols].T


def own_last_kernel(flags_ref, us_ref, *refs):
    refs = list(refs)

    def take(count):
        return [refs.pop(0) for _ in range(count)]

    direct, early, late, arrived = take(2), take(2), take(2), take(4)
    turned_ref, left_ref, right_ref, active_ref, early_ref, late_ref = take(6)
    out_ref, u_buf, d_act, out_buf, sems = take(5)
    features = turned_ref.shape[0]
    size = chunk_of(features)
    count = features // size
    pieces, half = us_ref.shape[:2]
    is_near = flags_ref[NEAR] == 1
    is_outer = flags_ref[OUTER] == 1

    def fill(sources, w_ref):
        fill_rows(u_buf, sources)
        total = None
        for k in range(count):
            cols = pl.ds(k * size, size)
            part = dot(u_buf[:, cols], w_ref[2, cols])
            total = part if total is None else total + part
        d_act[...] = total

    half = early[0].shape[0]

    def lanes(source, *places):
        return [source.at[pl.ds(i * half, half)] for i in places]

    near_sources = early + lanes(direct[0], 0, 3, 2) + lanes(direct[1], 0, 3, 2)
    cases = (
        (True, True, direct, early_ref),
        (True, False, [us_ref.at[i] for i in range(pieces)], late_ref),
        (False, True, near_sources, early_ref),
        (False, False, late + arrived, late_ref),
    )
    for outer, near, sources, w_ref in cases:

        @pl.when(jnp.logical_and(is_outer == outer, is_near == near))
        def _(sources=sources, w_ref=w_ref):
            fill(sources, w_ref)

    copies = []

    def send(matrix, k):
        rows = pl.ds(k * size, size)
        copy = pltpu.make_async_copy(out_buf.at[matrix, rows], out_ref.at[0, matrix, rows], sems.at[matrix, k])
        copy.start()
        copies.append(copy)

    active = active_ref[...]
    d_active = d_act[...]
    for k in range(count):
        cols = pl.ds(k * size, size)
        out_buf[2, cols] = dot_first(u_buf[:, cols], active).astype(BF)
        send(2, k)
    d_gate = (d_active * left_ref[...]).astype(BF)
    d_upper = (d_active * right_ref[...]).astype(BF)
    for k in range(count):
        cols = pl.ds(k * size, size)
        turned = turned_ref[cols]
        out_buf[0, cols] = dot(turned, d_gate).astype(BF)
        send(0, k)
        out_buf[1, cols] = dot(turned, d_upper).astype(BF)
        send(1, k)
    for copy in copies:
        copy.wait()


def call(kernel, name, operands, outs, scratch, limit, flops, moved, hbm=(), out_hbm=False, smem=(0,)):
    specs = [
        SMEM_SPEC if i in smem else HBM_SPEC if i in hbm else VMEM_SPEC for i in range(len(operands))
    ]
    out_spec = HBM_SPEC if out_hbm else VMEM_SPEC
    results = pl.pallas_call(
        kernel,
        out_shape=outs,
        in_specs=specs,
        out_specs=[out_spec] * len(outs),
        scratch_shapes=scratch,
        cost_estimate=pl.CostEstimate(flops=flops, bytes_accessed=moved, transcendentals=0),
        compiler_params=pltpu.CompilerParams(vmem_limit_bytes=limit * MIB),
        name=name,
    )(*operands)
    return list(results)


def body(inputs, cotangent, section_weights, section_gains):
    sections = lax.axis_size("pipe") // REPL
    ranks = lax.axis_size("tensor")
    pipe = lax.axis_index("pipe")
    tensor = lax.axis_index("tensor")
    position = pipe % sections
    replica = pipe // sections
    middle = sections // 2
    near = position < middle
    side = jnp.where(near, 0, 1)
    kind = jnp.where(near, position, sections - 1 - position)
    core = tensor % 2
    chip = tensor // 2
    rows, features = inputs.shape[2:]
    narrow = section_weights.shape[-1]
    group = rows // 2
    chunks = features // chunk_of(features)
    weights = pltpu.with_memory_space_constraint(section_weights[0], pltpu.HBM)
    blocks = pltpu.with_memory_space_constraint(inputs.reshape(-1, rows, features), pltpu.HBM)
    cot_blocks = pltpu.with_memory_space_constraint(cotangent.reshape(-1, rows, features), pltpu.HBM)
    gains = section_gains[0]
    core_swap = [(i, i ^ 1) for i in range(ranks)]
    chip_swap = [(i, (i + 2) % ranks) for i in range(ranks)]

    def spot(across, end, batch):
        return (((replica + across) % REPL) * 2 + end) * 2 + batch

    pairs = ((0, 0), (0, 1), (1, 0), (1, 1))
    pairs_of = ((1, 0), (0, 1), (1, 1))
    own = [spot(across, side ^ turn, batch) for batch in (core, 1 - core) for across, turn in pairs]
    own = [own[i] for i in (0, 4, 1, 2, 3, 5, 6, 7)]
    top = [spot(across, end, batch) for batch in (core, 1 - core) for across, end in pairs]
    bottom = [spot(across, 1 - end, batch) for batch in (core, 1 - core) for across, end in pairs]
    flags = [side, near, kind == 0, chip == 0, kind] + own + top + bottom
    flags = jnp.stack([jnp.asarray(flag).astype(jnp.int32) for flag in flags])

    def swap_core(block):
        return lax.ppermute(block, "tensor", core_swap)

    def swap_chip(block):
        return lax.ppermute(block, "tensor", chip_swap)

    def place(copy, end, c, rank):
        at = c if end == 0 else sections - 1 - c
        return (copy * sections + at) * ranks + rank

    def completed(moves):
        per_copy = sections * ranks
        target = dict(moves)
        back = {end: start for start, end in moves}
        sources = [i for i in range(REPL * per_copy) if i not in target]
        ends = {i for i in range(REPL * per_copy) if i not in back}
        rules = (
            lambda i: i ^ 1 if i in ends else None,
            lambda i: back.get(i) if back.get(i, -1) // per_copy == i // per_copy else None,
            lambda i: next((j for j in sorted(ends) if j // per_copy == i // per_copy and j % ranks == i % ranks), None),
            lambda i: min(ends),
        )
        for rule in rules:
            for i in sources:
                if i not in target and rule(i) in ends:
                    target[i] = rule(i)
                    if rule is rules[0] and i ^ 1 not in target:
                        target[i ^ 1] = i
                        ends.remove(i)
                    ends.remove(target[i])
        return sorted(target.items())

    def send(block, *routes):
        moves = []
        for copy in range(REPL):
            for end in range(2):
                for c in range(middle):
                    for route in routes:
                        source = route(copy, end, c)
                        if source is None:
                            continue
                        for rank in range(ranks):
                            came = (rank + 2) % ranks if source[3] else rank
                            moves.append((place(*source[:3], came), place(copy, end, c, rank)))
        return lax.ppermute(block, ("pipe", "tensor"), completed(moves))

    def hop(block, source, target, turn, other):
        return send(block, lambda copy, end, c: (copy, end ^ turn, source, other) if c == target else None)

    def flow_route(which, wanted):
        turn, shift = pairs_of[which]
        return lambda copy, end, c: ((copy + shift) % REPL, end ^ turn, c, False) if wanted(c, end) else None

    def flow(payload, which, wanted):
        return send(payload, flow_route(which, wanted))

    def joined(*parts):
        return call(stack_kernel, "stack", list(parts), [shape(len(parts) * rows, features)], [], 4, 0, 0, smem=())[0]

    def with_other_core(arrived):
        return arrived + [swap_core(block) for block in arrived]

    def shape(*extent, dtype=BF):
        return jax.ShapeDtypeStruct(extent, dtype)

    row = shape(rows, features)
    pieces = shape(4 * REPL, rows, features)
    gate_shape = shape(2 * rows, narrow, dtype=F32)
    held_shape = pltpu.VMEM((3, features, narrow), BF)
    normed_scratch = pltpu.VMEM((2 * rows, features), BF)
    layer_flops = 12 * rows * features * narrow
    layer_bytes = 6 * features * narrow
    row_bytes = 2 * rows * features

    def layer(kernel, name, operands, outs):
        return call(kernel, name, operands, outs, [normed_scratch], 8, layer_flops, layer_bytes, smem=())

    def hold(part, backward, operands, split):
        kernel = functools.partial(hold_kernel, part, backward)
        outs = [shape(group, features)] * 2 if split else [row]
        found = call(kernel, "hold", [marks] + operands, outs, [], 4, 0, 4 * row_bytes, smem=())
        return found if split else found[0]

    def total(terms):
        return call(sum_kernel, "total", terms, [row], [], 4, 0, 3 * row_bytes, smem=())[0]

    def kind_of(step):
        return min(step, sections - 1 - step)

    def across(held, source, target, during, later=()):
        straight = [hop(held[turn], source, target, turn, False) for turn in range(2)]
        crossed = [hop(held[turn], source, target, turn, True) for turn in range(2)]
        straight, crossed, during = lax.optimization_barrier((straight, crossed, during))
        mine = total(straight + crossed)
        other, later = lax.optimization_barrier((swap_core(mine), later))
        return mine, other, during, later

    def far(c, end):
        return end == 1

    def middle_near(c, end):
        return c > 0 and end == 0

    def middle_class(c, end):
        return c > 0

    pm, po, gate, upper, held_early, mine, other, marks = call(
        first_kernel,
        "first_layer",
        [flags, blocks, pltpu.with_memory_space_constraint(gains, pltpu.HBM), weights],
        [row, row, gate_shape, gate_shape, held_shape, row, row, shape(8, 128, dtype=jnp.int32)],
        [
            normed_scratch,
            pltpu.VMEM(gains.shape, F32),
            pltpu.SemaphoreType.DMA((3, chunks)),
            pltpu.SemaphoreType.DMA((3,)),
        ],
        8,
        layer_flops,
        layer_bytes,
        hbm=(1, 2, 3),
    )
    saved = [(gate, upper, mine, other), None]
    loaded = call(
        load_kernel,
        "load_late",
        [flags, blocks, cot_blocks, weights],
        [held_shape, pieces, pieces, row, row],
        [pltpu.SemaphoreType.DMA((3, 1)), pltpu.SemaphoreType.DMA((4, 4 * REPL))],
        4,
        0,
        2 * layer_bytes,
        hbm=(1, 2, 3),
    )
    for step in range(sections - 1):
        part = 0 if step < middle else 1
        if step > 0:
            old = list(saved[part] or ())
            pm, po, *saved[part] = layer(
                functools.partial(forward_kernel, part, kind_of(step)),
                "forward_layer",
                [marks, mine, other, gains, held_late if part else held_early] + old,
                [row, row, gate_shape, gate_shape, row, row],
            )
        held = hold(part, False, [pm, swap_core(po), mine], step != middle - 1)
        during = ()
        if step == 0:
            during = loaded
        if step == middle:
            during = call(
                cotangent_kernel,
                "cotangent",
                [up_mine, up_other, held_late],
                [gate_shape],
                [],
                4,
                layer_flops // 3,
                layer_bytes // 3,
                smem=(),
            )
        if step == middle - 1:
            mine = total([held, swap_chip(held)])
            other = swap_core(mine)
        else:
            mine, other, during, _ = across(held, kind_of(step), kind_of(step + 1), during)
        if step == 0:
            held_late, input_rows, cot_rows, up_mine, up_other = during
        if step == middle:
            (d_active,) = during

    early_rows = saved[0][2:]
    sides = call(sides_kernel, "sides", [marks, saved[0][2], saved[1][2]], [row, row], [], 4, 0, 0, smem=())
    mine, (same, opposite) = lax.optimization_barrier((mine, sides))
    state_first = flow(opposite, 0, middle_class)
    state_second = flow(joined(same, state_first), 1, middle_class)
    gates = [saved[0][:2], saved[1][:2]]
    pm, po, late_mine, late_other = layer(
        turn_kernel,
        "turn_layer",
        [marks, d_active, mine, other, *saved[1][2:], gains, held_late],
        [row] * 4,
    )
    state_mine = [early_rows[0], late_mine]
    ups = [None, (up_mine, up_other)]
    own_rows = 4 * REPL * rows
    for step in range(sections - 1, 0, -1):
        part = 0 if step < middle else 1
        if step < sections - 1:
            old = list(ups[part] or ())
            extra = [late_mine] if step == middle else []
            pm, po, *kept = layer(
                functools.partial(backward_kernel, kind_of(step), bool(old), bool(extra)),
                "backward_layer",
                [marks, up_mine, up_other, *gates[part], held_late if part else held_early] + old + extra,
                [row] * (5 if extra else 4),
            )
            ups[part] = kept[:2]
        held = hold(part, True, [pm, swap_core(po), up_mine, state_mine[part], gains], step not in (middle, 1))
        if step == 1:
            mine = total([held, swap_chip(held)])
        elif step == middle:
            held, mixed = lax.optimization_barrier((held, kept[2]))
            up_mine = total([held, swap_chip(held)])
            mixed_first = flow(mixed, 0, far)
            up_other, mixed_first, middle_arrived = lax.optimization_barrier(
                (swap_core(up_mine), mixed_first, middle_arrived)
            )
            mixed_second = flow(joined(mixed, mixed_first), 1, far)
        else:
            later = ()
            if step == sections - 1:
                later = [state_first, state_second]
            up_mine, up_other, _, later = across(held, kind_of(step), kind_of(step - 1), (), later)
            if step == sections - 1:
                middle_arrived = with_other_core(later)
    _, mixed_second = lax.optimization_barrier((mine, mixed_second))
    def last_route(shift, source):
        return lambda copy, end, c: ((copy + shift) % REPL, source, 1, False) if c == 0 and end == 0 else None

    payloads = call(last_kernel, "last", [marks, mine, ups[0][0]], [row] * 2, [], 4, 0, 0, smem=())
    straight = [
        send(payloads[0], last_route(0, 0), flow_route(0, middle_near)),
        send(payloads[1], last_route(0, 1)),
        send(payloads[0], last_route(1, 0), flow_route(2, middle_near)),
        send(payloads[1], last_route(1, 1), flow_route(1, middle_near)),
    ]
    mixed_arrived = with_other_core([mixed_first, mixed_second])
    prepared = call(
        own_first_kernel,
        "own_first",
        [flags, input_rows, *early_rows, late_mine, late_other, *middle_arrived, *mixed_arrived, gains, weights],
        [
            shape(features, own_rows),
            shape(own_rows, narrow, dtype=F32),
            shape(own_rows, narrow, dtype=F32),
            shape(own_rows, narrow),
        ],
        [
            pltpu.VMEM((2, features, narrow), BF),
            pltpu.VMEM((own_rows, features), BF),
            pltpu.SemaphoreType.DMA((2, chunks)),
        ],
        12,
        4 * own_rows * features * narrow,
        8 * features * narrow,
        hbm=(15,),
    )
    straight, prepared = lax.optimization_barrier((straight, prepared))
    direct = with_other_core([joined(*straight)])
    return call(
        own_last_kernel,
        "own_last",
        [flags, cot_rows, *direct, *ups[0], *ups[1], *mixed_arrived]
        + [*prepared, held_early, held_late],
        [shape(1, 3, features, narrow)],
        [
            pltpu.VMEM((own_rows, features), BF),
            pltpu.VMEM((own_rows, narrow), F32),
            pltpu.VMEM((3, features, narrow), BF),
            pltpu.SemaphoreType.DMA((3, chunks)),
        ],
        16,
        8 * own_rows * features * narrow,
        8 * features * narrow,
        out_hbm=True,
    )[0]


def solution(mesh):
    return jax.shard_map(
        body,
        mesh=mesh,
        in_specs=(P(), P(), P("pipe", None, None, None, "tensor"), P("pipe", None, None)),
        out_specs=P("pipe", None, None, "tensor"),
        check_vma=False,
    )
```

profile of v0, /device:TPU:0, one launch (start us, length us, event | category | flops | bytes accessed | tf_op | source)
XLA Modules:
  0.0 135.9 jit_solution(11869668942285878861)
XLA Ops:
  0.1 5.5 %first_layer.1 = (bf16[32,3584]{1,0:T(8,128)(2,1)S(1)}, bf16[32,3584]{1,0:T(8,128)(2,1)S(1)}, f32[64,256]{1,0:T(8,128)S(1)}, f32[64,256]{1,0:T(8,128)S(1)}, bf16...) custom-call(s32[29]{0:T(128)S(1)} %stack.110.flags_ref, ...), custom_call_target="tpu_custom_call" | custom-call | flops 352321536 | bytes 5505024 | tf_op jit(solution)/shard_map/first_layer/pallas_call | solution.py:408
  6.1 1.1 collective-permute-done.recv_ref
  7.4 3.9 %collective-permute-start.3 = (bf16[16,3584]{1,0:T(8,128)(2,1)S(1)}, bf16[16,3584]{1,0:T(8,128)(2,1)S(1)}, u32[]{:S(2)}, u32[]{:S(2)}) collective-permute-start(bf16[16,3584]{1,0:T(8,128)(2,1)S(1)} %get-tuple-element.102), channel_id=1, source_target_pairs={{0,6},{1,7},{2,4},{3,5},{4,2},{5,3},{6,0},{7,1},{8,14},{9,15},{10,... | collective-permute-start | bytes 344072 | tf_op jit(solution)/shard_map/ppermute | solution.py:501
  11.3 0.5 collective-permute-start.1
  11.8 1.5 %collective-permute-start.4 = (bf16[16,3584]{1,0:T(8,128)(2,1)S(1)}, bf16[16,3584]{1,0:T(8,128)(2,1)S(1)}, u32[]{:S(2)}, u32[]{:S(2)}) collective-permute-start(bf16[16,3584]{1,0:T(8,128)(2,1)S(1)} %get-tuple-element.103), channel_id=1, source_target_pairs={{0,10},{1,11},{2,8},{3,9},{4,14},{5,15},{6,12},{7,13},{8,2},{9,3},... | collective-permute-start | bytes 344072 | tf_op jit(solution)/shard_map/ppermute | solution.py:501
  13.4 4.8 %load_late.1 = (bf16[3,3584,256]{2,1,0:T(8,128)(2,1)S(1)}, bf16[8,32,3584]{2,1,0:T(8,128)(2,1)S(1)}, bf16[8,32,3584]{2,1,0:T(8,128)(2,1)S(1)}, bf16[32,3584]{1,0:T(8,128)(2,1)S(1)}, bf16[32,3584]{1,0:T(8,128)(2,1)S(1)}) custom-call(s32[29]{0:T(128)S(1)} %stack.110.flags_ref, bf16[8,32,3584]{2,1,0:T(8,128)(2,1)} %bitcast.37, bf16[8,32,3584]{2,1,0:T(8,128)(2,1)} %bitcast.38, ...), custom_call_target="tpu_custom_call" | custom-call | bytes 11010048 | tf_op jit(solution)/shard_map/load_late/pallas_call | solution.py:408
  19.2 1.5 %collective-permute-done.5.xo_ref = bf16[32,3584]{1,0:T(8,128)(2,1)S(1)} collective-permute-done((bf16[32,3584]{1,0:T(8,128)(2,1)S(1)}, bf16[32,3584]{1,0:T(8,128)(2,1)S(1)}, u32[]{:S(2)}, u32[]{:S(2)}) %collective-permute-start.5) | collective-permute-done | bytes 229408 | tf_op jit(solution)/shard_map/ppermute | solution.py:458
  20.7 1.6 %forward_layer.2 = (bf16[32,3584]{1,0:T(8,128)(2,1)S(1)}, bf16[32,3584]{1,0:T(8,128)(2,1)S(1)}, f32[64,256]{1,0:T(8,128)S(1)}, f32[64,256]{1,0:T(8,128)S(1)}, bf...) custom-call(s32[8,128]{1,0:T(8,128)S(1)} %get-tuple-element.98.flags_ref.marks_ref, ...), custom_call_target="tpu_custom_call" | custom-call | flops 352321536 | bytes 5505024 | tf_op jit(solution)/shard_map/forward_layer/pallas_call | solution.py:408
  22.5 1.4 collective-permute-done.6.recv_ref
  24.0 1.4 %collective-permute-start.7 = (bf16[32,3584]{1,0:T(8,128)(2,1)S(1)}, bf16[32,3584]{1,0:T(8,128)(2,1)S(1)}, u32[]{:S(2)}, u32[]{:S(2)}) collective-permute-start(bf16[32,3584]{1,0:T(8,128)(2,1)S(1)} %hold.7.refs_0_), channel_id=1, source_target_pairs={{0,2},{1,3},{2,0},{3,1},{4,6},{5,7},{6,4},{7,5},{8,10},{9,11},{10,... | collective-permute-start | bytes 688136 | tf_op jit(solution)/shard_map/ppermute | solution.py:461
  25.5 6.3 %collective-permute-done.7.refs_1_ = bf16[32,3584]{1,0:T(8,128)(2,1)S(1)} collective-permute-done((bf16[32,3584]{1,0:T(8,128)(2,1)S(1)}, bf16[32,3584]{1,0:T(8,128)(2,1)S(1)}, u32[]{:S(2)}, u32[]{:S(2)}) %collective-permute-start.7) | collective-permute-done | bytes 229408 | tf_op jit(solution)/shard_map/ppermute | solution.py:461
  31.9 1.5 %collective-permute-done.8.xo_ref = bf16[32,3584]{1,0:T(8,128)(2,1)S(1)} collective-permute-done((bf16[32,3584]{1,0:T(8,128)(2,1)S(1)}, bf16[32,3584]{1,0:T(8,128)(2,1)S(1)}, u32[]{:S(2)}, u32[]{:S(2)}) %collective-permute-start.8) | collective-permute-done | bytes 229408 | tf_op jit(solution)/shard_map/ppermute | solution.py:458
  33.4 1.5 %forward_layer.3 = (bf16[32,3584]{1,0:T(8,128)(2,1)S(1)}, bf16[32,3584]{1,0:T(8,128)(2,1)S(1)}, f32[64,256]{1,0:T(8,128)S(1)}, f32[64,256]{1,0:T(8,128)S(1)}, bf...) custom-call(s32[8,128]{1,0:T(8,128)S(1)} %get-tuple-element.98.flags_ref.marks_ref, ...), custom_call_target="tpu_custom_call" | custom-call | flops 352321536 | bytes 5505024 | tf_op jit(solution)/shard_map/forward_layer/pallas_call | solution.py:408
  35.1 1.3 collective-permute-done.9.recv_ref
  36.6 2.4 %collective-permute-start.12 = (bf16[16,3584]{1,0:T(8,128)(2,1)S(1)}, bf16[16,3584]{1,0:T(8,128)(2,1)S(1)}, u32[]{:S(2)}, u32[]{:S(2)}) collective-permute-start(bf16[16,3584]{1,0:T(8,128)(2,1)S(1)} %get-tuple-element.123), channel_id=1, source_target_pairs={{0,6},{1,7},{2,4},{3,5},{4,2},{5,3},{6,0},{7,1},{8,14},{9,15},{10,... | collective-permute-start | bytes 344072 | tf_op jit(solution)/shard_map/ppermute | solution.py:501
  39.0 0.5 collective-permute-start.10
  39.5 1.6 %collective-permute-start.13 = (bf16[16,3584]{1,0:T(8,128)(2,1)S(1)}, bf16[16,3584]{1,0:T(8,128)(2,1)S(1)}, u32[]{:S(2)}, u32[]{:S(2)}) collective-permute-start(bf16[16,3584]{1,0:T(8,128)(2,1)S(1)} %get-tuple-element.124), channel_id=1, source_target_pairs={{0,10},{1,11},{2,8},{3,9},{4,14},{5,15},{6,12},{7,13},{8,2},{9,3},... | collective-permute-start | bytes 344072 | tf_op jit(solution)/shard_map/ppermute | solution.py:501
  42.1 2.0 %collective-permute-done.12.refs_2_ = bf16[16,3584]{1,0:T(8,128)(2,1)S(1)} collective-permute-done((bf16[16,3584]{1,0:T(8,128)(2,1)S(1)}, bf16[16,3584]{1,0:T(8,128)(2,1)S(1)}, u32[]{:S(2)}, u32[]{:S(2)}) %collective-permute-start.12) | collective-permute-done | bytes 114720 | tf_op jit(solution)/shard_map/ppermute | solution.py:501
  44.0 1.1 collective-permute-done.10.refs_0_
  45.1 1.2 collective-permute-done.13.refs_3_
  47.1 0.6 collective-permute-start.21
  47.7 0.7 collective-permute-done.14.xo_ref
  48.4 2.2 %turn_layer.1 = (bf16[32,3584]{1,0:T(8,128)(2,1)S(1)}, bf16[32,3584]{1,0:T(8,128)(2,1)S(1)}, bf16[32,3584]{1,0:T(8,128)(2,1)S(1)}, bf16[32,3584]{1,0:T(8,128)(2,1)S(1)}) custom-call(s32[8,128]{1,0:T(8,128)S(1)} %get-tuple-element.98.flags_ref.marks_ref, f32[64,256]{1,0:T(8,128)S(1)} %cotangent.1.d_ref, bf16[32,3584]{1,0:T(8,128)(2,1)S(1)} %total.8.xm_ref, ...), custom_call_target="tpu_custom_call" | custom-call | flops 352321536 | bytes 5505024 | tf_op jit(solution)/shard_map/turn_layer/pallas_call | solution.py:408
  51.3 0.9 collective-permute-done.15.recv_ref
  52.5 9.0 %collective-permute-start.18 = (bf16[16,3584]{1,0:T(8,128)(2,1)S(1)}, bf16[16,3584]{1,0:T(8,128)(2,1)S(1)}, u32[]{:S(2)}, u32[]{:S(2)}) collective-permute-start(bf16[16,3584]{1,0:T(8,128)(2,1)S(1)} %get-tuple-element.141), channel_id=1, source_target_pairs={{0,6},{1,7},{2,4},{3,5},{4,2},{5,3},{6,0},{7,1},{8,14},{9,15},{10,... | collective-permute-start | bytes 344072 | tf_op jit(solution)/shard_map/ppermute | solution.py:501
  61.5 2.2 %collective-permute-start.19 = (bf16[16,3584]{1,0:T(8,128)(2,1)S(1)}, bf16[16,3584]{1,0:T(8,128)(2,1)S(1)}, u32[]{:S(2)}, u32[]{:S(2)}) collective-permute-start(bf16[16,3584]{1,0:T(8,128)(2,1)S(1)} %get-tuple-element.142), channel_id=1, source_target_pairs={{0,10},{1,11},{2,8},{3,9},{4,14},{5,15},{6,12},{7,13},{8,2},{9,3},... | collective-permute-start | bytes 344072 | tf_op jit(solution)/shard_map/ppermute | solution.py:501
  63.7 1.9 %collective-permute-done.18.refs_2_ = bf16[16,3584]{1,0:T(8,128)(2,1)S(1)} collective-permute-done((bf16[16,3584]{1,0:T(8,128)(2,1)S(1)}, bf16[16,3584]{1,0:T(8,128)(2,1)S(1)}, u32[]{:S(2)}, u32[]{:S(2)}) %collective-permute-start.18) | collective-permute-done | bytes 114720 | tf_op jit(solution)/shard_map/ppermute | solution.py:501
  65.7 0.6 collective-permute-done.16.refs_0_
  66.3 1.9 %collective-permute-done.19.refs_3_ = bf16[16,3584]{1,0:T(8,128)(2,1)S(1)} collective-permute-done((bf16[16,3584]{1,0:T(8,128)(2,1)S(1)}, bf16[16,3584]{1,0:T(8,128)(2,1)S(1)}, u32[]{:S(2)}, u32[]{:S(2)}) %collective-permute-start.19) | collective-permute-done | bytes 114720 | tf_op jit(solution)/shard_map/ppermute | solution.py:501
  68.7 1.5 %collective-permute-done.20.uo_ref = bf16[32,3584]{1,0:T(8,128)(2,1)S(1)} collective-permute-done((bf16[32,3584]{1,0:T(8,128)(2,1)S(1)}, bf16[32,3584]{1,0:T(8,128)(2,1)S(1)}, u32[]{:S(2)}, u32[]{:S(2)}) %collective-permute-start.20) | collective-permute-done | bytes 229408 | tf_op jit(solution)/shard_map/ppermute | solution.py:458
  70.2 2.1 %backward_layer.2 = (bf16[32,3584]{1,0:T(8,128)(2,1)S(1)}, bf16[32,3584]{1,0:T(8,128)(2,1)S(1)}, bf16[32,3584]{1,0:T(8,128)(2,1)S(1)}, bf16[32,3584]{1,0:T(8,128)(2,1)S(1)}, bf16[32,3584]{1,0:T(8,128)(2,1)S(1)}) custom-call(s32[8,128]{1,0:T(8,128)S(1)} %get-tuple-element.98.flags_ref.marks_ref, bf16[32,3584]{1,0:T(8,128)(2,1)S(1)} %total.9.um_ref.base_ref, ...), custom_call_target="tpu_custom_call" | custom-call | flops 352321536 | bytes 5505024 | tf_op jit(solution)/shard_map/backward_layer/pallas_call | solution.py:408
  72.5 1.3 collective-permute-done.23.recv_ref
  74.3 1.4 %collective-permute-start.24 = (bf16[32,3584]{1,0:T(8,128)(2,1)S(1)}, bf16[32,3584]{1,0:T(8,128)(2,1)S(1)}, u32[]{:S(2)}, u32[]{:S(2)}) collective-permute-start(bf16[32,3584]{1,0:T(8,128)(2,1)S(1)} %hold.10.refs_0_), channel_id=1, source_target_pairs={{0,2},{1,3},{2,0},{3,1},{4,6},{5,7},{6,4},{7,5},{8,10},{9,11},{10,... | collective-permute-start | bytes 688136 | tf_op jit(solution)/shard_map/ppermute | solution.py:461
  76.2 8.1 %collective-permute-start.26 = (bf16[32,3584]{1,0:T(8,128)(2,1)S(1)}, bf16[32,3584]{1,0:T(8,128)(2,1)S(1)}, u32[]{:S(2)}, u32[]{:S(2)}) collective-permute-start(bf16[32,3584]{1,0:T(8,128)(2,1)S(1)} %get-tuple-element.156.refs_0_), channel_id=1, source_target_pairs={{0,12},{1,13},{2,14},{3,15},{4,8},{5,9},{6,10},{7,11},{8,4},{9,5},... | collective-permute-start | bytes 688136 | tf_op jit(solution)/shard_map/ppermute | solution.py:501
  84.5 5.6 %collective-permute-done.26.refs_1_.q0.refs_6_ = bf16[32,3584]{1,0:T(8,128)(2,1)S(1)} collective-permute-done((bf16[32,3584]{1,0:T(8,128)(2,1)S(1)}, bf16[32,3584]{1,0:T(8,128)(2,1)S(1)}, u32[]{:S(2)}, u32[]{:S(2)}) %collective-permute-start.26) | collective-permute-done | bytes 229408 | tf_op jit(solution)/shard_map/ppermute | solution.py:501
  90.1 1.9 %backward_layer.3 = (bf16[32,3584]{1,0:T(8,128)(2,1)S(1)}, bf16[32,3584]{1,0:T(8,128)(2,1)S(1)}, bf16[32,3584]{1,0:T(8,128)(2,1)S(1)}, bf16[32,3584]{1,0:T(8,128)(2,1)S(1)}) custom-call(s32[8,128]{1,0:T(8,128)S(1)} %get-tuple-element.98.flags_ref.marks_ref, bf16[32,3584]{1,0:T(8,128)(2,1)S(1)} %total.10.um_ref.base_ref, ...), custom_call_target="tpu_custom_call" | custom-call | flops 352321536 | bytes 5505024 | tf_op jit(solution)/shard_map/backward_layer/pallas_call | solution.py:408
  92.2 0.6 collective-permute-start.35
  92.7 0.9 collective-permute-done.29.recv_ref
  94.0 0.7 collective-permute-start.30
  94.7 7.0 %collective-permute-done.30.refs_1_ = bf16[32,3584]{1,0:T(8,128)(2,1)S(1)} collective-permute-done((bf16[32,3584]{1,0:T(8,128)(2,1)S(1)}, bf16[32,3584]{1,0:T(8,128)(2,1)S(1)}, u32[]{:S(2)}, u32[]{:S(2)}) %collective-permute-start.30) | collective-permute-done | bytes 229408 | tf_op jit(solution)/shard_map/ppermute | solution.py:461
  102.7 5.8 %collective-permute-start.33 = (bf16[32,3584]{1,0:T(8,128)(2,1)S(1)}, bf16[32,3584]{1,0:T(8,128)(2,1)S(1)}, u32[]{:S(2)}, u32[]{:S(2)}) collective-permute-start(bf16[32,3584]{1,0:T(8,128)(2,1)S(1)} %get-tuple-element.165), channel_id=1, source_target_pairs={{0,8},{1,9},{2,10},{3,11},{4,16},{5,17},{6,18},{7,19},{8,20},{9,21... | collective-permute-start | bytes 688136 | tf_op jit(solution)/shard_map/ppermute | solution.py:501
  108.6 3.1 %collective-permute-start.32 = (bf16[32,3584]{1,0:T(8,128)(2,1)S(1)}, bf16[32,3584]{1,0:T(8,128)(2,1)S(1)}, u32[]{:S(2)}, u32[]{:S(2)}) collective-permute-start(bf16[32,3584]{1,0:T(8,128)(2,1)S(1)} %get-tuple-element.166), channel_id=1, source_target_pairs={{0,8},{1,9},{2,10},{3,11},{4,5},{5,4},{6,7},{7,6},{8,0},{9,1},{10,... | collective-permute-start | bytes 688136 | tf_op jit(solution)/shard_map/ppermute | solution.py:501
  111.8 3.5 %own_first.1 = (bf16[3584,256]{1,0:T(8,128)(2,1)S(1)}, f32[256,256]{1,0:T(8,128)S(1)}, f32[256,256]{1,0:T(8,128)S(1)}, bf16[256,256]{1,0:T(8,128)(2,1)S(1)}) custom-call(s32[29]{0:T(128)S(1)} %stack.110.flags_ref, bf16[8,32,3584]{2,1,0:T(8,128)(2,1)S(1)} %get-tuple-element.167.xs_ref, bf16[32,3584]{1,0:T(8,128)(2,1)S(1)} %get-tuple-element.132.early_ref.refs_0_.em_ref, ...), custom_call_target="tpu_custom_call" | custom-call | flops 939524096 | bytes 7340032 | tf_op jit(solution)/shard_map/own_first/pallas_call | solution.py:408
  115.3 4.1 %collective-permute-done.31.refs_0_ = bf16[32,3584]{1,0:T(8,128)(2,1)S(1)} collective-permute-done((bf16[32,3584]{1,0:T(8,128)(2,1)S(1)}, bf16[32,3584]{1,0:T(8,128)(2,1)S(1)}, u32[]{:S(2)}, u32[]{:S(2)}) %collective-permute-start.31) | collective-permute-done | bytes 229408 | tf_op jit(solution)/shard_map/ppermute | solution.py:501
  119.4 7.4 %collective-permute-done.34.refs_3_ = bf16[32,3584]{1,0:T(8,128)(2,1)S(1)} collective-permute-done((bf16[32,3584]{1,0:T(8,128)(2,1)S(1)}, bf16[32,3584]{1,0:T(8,128)(2,1)S(1)}, u32[]{:S(2)}, u32[]{:S(2)}) %collective-permute-start.34) | collective-permute-done | bytes 229408 | tf_op jit(solution)/shard_map/ppermute | solution.py:501
  126.8 2.3 %collective-permute-done.32.refs_1_ = bf16[32,3584]{1,0:T(8,128)(2,1)S(1)} collective-permute-done((bf16[32,3584]{1,0:T(8,128)(2,1)S(1)}, bf16[32,3584]{1,0:T(8,128)(2,1)S(1)}, u32[]{:S(2)}, u32[]{:S(2)}) %collective-permute-start.32) | collective-permute-done | bytes 229408 | tf_op jit(solution)/shard_map/ppermute | solution.py:501
  129.2 2.5 %collective-permute-done.38.refs_1_ = bf16[128,3584]{1,0:T(8,128)(2,1)S(1)} collective-permute-done((bf16[128,3584]{1,0:T(8,128)(2,1)S(1)}, bf16[128,3584]{1,0:T(8,128)(2,1)S(1)}, u32[]{:S(2)}, u32[]{:S(2)}) %collective-permute-start.38) | collective-permute-done | bytes 917536 | tf_op jit(solution)/shard_map/ppermute | solution.py:458
  131.7 4.1 %own_last.1 = bf16[1,3,3584,256]{3,2,1,0:T(8,128)(2,1)} custom-call(s32[29]{0:T(128)S(1)} %stack.110.flags_ref, bf16[8,32,3584]{2,1,0:T(8,128)(2,1)S(1)} %get-tuple-element.109.us_ref, bf16[128,3584]{1,0:T(8,128)(2,1)S(1)} %stack.116.refs_0_, bf16[128,3584]{1,0:T(8,128)(2,1)S(1)} %collective-permute-done.38.refs_1_, ...), custom_call_target="tpu_custom_call" | custom-call | flops 1879048192 | bytes 7340032 | tf_op jit(solution)/shard_map/own_last/pallas_call | solution.py:408
  (60 shorter events, 9.0 us)
Async XLA Ops:
  5.6 1.6 %collective-permute-start = (bf16[32,3584]{1,0:T(8,128)(2,1)S(1)}, bf16[32,3584]{1,0:T(8,128)(2,1)S(1)}, u32[]{:S(2)}, u32[]{:S(2)}) collective-permute-start(bf16[32,3584]{1,0:T(8,128)(2,1)S(1)} %get-tuple-element.100), channel_id=1, source_target_pairs={{0,1},{1,0},{2,3},{3,2},{4,5},{5,4},{6,7},{7,6},{8,9},{9,8},{10,11... | collective-permute-start | bytes 688136 | tf_op jit(solution)/shard_map/ppermute | solution.py:458
  7.4 10.8 %collective-permute-start.3 = (bf16[16,3584]{1,0:T(8,128)(2,1)S(1)}, bf16[16,3584]{1,0:T(8,128)(2,1)S(1)}, u32[]{:S(2)}, u32[]{:S(2)}) collective-permute-start(bf16[16,3584]{1,0:T(8,128)(2,1)S(1)} %get-tuple-element.102), channel_id=1, source_target_pairs={{0,6},{1,7},{2,4},{3,5},{4,2},{5,3},{6,0},{7,1},{8,14},{9,15},{10,... | collective-permute-start | bytes 344072 | tf_op jit(solution)/shard_map/ppermute | solution.py:501
  11.3 6.9 %collective-permute-start.1 = (bf16[16,3584]{1,0:T(8,128)(2,1)S(1)}, bf16[16,3584]{1,0:T(8,128)(2,1)S(1)}, u32[]{:S(2)}, u32[]{:S(2)}) collective-permute-start(bf16[16,3584]{1,0:T(8,128)(2,1)S(1)} %get-tuple-element.102), channel_id=1, source_target_pairs={{0,4},{1,5},{2,6},{3,7},{4,0},{5,1},{6,2},{7,3},{8,12},{9,13},{10,... | collective-permute-start | bytes 344072 | tf_op jit(solution)/shard_map/ppermute | solution.py:501
  11.8 6.8 %collective-permute-start.4 = (bf16[16,3584]{1,0:T(8,128)(2,1)S(1)}, bf16[16,3584]{1,0:T(8,128)(2,1)S(1)}, u32[]{:S(2)}, u32[]{:S(2)}) collective-permute-start(bf16[16,3584]{1,0:T(8,128)(2,1)S(1)} %get-tuple-element.103), channel_id=1, source_target_pairs={{0,10},{1,11},{2,8},{3,9},{4,14},{5,15},{6,12},{7,13},{8,2},{9,3},... | collective-permute-start | bytes 344072 | tf_op jit(solution)/shard_map/ppermute | solution.py:501
  13.4 5.7 %collective-permute-start.2 = (bf16[16,3584]{1,0:T(8,128)(2,1)S(1)}, bf16[16,3584]{1,0:T(8,128)(2,1)S(1)}, u32[]{:S(2)}, u32[]{:S(2)}) collective-permute-start(bf16[16,3584]{1,0:T(8,128)(2,1)S(1)} %get-tuple-element.103), channel_id=1, source_target_pairs={{0,8},{1,9},{2,10},{3,11},{4,12},{5,13},{6,14},{7,15},{8,0},{9,1},... | collective-permute-start | bytes 344072 | tf_op jit(solution)/shard_map/ppermute | solution.py:501
  13.4 7.3 %copy-start = (f32[1,2,3584]{2,1,0:T(2,128)S(1)}, f32[1,2,3584]{2,1,0:T(2,128)}, u32[]{:S(2)}) copy-start(f32[1,2,3584]{2,1,0:T(2,128)} %param.7) | copy-start | bytes 86020
  19.2 1.6 %collective-permute-start.5 = (bf16[32,3584]{1,0:T(8,128)(2,1)S(1)}, bf16[32,3584]{1,0:T(8,128)(2,1)S(1)}, u32[]{:S(2)}, u32[]{:S(2)}) collective-permute-start(bf16[32,3584]{1,0:T(8,128)(2,1)S(1)} %total.6.xm_ref.base_ref), channel_id=1, source_target_pairs={{0,1},{1,0},{2,3},{3,2},{4,5},{5,4},{6,7},{7,6},{8,9},{9,8},{10,11... | collective-permute-start | bytes 688136 | tf_op jit(solution)/shard_map/ppermute | solution.py:458
  22.3 1.6 %collective-permute-start.6 = (bf16[32,3584]{1,0:T(8,128)(2,1)S(1)}, bf16[32,3584]{1,0:T(8,128)(2,1)S(1)}, u32[]{:S(2)}, u32[]{:S(2)}) collective-permute-start(bf16[32,3584]{1,0:T(8,128)(2,1)S(1)} %get-tuple-element.119), channel_id=1, source_target_pairs={{0,1},{1,0},{2,3},{3,2},{4,5},{5,4},{6,7},{7,6},{8,9},{9,8},{10,11... | collective-permute-start | bytes 688136 | tf_op jit(solution)/shard_map/ppermute | solution.py:458
  24.0 7.7 %collective-permute-start.7 = (bf16[32,3584]{1,0:T(8,128)(2,1)S(1)}, bf16[32,3584]{1,0:T(8,128)(2,1)S(1)}, u32[]{:S(2)}, u32[]{:S(2)}) collective-permute-start(bf16[32,3584]{1,0:T(8,128)(2,1)S(1)} %hold.7.refs_0_), channel_id=1, source_target_pairs={{0,2},{1,3},{2,0},{3,1},{4,6},{5,7},{6,4},{7,5},{8,10},{9,11},{10,... | collective-permute-start | bytes 688136 | tf_op jit(solution)/shard_map/ppermute | solution.py:461
  31.8 1.6 %collective-permute-start.8 = (bf16[32,3584]{1,0:T(8,128)(2,1)S(1)}, bf16[32,3584]{1,0:T(8,128)(2,1)S(1)}, u32[]{:S(2)}, u32[]{:S(2)}) collective-permute-start(bf16[32,3584]{1,0:T(8,128)(2,1)S(1)} %total.7.xm_ref.base_ref), channel_id=1, source_target_pairs={{0,1},{1,0},{2,3},{3,2},{4,5},{5,4},{6,7},{7,6},{8,9},{9,8},{10,11... | collective-permute-start | bytes 688136 | tf_op jit(solution)/shard_map/ppermute | solution.py:458
  34.9 1.6 %collective-permute-start.9 = (bf16[32,3584]{1,0:T(8,128)(2,1)S(1)}, bf16[32,3584]{1,0:T(8,128)(2,1)S(1)}, u32[]{:S(2)}, u32[]{:S(2)}) collective-permute-start(bf16[32,3584]{1,0:T(8,128)(2,1)S(1)} %get-tuple-element.122), channel_id=1, source_target_pairs={{0,1},{1,0},{2,3},{3,2},{4,5},{5,4},{6,7},{7,6},{8,9},{9,8},{10,11... | collective-permute-start | bytes 688136 | tf_op jit(solution)/shard_map/ppermute | solution.py:458
  36.6 7.4 %collective-permute-start.12 = (bf16[16,3584]{1,0:T(8,128)(2,1)S(1)}, bf16[16,3584]{1,0:T(8,128)(2,1)S(1)}, u32[]{:S(2)}, u32[]{:S(2)}) collective-permute-start(bf16[16,3584]{1,0:T(8,128)(2,1)S(1)} %get-tuple-element.123), channel_id=1, source_target_pairs={{0,6},{1,7},{2,4},{3,5},{4,2},{5,3},{6,0},{7,1},{8,14},{9,15},{10,... | collective-permute-start | bytes 344072 | tf_op jit(solution)/shard_map/ppermute | solution.py:501
  39.0 6.2 %collective-permute-start.10 = (bf16[16,3584]{1,0:T(8,128)(2,1)S(1)}, bf16[16,3584]{1,0:T(8,128)(2,1)S(1)}, u32[]{:S(2)}, u32[]{:S(2)}) collective-permute-start(bf16[16,3584]{1,0:T(8,128)(2,1)S(1)} %get-tuple-element.123), channel_id=1, source_target_pairs={{0,4},{1,5},{2,6},{3,7},{4,0},{5,1},{6,2},{7,3},{8,12},{9,13},{10,... | collective-permute-start | bytes 344072 | tf_op jit(solution)/shard_map/ppermute | solution.py:501
  39.5 6.8 %collective-permute-start.13 = (bf16[16,3584]{1,0:T(8,128)(2,1)S(1)}, bf16[16,3584]{1,0:T(8,128)(2,1)S(1)}, u32[]{:S(2)}, u32[]{:S(2)}) collective-permute-start(bf16[16,3584]{1,0:T(8,128)(2,1)S(1)} %get-tuple-element.124), channel_id=1, source_target_pairs={{0,10},{1,11},{2,8},{3,9},{4,14},{5,15},{6,12},{7,13},{8,2},{9,3},... | collective-permute-start | bytes 344072 | tf_op jit(solution)/shard_map/ppermute | solution.py:501
  41.1 5.7 %collective-permute-start.11 = (bf16[16,3584]{1,0:T(8,128)(2,1)S(1)}, bf16[16,3584]{1,0:T(8,128)(2,1)S(1)}, u32[]{:S(2)}, u32[]{:S(2)}) collective-permute-start(bf16[16,3584]{1,0:T(8,128)(2,1)S(1)} %get-tuple-element.124), channel_id=1, source_target_pairs={{0,8},{1,9},{2,10},{3,11},{4,12},{5,13},{6,14},{7,15},{8,0},{9,1},... | collective-permute-start | bytes 344072 | tf_op jit(solution)/shard_map/ppermute | solution.py:501
  46.9 1.6 %collective-permute-start.14 = (bf16[32,3584]{1,0:T(8,128)(2,1)S(1)}, bf16[32,3584]{1,0:T(8,128)(2,1)S(1)}, u32[]{:S(2)}, u32[]{:S(2)}) collective-permute-start(bf16[32,3584]{1,0:T(8,128)(2,1)S(1)} %total.8.xm_ref), channel_id=1, source_target_pairs={{0,1},{1,0},{2,3},{3,2},{4,5},{5,4},{6,7},{7,6},{8,9},{9,8},{10,11... | collective-permute-start | bytes 688136 | tf_op jit(solution)/shard_map/ppermute | solution.py:458
  47.1 3.7 %collective-permute-start.21 = (bf16[32,3584]{1,0:T(8,128)(2,1)S(1)}, bf16[32,3584]{1,0:T(8,128)(2,1)S(1)}, u32[]{:S(2)}, u32[]{:S(2)}) collective-permute-start(bf16[32,3584]{1,0:T(8,128)(2,1)S(1)} %get-tuple-element.147), channel_id=1, source_target_pairs={{0,1},{1,0},{2,3},{3,2},{4,8},{5,9},{6,10},{7,11},{8,4},{9,5},{10,... | collective-permute-start | bytes 688136 | tf_op jit(solution)/shard_map/ppermute | solution.py:501
  50.6 1.6 %collective-permute-start.15 = (bf16[32,3584]{1,0:T(8,128)(2,1)S(1)}, bf16[32,3584]{1,0:T(8,128)(2,1)S(1)}, u32[]{:S(2)}, u32[]{:S(2)}) collective-permute-start(bf16[32,3584]{1,0:T(8,128)(2,1)S(1)} %get-tuple-element.139), channel_id=1, source_target_pairs={{0,1},{1,0},{2,3},{3,2},{4,5},{5,4},{6,7},{7,6},{8,9},{9,8},{10,11... | collective-permute-start | bytes 688136 | tf_op jit(solution)/shard_map/ppermute | solution.py:458
  50.8 17.9 %collective-permute-start.22 = (bf16[64,3584]{1,0:T(8,128)(2,1)S(1)}, bf16[64,3584]{1,0:T(8,128)(2,1)S(1)}, u32[]{:S(2)}, u32[]{:S(2)}) collective-permute-start(bf16[64,3584]{1,0:T(8,128)(2,1)S(1)} %stack.114), channel_id=1, source_target_pairs={{0,1},{1,0},{2,3},{3,2},{4,20},{5,21},{6,22},{7,23},{8,24},{9,25},... | collective-permute-start | bytes 1376264 | tf_op jit(solution)/shard_map/ppermute | solution.py:501
  52.5 13.1 %collective-permute-start.18 = (bf16[16,3584]{1,0:T(8,128)(2,1)S(1)}, bf16[16,3584]{1,0:T(8,128)(2,1)S(1)}, u32[]{:S(2)}, u32[]{:S(2)}) collective-permute-start(bf16[16,3584]{1,0:T(8,128)(2,1)S(1)} %get-tuple-element.141), channel_id=1, source_target_pairs={{0,6},{1,7},{2,4},{3,5},{4,2},{5,3},{6,0},{7,1},{8,14},{9,15},{10,... | collective-permute-start | bytes 344072 | tf_op jit(solution)/shard_map/ppermute | solution.py:501
  61.5 4.8 %collective-permute-start.16 = (bf16[16,3584]{1,0:T(8,128)(2,1)S(1)}, bf16[16,3584]{1,0:T(8,128)(2,1)S(1)}, u32[]{:S(2)}, u32[]{:S(2)}) collective-permute-start(bf16[16,3584]{1,0:T(8,128)(2,1)S(1)} %get-tuple-element.141), channel_id=1, source_target_pairs={{0,4},{1,5},{2,6},{3,7},{4,0},{5,1},{6,2},{7,3},{8,12},{9,13},{10,... | collective-permute-start | bytes 344072 | tf_op jit(solution)/shard_map/ppermute | solution.py:501
  61.5 6.6 %collective-permute-start.19 = (bf16[16,3584]{1,0:T(8,128)(2,1)S(1)}, bf16[16,3584]{1,0:T(8,128)(2,1)S(1)}, u32[]{:S(2)}, u32[]{:S(2)}) collective-permute-start(bf16[16,3584]{1,0:T(8,128)(2,1)S(1)} %get-tuple-element.142), channel_id=1, source_target_pairs={{0,10},{1,11},{2,8},{3,9},{4,14},{5,15},{6,12},{7,13},{8,2},{9,3},... | collective-permute-start | bytes 344072 | tf_op jit(solution)/shard_map/ppermute | solution.py:501
  63.7 4.9 %collective-permute-start.17 = (bf16[16,3584]{1,0:T(8,128)(2,1)S(1)}, bf16[16,3584]{1,0:T(8,128)(2,1)S(1)}, u32[]{:S(2)}, u32[]{:S(2)}) collective-permute-start(bf16[16,3584]{1,0:T(8,128)(2,1)S(1)} %get-tuple-element.142), channel_id=1, source_target_pairs={{0,8},{1,9},{2,10},{3,11},{4,12},{5,13},{6,14},{7,15},{8,0},{9,1},... | collective-permute-start | bytes 344072 | tf_op jit(solution)/shard_map/ppermute | solution.py:501
  68.7 1.6 %collective-permute-start.20 = (bf16[32,3584]{1,0:T(8,128)(2,1)S(1)}, bf16[32,3584]{1,0:T(8,128)(2,1)S(1)}, u32[]{:S(2)}, u32[]{:S(2)}) collective-permute-start(bf16[32,3584]{1,0:T(8,128)(2,1)S(1)} %total.9.um_ref.base_ref), channel_id=1, source_target_pairs={{0,1},{1,0},{2,3},{3,2},{4,5},{5,4},{6,7},{7,6},{8,9},{9,8},{10,11... | collective-permute-start | bytes 688136 | tf_op jit(solution)/shard_map/ppermute | solution.py:458
  72.3 1.6 %collective-permute-start.23 = (bf16[32,3584]{1,0:T(8,128)(2,1)S(1)}, bf16[32,3584]{1,0:T(8,128)(2,1)S(1)}, u32[]{:S(2)}, u32[]{:S(2)}) collective-permute-start(bf16[32,3584]{1,0:T(8,128)(2,1)S(1)} %get-tuple-element.153), channel_id=1, source_target_pairs={{0,1},{1,0},{2,3},{3,2},{4,5},{5,4},{6,7},{7,6},{8,9},{9,8},{10,11... | collective-permute-start | bytes 688136 | tf_op jit(solution)/shard_map/ppermute | solution.py:458
  74.3 10.1 %collective-permute-start.24 = (bf16[32,3584]{1,0:T(8,128)(2,1)S(1)}, bf16[32,3584]{1,0:T(8,128)(2,1)S(1)}, u32[]{:S(2)}, u32[]{:S(2)}) collective-permute-start(bf16[32,3584]{1,0:T(8,128)(2,1)S(1)} %hold.10.refs_0_), channel_id=1, source_target_pairs={{0,2},{1,3},{2,0},{3,1},{4,6},{5,7},{6,4},{7,5},{8,10},{9,11},{10,... | collective-permute-start | bytes 688136 | tf_op jit(solution)/shard_map/ppermute | solution.py:461
  75.7 8.8 %collective-permute-start.28 = (bf16[64,3584]{1,0:T(8,128)(2,1)S(1)}, bf16[64,3584]{1,0:T(8,128)(2,1)S(1)}, u32[]{:S(2)}, u32[]{:S(2)}) collective-permute-start(bf16[64,3584]{1,0:T(8,128)(2,1)S(1)} %collective-permute-done.22.p1), channel_id=1, source_target_pairs={{0,1},{1,0},{2,3},{3,2},{4,5},{5,4},{6,7},{7,6},{8,9},{9,8},{10,11... | collective-permute-start | bytes 1376264 | tf_op jit(solution)/shard_map/ppermute | solution.py:458
  75.7 8.8 %collective-permute-start.27 = (bf16[32,3584]{1,0:T(8,128)(2,1)S(1)}, bf16[32,3584]{1,0:T(8,128)(2,1)S(1)}, u32[]{:S(2)}, u32[]{:S(2)}) collective-permute-start(bf16[32,3584]{1,0:T(8,128)(2,1)S(1)} %collective-permute-done.21.refs_1_.p0), channel_id=1, source_target_pairs={{0,1},{1,0},{2,3},{3,2},{4,5},{5,4},{6,7},{7,6},{8,9},{9,8},{10,11... | collective-permute-start | bytes 688136 | tf_op jit(solution)/shard_map/ppermute | solution.py:458
  76.2 13.9 %collective-permute-start.26 = (bf16[32,3584]{1,0:T(8,128)(2,1)S(1)}, bf16[32,3584]{1,0:T(8,128)(2,1)S(1)}, u32[]{:S(2)}, u32[]{:S(2)}) collective-permute-start(bf16[32,3584]{1,0:T(8,128)(2,1)S(1)} %get-tuple-element.156.refs_0_), channel_id=1, source_target_pairs={{0,12},{1,13},{2,14},{3,15},{4,8},{5,9},{6,10},{7,11},{8,4},{9,5},... | collective-permute-start | bytes 688136 | tf_op jit(solution)/shard_map/ppermute | solution.py:501
  84.4 5.7 %collective-permute-start.25 = (bf16[32,3584]{1,0:T(8,128)(2,1)S(1)}, bf16[32,3584]{1,0:T(8,128)(2,1)S(1)}, u32[]{:S(2)}, u32[]{:S(2)}) collective-permute-start(bf16[32,3584]{1,0:T(8,128)(2,1)S(1)} %total.10.um_ref.base_ref), channel_id=1, source_target_pairs={{0,1},{1,0},{2,3},{3,2},{4,5},{5,4},{6,7},{7,6},{8,9},{9,8},{10,11... | collective-permute-start | bytes 688136 | tf_op jit(solution)/shard_map/ppermute | solution.py:458
  92.1 1.6 %collective-permute-start.29 = (bf16[32,3584]{1,0:T(8,128)(2,1)S(1)}, bf16[32,3584]{1,0:T(8,128)(2,1)S(1)}, u32[]{:S(2)}, u32[]{:S(2)}) collective-permute-start(bf16[32,3584]{1,0:T(8,128)(2,1)S(1)} %get-tuple-element.163), channel_id=1, source_target_pairs={{0,1},{1,0},{2,3},{3,2},{4,5},{5,4},{6,7},{7,6},{8,9},{9,8},{10,11... | collective-permute-start | bytes 688136 | tf_op jit(solution)/shard_map/ppermute | solution.py:458
  92.2 9.6 %collective-permute-start.35 = (bf16[64,3584]{1,0:T(8,128)(2,1)S(1)}, bf16[64,3584]{1,0:T(8,128)(2,1)S(1)}, u32[]{:S(2)}, u32[]{:S(2)}) collective-permute-start(bf16[64,3584]{1,0:T(8,128)(2,1)S(1)} %stack.115), channel_id=1, source_target_pairs={{0,1},{1,0},{2,3},{3,2},{4,5},{5,4},{6,7},{7,6},{8,24},{9,25},{10,... | collective-permute-start | bytes 1376264 | tf_op jit(solution)/shard_map/ppermute | solution.py:501
  94.0 7.7 %collective-permute-start.30 = (bf16[32,3584]{1,0:T(8,128)(2,1)S(1)}, bf16[32,3584]{1,0:T(8,128)(2,1)S(1)}, u32[]{:S(2)}, u32[]{:S(2)}) collective-permute-start(bf16[32,3584]{1,0:T(8,128)(2,1)S(1)} %hold.11.refs_0_), channel_id=1, source_target_pairs={{0,2},{1,3},{2,0},{3,1},{4,6},{5,7},{6,4},{7,5},{8,10},{9,11},{10,... | collective-permute-start | bytes 688136 | tf_op jit(solution)/shard_map/ppermute | solution.py:461
  101.8 10.0 %collective-permute-start.37 = (bf16[64,3584]{1,0:T(8,128)(2,1)S(1)}, bf16[64,3584]{1,0:T(8,128)(2,1)S(1)}, u32[]{:S(2)}, u32[]{:S(2)}) collective-permute-start(bf16[64,3584]{1,0:T(8,128)(2,1)S(1)} %collective-permute-done.35.q1.refs_7_), channel_id=1, source_target_pairs={{0,1},{1,0},{2,3},{3,2},{4,5},{5,4},{6,7},{7,6},{8,9},{9,8},{10,11... | collective-permute-start | bytes 1376264 | tf_op jit(solution)/shard_map/ppermute | solution.py:458
  101.9 6.8 %collective-permute-start.36 = (bf16[32,3584]{1,0:T(8,128)(2,1)S(1)}, bf16[32,3584]{1,0:T(8,128)(2,1)S(1)}, u32[]{:S(2)}, u32[]{:S(2)}) collective-permute-start(bf16[32,3584]{1,0:T(8,128)(2,1)S(1)} %collective-permute-done.26.refs_1_.q0.refs_6_), channel_id=1, source_target_pairs={{0,1},{1,0},{2,3},{3,2},{4,5},{5,4},{6,7},{7,6},{8,9},{9,8},{10,11... | collective-permute-start | bytes 688136 | tf_op jit(solution)/shard_map/ppermute | solution.py:458
  102.7 12.6 %collective-permute-start.33 = (bf16[32,3584]{1,0:T(8,128)(2,1)S(1)}, bf16[32,3584]{1,0:T(8,128)(2,1)S(1)}, u32[]{:S(2)}, u32[]{:S(2)}) collective-permute-start(bf16[32,3584]{1,0:T(8,128)(2,1)S(1)} %get-tuple-element.165), channel_id=1, source_target_pairs={{0,8},{1,9},{2,10},{3,11},{4,16},{5,17},{6,18},{7,19},{8,20},{9,21... | collective-permute-start | bytes 688136 | tf_op jit(solution)/shard_map/ppermute | solution.py:501
  108.5 10.9 %collective-permute-start.31 = (bf16[32,3584]{1,0:T(8,128)(2,1)S(1)}, bf16[32,3584]{1,0:T(8,128)(2,1)S(1)}, u32[]{:S(2)}, u32[]{:S(2)}) collective-permute-start(bf16[32,3584]{1,0:T(8,128)(2,1)S(1)} %get-tuple-element.165), channel_id=1, source_target_pairs={{0,8},{1,9},{2,10},{3,11},{4,0},{5,1},{6,2},{7,3},{8,4},{9,5},{10,... | collective-permute-start | bytes 688136 | tf_op jit(solution)/shard_map/ppermute | solution.py:501
  108.6 18.3 %collective-permute-start.34 = (bf16[32,3584]{1,0:T(8,128)(2,1)S(1)}, bf16[32,3584]{1,0:T(8,128)(2,1)S(1)}, u32[]{:S(2)}, u32[]{:S(2)}) collective-permute-start(bf16[32,3584]{1,0:T(8,128)(2,1)S(1)} %get-tuple-element.166), channel_id=1, source_target_pairs={{0,8},{1,9},{2,10},{3,11},{4,20},{5,21},{6,22},{7,23},{8,16},{9,17... | collective-permute-start | bytes 688136 | tf_op jit(solution)/shard_map/ppermute | solution.py:501
  108.6 20.4 %collective-permute-start.32 = (bf16[32,3584]{1,0:T(8,128)(2,1)S(1)}, bf16[32,3584]{1,0:T(8,128)(2,1)S(1)}, u32[]{:S(2)}, u32[]{:S(2)}) collective-permute-start(bf16[32,3584]{1,0:T(8,128)(2,1)S(1)} %get-tuple-element.166), channel_id=1, source_target_pairs={{0,8},{1,9},{2,10},{3,11},{4,5},{5,4},{6,7},{7,6},{8,0},{9,1},{10,... | collective-permute-start | bytes 688136 | tf_op jit(solution)/shard_map/ppermute | solution.py:501
  129.2 2.5 %collective-permute-start.38 = (bf16[128,3584]{1,0:T(8,128)(2,1)S(1)}, bf16[128,3584]{1,0:T(8,128)(2,1)S(1)}, u32[]{:S(2)}, u32[]{:S(2)}) collective-permute-start(bf16[128,3584]{1,0:T(8,128)(2,1)S(1)} %stack.116.refs_0_), channel_id=1, source_target_pairs={{0,1},{1,0},{2,3},{3,2},{4,5},{5,4},{6,7},{7,6},{8,9},{9,8},{10,11... | collective-permute-start | bytes 2752520 | tf_op jit(solution)/shard_map/ppermute | solution.py:458
where the time goes:
time: 136 us
  waiting for transfers between devices  57.7 us (42%)
  starting transfers between devices  47.5 us (35%)
  Pallas kernels  30.3 us (22%)
    ppermute x20, starting transfers between devices, send(): return lax.ppermute(block, ('pipe', 'tensor'), completed(moves))  41 us
    pallas_call x27, Pallas kernels, call(): pl.pallas_call(kernel, out_shape=outs, in_specs=specs, out_specs=[out_spe...  30.3 us
    ppermute x20, waiting for transfers between devices, send(): return lax.ppermute(block, ('pipe', 'tensor'), completed(moves))  29.9 us
    ppermute x16, waiting for transfers between devices, swap_core(): return lax.ppermute(block, 'tensor', core_swap)  14.5 us
    ppermute x3, waiting for transfers between devices, swap_chip(): return lax.ppermute(block, 'tensor', chip_swap)  13.2 us
    ppermute x3, starting transfers between devices, swap_chip(): return lax.ppermute(block, 'tensor', chip_swap)  3.59 us
    ppermute x16, starting transfers between devices, swap_core(): return lax.ppermute(block, 'tensor', core_swap)  2.91 us
  transfers between devices with their start and end apart: 39, of which 27 were waited for; matrix products, arithmetic and copies ran while one was open for 0% of the time, Pallas kernels for 9%

commit v1 on v0

--- a/solution.py
+++ b/solution.py
@@ -137,8 +137,20 @@
     gate_ref[...], upper_ref[...] = forward_math(copies, xm_ref, xo_ref, gain, w_buf, pm_ref, po_ref, normed)
 
 
-def load_kernel(flags_ref, rows_ref, cot_ref, w_ref, w_buf, xs_ref, us_ref, um_ref, uo_ref, sems, row_sems):
-    copies = list(weight_copies(own_index(flags_ref, 1), w_ref, w_buf, sems, w_buf.shape[1]).values())
+def load_kernel(flags_ref, cot_ref, w_ref, w_buf, um_ref, uo_ref, sems, row_sems):
+    copies = [
+        pltpu.make_async_copy(cot_ref.at[flags_ref[OWN + i]], ref, row_sems.at[i])
+        for i, ref in enumerate((um_ref, uo_ref))
+    ]
+    copies += list(weight_copies(own_index(flags_ref, 1), w_ref, w_buf, sems, w_buf.shape[1]).values())
+    for copy in copies:
+        copy.start()
+    for copy in copies:
+        copy.wait()
+
+
+def rows_kernel(flags_ref, rows_ref, cot_ref, xs_ref, us_ref, row_sems):
+    copies = []
     pieces, rows = xs_ref.shape[:2]
     group = rows // 2
     for i in range(pieces):
@@ -150,8 +162,6 @@
                     rows_ref.at[flags_ref[base + i], part], xs_ref.at[i, part], row_sems.at[1 + half, i]
                 )
             )
-    for i, ref in enumerate((um_ref, uo_ref)):
-        copies.append(pltpu.make_async_copy(cot_ref.at[flags_ref[OWN + i]], ref, row_sems.at[3, i]))
     for copy in copies:
         copy.start()
     for copy in copies:
@@ -486,7 +496,7 @@
                     ends.remove(target[i])
         return sorted(target.items())
 
-    def send(block, *routes):
+    def send(block, *routes, whole=True):
         moves = []
         for copy in range(REPL):
             for end in range(2):
@@ -498,7 +508,7 @@
                         for rank in range(ranks):
                             came = (rank + 2) % ranks if source[3] else rank
                             moves.append((place(*source[:3], came), place(copy, end, c, rank)))
-        return lax.ppermute(block, ("pipe", "tensor"), completed(moves))
+        return lax.ppermute(block, ("pipe", "tensor"), completed(moves) if whole else moves)
 
     def hop(block, source, target, turn, other):
         return send(block, lambda copy, end, c: (copy, end ^ turn, source, other) if c == target else None)
@@ -580,13 +590,24 @@
     loaded = call(
         load_kernel,
         "load_late",
-        [flags, blocks, cot_blocks, weights],
-        [held_shape, pieces, pieces, row, row],
-        [pltpu.SemaphoreType.DMA((3, 1)), pltpu.SemaphoreType.DMA((4, 4 * REPL))],
+        [flags, cot_blocks, weights],
+        [held_shape, row, row],
+        [pltpu.SemaphoreType.DMA((3, 1)), pltpu.SemaphoreType.DMA((2,))],
         4,
         0,
         2 * layer_bytes,
-        hbm=(1, 2, 3),
+        hbm=(1, 2),
+    )
+    loaded_rows = call(
+        rows_kernel,
+        "load_rows",
+        [flags, blocks, cot_blocks],
+        [pieces, pieces],
+        [pltpu.SemaphoreType.DMA((3, 4 * REPL))],
+        4,
+        0,
+        layer_bytes,
+        hbm=(1, 2),
     )
     for step in range(sections - 1):
         part = 0 if step < middle else 1
@@ -613,22 +634,21 @@
                 layer_flops // 3,
                 layer_bytes // 3,
                 smem=(),
-            )
+            ) + loaded_rows
         if step == middle - 1:
             mine = total([held, swap_chip(held)])
             other = swap_core(mine)
         else:
             mine, other, during, _ = across(held, kind_of(step), kind_of(step + 1), during)
         if step == 0:
-            held_late, input_rows, cot_rows, up_mine, up_other = during
+            held_late, up_mine, up_other = during
         if step == middle:
-            (d_active,) = during
+            d_active, input_rows, cot_rows = during
 
     early_rows = saved[0][2:]
     sides = call(sides_kernel, "sides", [marks, saved[0][2], saved[1][2]], [row, row], [], 4, 0, 0, smem=())
     mine, (same, opposite) = lax.optimization_barrier((mine, sides))
     state_first = flow(opposite, 0, middle_class)
-    state_second = flow(joined(same, state_first), 1, middle_class)
     gates = [saved[0][:2], saved[1][:2]]
     pm, po, late_mine, late_other = layer(
         turn_kernel,
@@ -653,32 +673,33 @@
             ups[part] = kept[:2]
         held = hold(part, True, [pm, swap_core(po), up_mine, state_mine[part], gains], step not in (middle, 1))
         if step == 1:
+            held, middle_arrived = lax.optimization_barrier((held, middle_arrived))
             mine = total([held, swap_chip(held)])
         elif step == middle:
             held, mixed = lax.optimization_barrier((held, kept[2]))
             up_mine = total([held, swap_chip(held)])
             mixed_first = flow(mixed, 0, far)
-            up_other, mixed_first, middle_arrived = lax.optimization_barrier(
-                (swap_core(up_mine), mixed_first, middle_arrived)
+            up_other, mixed_first, state_second = lax.optimization_barrier(
+                (swap_core(up_mine), mixed_first, state_second)
             )
+            middle_arrived = with_other_core([state_first, state_second])
             mixed_second = flow(joined(mixed, mixed_first), 1, far)
         else:
-            later = ()
+            during = [state_first] if step == sections - 1 else []
+            up_mine, up_other, during, _ = across(held, kind_of(step), kind_of(step - 1), during)
             if step == sections - 1:
-                later = [state_first, state_second]
-            up_mine, up_other, _, later = across(held, kind_of(step), kind_of(step - 1), (), later)
-            if step == sections - 1:
-                middle_arrived = with_other_core(later)
+                (state_first,) = during
+                state_second = flow(joined(same, state_first), 1, middle_class)
     _, mixed_second = lax.optimization_barrier((mine, mixed_second))
     def last_route(shift, source):
         return lambda copy, end, c: ((copy + shift) % REPL, source, 1, False) if c == 0 and end == 0 else None
 
     payloads = call(last_kernel, "last", [marks, mine, ups[0][0]], [row] * 2, [], 4, 0, 0, smem=())
     straight = [
-        send(payloads[0], last_route(0, 0), flow_route(0, middle_near)),
-        send(payloads[1], last_route(0, 1)),
-        send(payloads[0], last_route(1, 0), flow_route(2, middle_near)),
-        send(payloads[1], last_route(1, 1), flow_route(1, middle_near)),
+        send(payloads[0], last_route(0, 0), flow_route(0, middle_near), whole=False),
+        send(payloads[1], last_route(0, 1), whole=False),
+        send(payloads[0], last_route(1, 0), flow_route(2, middle_near), whole=False),
+        send(payloads[1], last_route(1, 1), flow_route(1, middle_near), whole=False),
     ]
     mixed_arrived = with_other_core([mixed_first, mixed_second])
     prepared = call(

time: 136 us -> 136 us (level)
  starting transfers between devices: 47.5 us -> 31.3 us
  waiting for transfers between devices: 57.7 us -> 72.1 us
  Pallas kernels: 30.3 us -> 31.8 us
    ppermute x20, starting transfers between devices: 41 us -> 24.1 us  [send(): lax.ppermute(block, ('pipe', 'tensor'), completed(moves) if whole else mo...]
    ppermute x20, waiting for transfers between devices: 29.9 us -> 40.2 us  [send(): lax.ppermute(block, ('pipe', 'tensor'), completed(moves) if whole else mo...]
    ppermute x3, waiting for transfers between devices: 13.2 us -> 17.6 us  [swap_chip(): return lax.ppermute(block, 'tensor', chip_swap)]
    pallas_call x27 -> x28, Pallas kernels: 30.3 us -> 31.8 us  [call(): pl.pallas_call(kernel, out_shape=outs, in_specs=specs, out_specs=[out_spe...]
  transfers between devices with their start and end apart: 39 -> 39, of which waited for: 27 -> 28; matrix products, arithmetic and copies ran while one was open for 0% -> 0% of each run, Pallas kernels for 9% -> 10%
where the time goes in v1:
time: 136 us
  waiting for transfers between devices  72.1 us (53%)
  Pallas kernels  31.8 us (23%)
  starting transfers between devices  31.3 us (23%)
    ppermute x20, waiting for transfers between devices, send(): lax.ppermute(block, ('pipe', 'tensor'), completed(moves) if whole else mo...  40.2 us
    pallas_call x28, Pallas kernels, call(): pl.pallas_call(kernel, out_shape=outs, in_specs=specs, out_specs=[out_spe...  31.8 us
    ppermute x20, starting transfers between devices, send(): lax.ppermute(block, ('pipe', 'tensor'), completed(moves) if whole else mo...  24.1 us
    ppermute x3, waiting for transfers between devices, swap_chip(): return lax.ppermute(block, 'tensor', chip_swap)  17.6 us
    ppermute x16, waiting for transfers between devices, swap_core(): return lax.ppermute(block, 'tensor', core_swap)  14.3 us
    ppermute x3, starting transfers between devices, swap_chip(): return lax.ppermute(block, 'tensor', chip_swap)  4.26 us
    ppermute x16, starting transfers between devices, swap_core(): return lax.ppermute(block, 'tensor', core_swap)  3.01 us
  transfers between devices with their start and end apart: 39, of which 28 were waited for; matrix products, arithmetic and copies ran while one was open for 0% of the time, Pallas kernels for 10%

profile of v1, /device:TPU:0, one launch (start us, length us, event | category | flops | bytes accessed | tf_op | source)
XLA Modules:
  0.0 135.8 jit_solution(2688819195916597245)
XLA Ops:
  0.1 5.5 %first_layer.1 = (bf16[32,3584]{1,0:T(8,128)(2,1)S(1)}, bf16[32,3584]{1,0:T(8,128)(2,1)S(1)}, f32[64,256]{1,0:T(8,128)S(1)}, f32[64,256]{1,0:T(8,128)S(1)}, bf16...) custom-call(s32[29]{0:T(128)S(1)} %stack.110.flags_ref, ...), custom_call_target="tpu_custom_call" | custom-call | flops 352321536 | bytes 5505024 | tf_op jit(solution)/shard_map/first_layer/pallas_call | solution.py:418
  6.1 1.1 collective-permute-done.recv_ref
  7.4 3.9 %collective-permute-start.3 = (bf16[16,3584]{1,0:T(8,128)(2,1)S(1)}, bf16[16,3584]{1,0:T(8,128)(2,1)S(1)}, u32[]{:S(2)}, u32[]{:S(2)}) collective-permute-start(bf16[16,3584]{1,0:T(8,128)(2,1)S(1)} %get-tuple-element.102), channel_id=1, source_target_pairs={{0,6},{1,7},{2,4},{3,5},{4,2},{5,3},{6,0},{7,1},{8,14},{9,15},{10,... | collective-permute-start | bytes 344072 | tf_op jit(solution)/shard_map/ppermute | solution.py:511
  11.8 1.5 %collective-permute-start.4 = (bf16[16,3584]{1,0:T(8,128)(2,1)S(1)}, bf16[16,3584]{1,0:T(8,128)(2,1)S(1)}, u32[]{:S(2)}, u32[]{:S(2)}) collective-permute-start(bf16[16,3584]{1,0:T(8,128)(2,1)S(1)} %get-tuple-element.103), channel_id=1, source_target_pairs={{0,10},{1,11},{2,8},{3,9},{4,14},{5,15},{6,12},{7,13},{8,2},{9,3},... | collective-permute-start | bytes 344072 | tf_op jit(solution)/shard_map/ppermute | solution.py:511
  13.4 3.4 %load_late.1 = (bf16[3,3584,256]{2,1,0:T(8,128)(2,1)S(1)}, bf16[32,3584]{1,0:T(8,128)(2,1)S(1)}, bf16[32,3584]{1,0:T(8,128)(2,1)S(1)}) custom-call(s32[29]{0:T(128)S(1)} %stack.110.flags_ref, bf16[8,32,3584]{2,1,0:T(8,128)(2,1)} %bitcast.36, bf16[2,3,3584,256]{3,2,1,0:T(8,128)(2,1)} %bitcast.34), custom_call_target="tpu_custom_call" | custom-call | bytes 11010048 | tf_op jit(solution)/shard_map/load_late/pallas_call | solution.py:418
  16.8 0.6 collective-permute-done.1.refs_0_
  17.5 1.2 collective-permute-done.4.refs_3_
  19.2 1.5 %collective-permute-done.5.xo_ref = bf16[32,3584]{1,0:T(8,128)(2,1)S(1)} collective-permute-done((bf16[32,3584]{1,0:T(8,128)(2,1)S(1)}, bf16[32,3584]{1,0:T(8,128)(2,1)S(1)}, u32[]{:S(2)}, u32[]{:S(2)}) %collective-permute-start.5) | collective-permute-done | bytes 229408 | tf_op jit(solution)/shard_map/ppermute | solution.py:468
  20.7 1.6 %forward_layer.2 = (bf16[32,3584]{1,0:T(8,128)(2,1)S(1)}, bf16[32,3584]{1,0:T(8,128)(2,1)S(1)}, f32[64,256]{1,0:T(8,128)S(1)}, f32[64,256]{1,0:T(8,128)S(1)}, bf...) custom-call(s32[8,128]{1,0:T(8,128)S(1)} %get-tuple-element.98.flags_ref.marks_ref, ...), custom_call_target="tpu_custom_call" | custom-call | flops 352321536 | bytes 5505024 | tf_op jit(solution)/shard_map/forward_layer/pallas_call | solution.py:418
  22.5 1.3 collective-permute-done.6.recv_ref
  24.0 1.4 %collective-permute-start.7 = (bf16[32,3584]{1,0:T(8,128)(2,1)S(1)}, bf16[32,3584]{1,0:T(8,128)(2,1)S(1)}, u32[]{:S(2)}, u32[]{:S(2)}) collective-permute-start(bf16[32,3584]{1,0:T(8,128)(2,1)S(1)} %hold.7.refs_0_), channel_id=1, source_target_pairs={{0,2},{1,3},{2,0},{3,1},{4,6},{5,7},{6,4},{7,5},{8,10},{9,11},{10,... | collective-permute-start | bytes 688136 | tf_op jit(solution)/shard_map/ppermute | solution.py:471
  25.5 6.3 %collective-permute-done.7.refs_1_ = bf16[32,3584]{1,0:T(8,128)(2,1)S(1)} collective-permute-done((bf16[32,3584]{1,0:T(8,128)(2,1)S(1)}, bf16[32,3584]{1,0:T(8,128)(2,1)S(1)}, u32[]{:S(2)}, u32[]{:S(2)}) %collective-permute-start.7) | collective-permute-done | bytes 229408 | tf_op jit(solution)/shard_map/ppermute | solution.py:471
  31.9 1.5 %collective-permute-done.8.xo_ref = bf16[32,3584]{1,0:T(8,128)(2,1)S(1)} collective-permute-done((bf16[32,3584]{1,0:T(8,128)(2,1)S(1)}, bf16[32,3584]{1,0:T(8,128)(2,1)S(1)}, u32[]{:S(2)}, u32[]{:S(2)}) %collective-permute-start.8) | collective-permute-done | bytes 229408 | tf_op jit(solution)/shard_map/ppermute | solution.py:468
  33.4 1.5 %forward_layer.3 = (bf16[32,3584]{1,0:T(8,128)(2,1)S(1)}, bf16[32,3584]{1,0:T(8,128)(2,1)S(1)}, f32[64,256]{1,0:T(8,128)S(1)}, f32[64,256]{1,0:T(8,128)S(1)}, bf...) custom-call(s32[8,128]{1,0:T(8,128)S(1)} %get-tuple-element.98.flags_ref.marks_ref, ...), custom_call_target="tpu_custom_call" | custom-call | flops 352321536 | bytes 5505024 | tf_op jit(solution)/shard_map/forward_layer/pallas_call | solution.py:418
  35.1 1.4 collective-permute-done.9.recv_ref
  36.6 2.3 %collective-permute-start.12 = (bf16[16,3584]{1,0:T(8,128)(2,1)S(1)}, bf16[16,3584]{1,0:T(8,128)(2,1)S(1)}, u32[]{:S(2)}, u32[]{:S(2)}) collective-permute-start(bf16[16,3584]{1,0:T(8,128)(2,1)S(1)} %get-tuple-element.120), channel_id=1, source_target_pairs={{0,6},{1,7},{2,4},{3,5},{4,2},{5,3},{6,0},{7,1},{8,14},{9,15},{10,... | collective-permute-start | bytes 344072 | tf_op jit(solution)/shard_map/ppermute | solution.py:511
  39.5 1.6 %collective-permute-start.13 = (bf16[16,3584]{1,0:T(8,128)(2,1)S(1)}, bf16[16,3584]{1,0:T(8,128)(2,1)S(1)}, u32[]{:S(2)}, u32[]{:S(2)}) collective-permute-start(bf16[16,3584]{1,0:T(8,128)(2,1)S(1)} %get-tuple-element.121), channel_id=1, source_target_pairs={{0,10},{1,11},{2,8},{3,9},{4,14},{5,15},{6,12},{7,13},{8,2},{9,3},... | collective-permute-start | bytes 344072 | tf_op jit(solution)/shard_map/ppermute | solution.py:511
  41.6 2.9 %load_rows.1 = (bf16[8,32,3584]{2,1,0:T(8,128)(2,1)S(1)}, bf16[8,32,3584]{2,1,0:T(8,128)(2,1)S(1)}) custom-call(s32[29]{0:T(128)S(1)} %stack.110.flags_ref, bf16[8,32,3584]{2,1,0:T(8,128)(2,1)} %bitcast.39, bf16[8,32,3584]{2,1,0:T(8,128)(2,1)} %bitcast.37), custom_call_target="tpu_custom_call" | custom-call | bytes 5505024 | tf_op jit(solution)/shard_map/load_rows/pallas_call | solution.py:418
  45.1 1.2 collective-permute-done.13.refs_3_
  47.2 1.3 collective-permute-done.14.xo_ref
  48.4 2.2 %turn_layer.1 = (bf16[32,3584]{1,0:T(8,128)(2,1)S(1)}, bf16[32,3584]{1,0:T(8,128)(2,1)S(1)}, bf16[32,3584]{1,0:T(8,128)(2,1)S(1)}, bf16[32,3584]{1,0:T(8,128)(2,1)S(1)}) custom-call(s32[8,128]{1,0:T(8,128)S(1)} %get-tuple-element.98.flags_ref.marks_ref, f32[64,256]{1,0:T(8,128)S(1)} %cotangent.1.d_ref, bf16[32,3584]{1,0:T(8,128)(2,1)S(1)} %total.8.xm_ref, ...), custom_call_target="tpu_custom_call" | custom-call | flops 352321536 | bytes 5505024 | tf_op jit(solution)/shard_map/turn_layer/pallas_call | solution.py:418
  51.2 1.0 collective-permute-done.15.recv_ref
  52.6 2.5 %collective-permute-start.18 = (bf16[16,3584]{1,0:T(8,128)(2,1)S(1)}, bf16[16,3584]{1,0:T(8,128)(2,1)S(1)}, u32[]{:S(2)}, u32[]{:S(2)}) collective-permute-start(bf16[16,3584]{1,0:T(8,128)(2,1)S(1)} %get-tuple-element.141), channel_id=1, source_target_pairs={{0,6},{1,7},{2,4},{3,5},{4,2},{5,3},{6,0},{7,1},{8,14},{9,15},{10,... | collective-permute-start | bytes 344072 | tf_op jit(solution)/shard_map/ppermute | solution.py:511
  55.4 1.7 %collective-permute-start.19 = (bf16[16,3584]{1,0:T(8,128)(2,1)S(1)}, bf16[16,3584]{1,0:T(8,128)(2,1)S(1)}, u32[]{:S(2)}, u32[]{:S(2)}) collective-permute-start(bf16[16,3584]{1,0:T(8,128)(2,1)S(1)} %get-tuple-element.142), channel_id=1, source_target_pairs={{0,10},{1,11},{2,8},{3,9},{4,14},{5,15},{6,12},{7,13},{8,2},{9,3},... | collective-permute-start | bytes 344072 | tf_op jit(solution)/shard_map/ppermute | solution.py:511
  57.6 3.9 %collective-permute-done.18.refs_2_ = bf16[16,3584]{1,0:T(8,128)(2,1)S(1)} collective-permute-done((bf16[16,3584]{1,0:T(8,128)(2,1)S(1)}, bf16[16,3584]{1,0:T(8,128)(2,1)S(1)}, u32[]{:S(2)}, u32[]{:S(2)}) %collective-permute-start.18) | collective-permute-done | bytes 114720 | tf_op jit(solution)/shard_map/ppermute | solution.py:511
  61.5 2.4 %collective-permute-done.16.refs_0_ = bf16[16,3584]{1,0:T(8,128)(2,1)S(1)} collective-permute-done((bf16[16,3584]{1,0:T(8,128)(2,1)S(1)}, bf16[16,3584]{1,0:T(8,128)(2,1)S(1)}, u32[]{:S(2)}, u32[]{:S(2)}) %collective-permute-start.16) | collective-permute-done | bytes 114720 | tf_op jit(solution)/shard_map/ppermute | solution.py:511
  63.9 0.7 collective-permute-done.17.refs_1_
  64.7 1.5 %collective-permute-done.21.uo_ref = bf16[32,3584]{1,0:T(8,128)(2,1)S(1)} collective-permute-done((bf16[32,3584]{1,0:T(8,128)(2,1)S(1)}, bf16[32,3584]{1,0:T(8,128)(2,1)S(1)}, u32[]{:S(2)}, u32[]{:S(2)}) %collective-permute-start.21) | collective-permute-done | bytes 229408 | tf_op jit(solution)/shard_map/ppermute | solution.py:468
  66.2 2.1 %backward_layer.2 = (bf16[32,3584]{1,0:T(8,128)(2,1)S(1)}, bf16[32,3584]{1,0:T(8,128)(2,1)S(1)}, bf16[32,3584]{1,0:T(8,128)(2,1)S(1)}, bf16[32,3584]{1,0:T(8,128)(2,1)S(1)}, bf16[32,3584]{1,0:T(8,128)(2,1)S(1)}) custom-call(s32[8,128]{1,0:T(8,128)S(1)} %get-tuple-element.98.flags_ref.marks_ref, bf16[32,3584]{1,0:T(8,128)(2,1)S(1)} %total.9.um_ref.base_ref, ...), custom_call_target="tpu_custom_call" | custom-call | flops 352321536 | bytes 5505024 | tf_op jit(solution)/shard_map/backward_layer/pallas_call | solution.py:418
  69.0 0.9 collective-permute-done.22.recv_ref
  70.2 1.4 %collective-permute-start.23 = (bf16[32,3584]{1,0:T(8,128)(2,1)S(1)}, bf16[32,3584]{1,0:T(8,128)(2,1)S(1)}, u32[]{:S(2)}, u32[]{:S(2)}) collective-permute-start(bf16[32,3584]{1,0:T(8,128)(2,1)S(1)} %hold.10.refs_0_), channel_id=1, source_target_pairs={{0,2},{1,3},{2,0},{3,1},{4,6},{5,7},{6,4},{7,5},{8,10},{9,11},{10,... | collective-permute-start | bytes 688136 | tf_op jit(solution)/shard_map/ppermute | solution.py:471
  71.6 1.6 %collective-permute-start.25 = (bf16[32,3584]{1,0:T(8,128)(2,1)S(1)}, bf16[32,3584]{1,0:T(8,128)(2,1)S(1)}, u32[]{:S(2)}, u32[]{:S(2)}) collective-permute-start(bf16[32,3584]{1,0:T(8,128)(2,1)S(1)} %get-tuple-element.154.refs_0_), channel_id=1, source_target_pairs={{0,12},{1,13},{2,14},{3,15},{4,8},{5,9},{6,10},{7,11},{8,4},{9,5},... | collective-permute-start | bytes 688136 | tf_op jit(solution)/shard_map/ppermute | solution.py:511
  73.2 4.8 %collective-permute-done.23.refs_1_ = bf16[32,3584]{1,0:T(8,128)(2,1)S(1)} collective-permute-done((bf16[32,3584]{1,0:T(8,128)(2,1)S(1)}, bf16[32,3584]{1,0:T(8,128)(2,1)S(1)}, u32[]{:S(2)}, u32[]{:S(2)}) %collective-permute-start.23) | collective-permute-done | bytes 229408 | tf_op jit(solution)/shard_map/ppermute | solution.py:471
  78.1 10.3 %collective-permute-done.25.refs_1_.q0.refs_6_ = bf16[32,3584]{1,0:T(8,128)(2,1)S(1)} collective-permute-done((bf16[32,3584]{1,0:T(8,128)(2,1)S(1)}, bf16[32,3584]{1,0:T(8,128)(2,1)S(1)}, u32[]{:S(2)}, u32[]{:S(2)}) %collective-permute-start.25) | collective-permute-done | bytes 229408 | tf_op jit(solution)/shard_map/ppermute | solution.py:511
  88.4 1.9 %backward_layer.3 = (bf16[32,3584]{1,0:T(8,128)(2,1)S(1)}, bf16[32,3584]{1,0:T(8,128)(2,1)S(1)}, bf16[32,3584]{1,0:T(8,128)(2,1)S(1)}, bf16[32,3584]{1,0:T(8,128)(2,1)S(1)}) custom-call(s32[8,128]{1,0:T(8,128)S(1)} %get-tuple-element.98.flags_ref.marks_ref, bf16[32,3584]{1,0:T(8,128)(2,1)S(1)} %total.10.um_ref.base_ref, ...), custom_call_target="tpu_custom_call" | custom-call | flops 352321536 | bytes 5505024 | tf_op jit(solution)/shard_map/backward_layer/pallas_call | solution.py:418
  92.5 1.4 %collective-permute-start.30 = (bf16[32,3584]{1,0:T(8,128)(2,1)S(1)}, bf16[32,3584]{1,0:T(8,128)(2,1)S(1)}, u32[]{:S(2)}, u32[]{:S(2)}) collective-permute-start(bf16[32,3584]{1,0:T(8,128)(2,1)S(1)} %hold.11.refs_0_), channel_id=1, source_target_pairs={{0,2},{1,3},{2,0},{3,1},{4,6},{5,7},{6,4},{7,5},{8,10},{9,11},{10,... | collective-permute-start | bytes 688136 | tf_op jit(solution)/shard_map/ppermute | solution.py:471
  93.9 6.5 %collective-permute-done.30.refs_1_ = bf16[32,3584]{1,0:T(8,128)(2,1)S(1)} collective-permute-done((bf16[32,3584]{1,0:T(8,128)(2,1)S(1)}, bf16[32,3584]{1,0:T(8,128)(2,1)S(1)}, u32[]{:S(2)}, u32[]{:S(2)}) %collective-permute-start.30) | collective-permute-done | bytes 229408 | tf_op jit(solution)/shard_map/ppermute | solution.py:471
  101.4 1.3 collective-permute-start.33
  102.7 1.3 collective-permute-start.31
  104.0 1.3 collective-permute-start.34
  105.3 1.3 collective-permute-start.32
  106.7 3.5 %own_first.1 = (bf16[3584,256]{1,0:T(8,128)(2,1)S(1)}, f32[256,256]{1,0:T(8,128)S(1)}, f32[256,256]{1,0:T(8,128)S(1)}, bf16[256,256]{1,0:T(8,128)(2,1)S(1)}) custom-call(s32[29]{0:T(128)S(1)} %stack.110.flags_ref, bf16[8,32,3584]{2,1,0:T(8,128)(2,1)S(1)} %get-tuple-element.167.xs_ref, bf16[32,3584]{1,0:T(8,128)(2,1)S(1)} %get-tuple-element.132.early_ref.refs_0_.em_ref, ...), custom_call_target="tpu_custom_call" | custom-call | flops 939524096 | bytes 7340032 | tf_op jit(solution)/shard_map/own_first/pallas_call | solution.py:418
  110.2 3.1 %collective-permute-done.33.refs_2_ = bf16[32,3584]{1,0:T(8,128)(2,1)S(1)} collective-permute-done((bf16[32,3584]{1,0:T(8,128)(2,1)S(1)}, bf16[32,3584]{1,0:T(8,128)(2,1)S(1)}, u32[]{:S(2)}, u32[]{:S(2)}) %collective-permute-start.33) | collective-permute-done | bytes 229408 | tf_op jit(solution)/shard_map/ppermute | solution.py:511
  113.3 4.3 %collective-permute-done.31.refs_0_ = bf16[32,3584]{1,0:T(8,128)(2,1)S(1)} collective-permute-done((bf16[32,3584]{1,0:T(8,128)(2,1)S(1)}, bf16[32,3584]{1,0:T(8,128)(2,1)S(1)}, u32[]{:S(2)}, u32[]{:S(2)}) %collective-permute-start.31) | collective-permute-done | bytes 229408 | tf_op jit(solution)/shard_map/ppermute | solution.py:511
  117.6 8.2 %collective-permute-done.34.refs_3_ = bf16[32,3584]{1,0:T(8,128)(2,1)S(1)} collective-permute-done((bf16[32,3584]{1,0:T(8,128)(2,1)S(1)}, bf16[32,3584]{1,0:T(8,128)(2,1)S(1)}, u32[]{:S(2)}, u32[]{:S(2)}) %collective-permute-start.34) | collective-permute-done | bytes 229408 | tf_op jit(solution)/shard_map/ppermute | solution.py:511
  125.8 3.1 %collective-permute-done.32.refs_1_ = bf16[32,3584]{1,0:T(8,128)(2,1)S(1)} collective-permute-done((bf16[32,3584]{1,0:T(8,128)(2,1)S(1)}, bf16[32,3584]{1,0:T(8,128)(2,1)S(1)}, u32[]{:S(2)}, u32[]{:S(2)}) %collective-permute-start.32) | collective-permute-done | bytes 229408 | tf_op jit(solution)/shard_map/ppermute | solution.py:511
  129.1 2.4 %collective-permute-done.38.refs_1_ = bf16[128,3584]{1,0:T(8,128)(2,1)S(1)} collective-permute-done((bf16[128,3584]{1,0:T(8,128)(2,1)S(1)}, bf16[128,3584]{1,0:T(8,128)(2,1)S(1)}, u32[]{:S(2)}, u32[]{:S(2)}) %collective-permute-start.38) | collective-permute-done | bytes 917536 | tf_op jit(solution)/shard_map/ppermute | solution.py:468
  131.6 4.1 %own_last.1 = bf16[1,3,3584,256]{3,2,1,0:T(8,128)(2,1)} custom-call(s32[29]{0:T(128)S(1)} %stack.110.flags_ref, bf16[8,32,3584]{2,1,0:T(8,128)(2,1)S(1)} %get-tuple-element.126.us_ref, bf16[128,3584]{1,0:T(8,128)(2,1)S(1)} %stack.116.refs_0_, bf16[128,3584]{1,0:T(8,128)(2,1)S(1)} %collective-permute-done.38.refs_1_, ...), custom_call_target="tpu_custom_call" | custom-call | flops 1879048192 | bytes 7340032 | tf_op jit(solution)/shard_map/own_last/pallas_call | solution.py:418
  (61 shorter events, 11.5 us)
Async XLA Ops:
  5.6 1.6 %collective-permute-start = (bf16[32,3584]{1,0:T(8,128)(2,1)S(1)}, bf16[32,3584]{1,0:T(8,128)(2,1)S(1)}, u32[]{:S(2)}, u32[]{:S(2)}) collective-permute-start(bf16[32,3584]{1,0:T(8,128)(2,1)S(1)} %get-tuple-element.100), channel_id=1, source_target_pairs={{0,1},{1,0},{2,3},{3,2},{4,5},{5,4},{6,7},{7,6},{8,9},{9,8},{10,11... | collective-permute-start | bytes 688136 | tf_op jit(solution)/shard_map/ppermute | solution.py:468
  7.4 9.4 %collective-permute-start.3 = (bf16[16,3584]{1,0:T(8,128)(2,1)S(1)}, bf16[16,3584]{1,0:T(8,128)(2,1)S(1)}, u32[]{:S(2)}, u32[]{:S(2)}) collective-permute-start(bf16[16,3584]{1,0:T(8,128)(2,1)S(1)} %get-tuple-element.102), channel_id=1, source_target_pairs={{0,6},{1,7},{2,4},{3,5},{4,2},{5,3},{6,0},{7,1},{8,14},{9,15},{10,... | collective-permute-start | bytes 344072 | tf_op jit(solution)/shard_map/ppermute | solution.py:511
  11.3 6.2 %collective-permute-start.1 = (bf16[16,3584]{1,0:T(8,128)(2,1)S(1)}, bf16[16,3584]{1,0:T(8,128)(2,1)S(1)}, u32[]{:S(2)}, u32[]{:S(2)}) collective-permute-start(bf16[16,3584]{1,0:T(8,128)(2,1)S(1)} %get-tuple-element.102), channel_id=1, source_target_pairs={{0,4},{1,5},{2,6},{3,7},{4,0},{5,1},{6,2},{7,3},{8,12},{9,13},{10,... | collective-permute-start | bytes 344072 | tf_op jit(solution)/shard_map/ppermute | solution.py:511
  11.8 6.8 %collective-permute-start.4 = (bf16[16,3584]{1,0:T(8,128)(2,1)S(1)}, bf16[16,3584]{1,0:T(8,128)(2,1)S(1)}, u32[]{:S(2)}, u32[]{:S(2)}) collective-permute-start(bf16[16,3584]{1,0:T(8,128)(2,1)S(1)} %get-tuple-element.103), channel_id=1, source_target_pairs={{0,10},{1,11},{2,8},{3,9},{4,14},{5,15},{6,12},{7,13},{8,2},{9,3},... | collective-permute-start | bytes 344072 | tf_op jit(solution)/shard_map/ppermute | solution.py:511
  13.4 5.7 %collective-permute-start.2 = (bf16[16,3584]{1,0:T(8,128)(2,1)S(1)}, bf16[16,3584]{1,0:T(8,128)(2,1)S(1)}, u32[]{:S(2)}, u32[]{:S(2)}) collective-permute-start(bf16[16,3584]{1,0:T(8,128)(2,1)S(1)} %get-tuple-element.103), channel_id=1, source_target_pairs={{0,8},{1,9},{2,10},{3,11},{4,12},{5,13},{6,14},{7,15},{8,0},{9,1},... | collective-permute-start | bytes 344072 | tf_op jit(solution)/shard_map/ppermute | solution.py:511
  13.4 7.3 %copy-start = (f32[1,2,3584]{2,1,0:T(2,128)S(1)}, f32[1,2,3584]{2,1,0:T(2,128)}, u32[]{:S(2)}) copy-start(f32[1,2,3584]{2,1,0:T(2,128)} %param.7) | copy-start | bytes 86020
  19.2 1.6 %collective-permute-start.5 = (bf16[32,3584]{1,0:T(8,128)(2,1)S(1)}, bf16[32,3584]{1,0:T(8,128)(2,1)S(1)}, u32[]{:S(2)}, u32[]{:S(2)}) collective-permute-start(bf16[32,3584]{1,0:T(8,128)(2,1)S(1)} %total.6.xm_ref.base_ref), channel_id=1, source_target_pairs={{0,1},{1,0},{2,3},{3,2},{4,5},{5,4},{6,7},{7,6},{8,9},{9,8},{10,11... | collective-permute-start | bytes 688136 | tf_op jit(solution)/shard_map/ppermute | solution.py:468
  22.3 1.6 %collective-permute-start.6 = (bf16[32,3584]{1,0:T(8,128)(2,1)S(1)}, bf16[32,3584]{1,0:T(8,128)(2,1)S(1)}, u32[]{:S(2)}, u32[]{:S(2)}) collective-permute-start(bf16[32,3584]{1,0:T(8,128)(2,1)S(1)} %get-tuple-element.116), channel_id=1, source_target_pairs={{0,1},{1,0},{2,3},{3,2},{4,5},{5,4},{6,7},{7,6},{8,9},{9,8},{10,11... | collective-permute-start | bytes 688136 | tf_op jit(solution)/shard_map/ppermute | solution.py:468
  24.0 7.7 %collective-permute-start.7 = (bf16[32,3584]{1,0:T(8,128)(2,1)S(1)}, bf16[32,3584]{1,0:T(8,128)(2,1)S(1)}, u32[]{:S(2)}, u32[]{:S(2)}) collective-permute-start(bf16[32,3584]{1,0:T(8,128)(2,1)S(1)} %hold.7.refs_0_), channel_id=1, source_target_pairs={{0,2},{1,3},{2,0},{3,1},{4,6},{5,7},{6,4},{7,5},{8,10},{9,11},{10,... | collective-permute-start | bytes 688136 | tf_op jit(solution)/shard_map/ppermute | solution.py:471
  31.8 1.6 %collective-permute-start.8 = (bf16[32,3584]{1,0:T(8,128)(2,1)S(1)}, bf16[32,3584]{1,0:T(8,128)(2,1)S(1)}, u32[]{:S(2)}, u32[]{:S(2)}) collective-permute-start(bf16[32,3584]{1,0:T(8,128)(2,1)S(1)} %total.7.xm_ref.base_ref), channel_id=1, source_target_pairs={{0,1},{1,0},{2,3},{3,2},{4,5},{5,4},{6,7},{7,6},{8,9},{9,8},{10,11... | collective-permute-start | bytes 688136 | tf_op jit(solution)/shard_map/ppermute | solution.py:468
  34.9 1.6 %collective-permute-start.9 = (bf16[32,3584]{1,0:T(8,128)(2,1)S(1)}, bf16[32,3584]{1,0:T(8,128)(2,1)S(1)}, u32[]{:S(2)}, u32[]{:S(2)}) collective-permute-start(bf16[32,3584]{1,0:T(8,128)(2,1)S(1)} %get-tuple-element.119), channel_id=1, source_target_pairs={{0,1},{1,0},{2,3},{3,2},{4,5},{5,4},{6,7},{7,6},{8,9},{9,8},{10,11... | collective-permute-start | bytes 688136 | tf_op jit(solution)/shard_map/ppermute | solution.py:468
  36.6 8.3 %collective-permute-start.12 = (bf16[16,3584]{1,0:T(8,128)(2,1)S(1)}, bf16[16,3584]{1,0:T(8,128)(2,1)S(1)}, u32[]{:S(2)}, u32[]{:S(2)}) collective-permute-start(bf16[16,3584]{1,0:T(8,128)(2,1)S(1)} %get-tuple-element.120), channel_id=1, source_target_pairs={{0,6},{1,7},{2,4},{3,5},{4,2},{5,3},{6,0},{7,1},{8,14},{9,15},{10,... | collective-permute-start | bytes 344072 | tf_op jit(solution)/shard_map/ppermute | solution.py:511
  39.0 6.2 %collective-permute-start.10 = (bf16[16,3584]{1,0:T(8,128)(2,1)S(1)}, bf16[16,3584]{1,0:T(8,128)(2,1)S(1)}, u32[]{:S(2)}, u32[]{:S(2)}) collective-permute-start(bf16[16,3584]{1,0:T(8,128)(2,1)S(1)} %get-tuple-element.120), channel_id=1, source_target_pairs={{0,4},{1,5},{2,6},{3,7},{4,0},{5,1},{6,2},{7,3},{8,12},{9,13},{10,... | collective-permute-start | bytes 344072 | tf_op jit(solution)/shard_map/ppermute | solution.py:511
  39.5 6.8 %collective-permute-start.13 = (bf16[16,3584]{1,0:T(8,128)(2,1)S(1)}, bf16[16,3584]{1,0:T(8,128)(2,1)S(1)}, u32[]{:S(2)}, u32[]{:S(2)}) collective-permute-start(bf16[16,3584]{1,0:T(8,128)(2,1)S(1)} %get-tuple-element.121), channel_id=1, source_target_pairs={{0,10},{1,11},{2,8},{3,9},{4,14},{5,15},{6,12},{7,13},{8,2},{9,3},... | collective-permute-start | bytes 344072 | tf_op jit(solution)/shard_map/ppermute | solution.py:511
  41.2 5.7 %collective-permute-start.11 = (bf16[16,3584]{1,0:T(8,128)(2,1)S(1)}, bf16[16,3584]{1,0:T(8,128)(2,1)S(1)}, u32[]{:S(2)}, u32[]{:S(2)}) collective-permute-start(bf16[16,3584]{1,0:T(8,128)(2,1)S(1)} %get-tuple-element.121), channel_id=1, source_target_pairs={{0,8},{1,9},{2,10},{3,11},{4,12},{5,13},{6,14},{7,15},{8,0},{9,1},... | collective-permute-start | bytes 344072 | tf_op jit(solution)/shard_map/ppermute | solution.py:511
  46.9 1.6 %collective-permute-start.14 = (bf16[32,3584]{1,0:T(8,128)(2,1)S(1)}, bf16[32,3584]{1,0:T(8,128)(2,1)S(1)}, u32[]{:S(2)}, u32[]{:S(2)}) collective-permute-start(bf16[32,3584]{1,0:T(8,128)(2,1)S(1)} %total.8.xm_ref), channel_id=1, source_target_pairs={{0,1},{1,0},{2,3},{3,2},{4,5},{5,4},{6,7},{7,6},{8,9},{9,8},{10,11... | collective-permute-start | bytes 688136 | tf_op jit(solution)/shard_map/ppermute | solution.py:468
  50.6 1.6 %collective-permute-start.15 = (bf16[32,3584]{1,0:T(8,128)(2,1)S(1)}, bf16[32,3584]{1,0:T(8,128)(2,1)S(1)}, u32[]{:S(2)}, u32[]{:S(2)}) collective-permute-start(bf16[32,3584]{1,0:T(8,128)(2,1)S(1)} %get-tuple-element.139), channel_id=1, source_target_pairs={{0,1},{1,0},{2,3},{3,2},{4,5},{5,4},{6,7},{7,6},{8,9},{9,8},{10,11... | collective-permute-start | bytes 688136 | tf_op jit(solution)/shard_map/ppermute | solution.py:468
  50.8 6.8 %collective-permute-start.20 = (bf16[32,3584]{1,0:T(8,128)(2,1)S(1)}, bf16[32,3584]{1,0:T(8,128)(2,1)S(1)}, u32[]{:S(2)}, u32[]{:S(2)}) collective-permute-start(bf16[32,3584]{1,0:T(8,128)(2,1)S(1)} %get-tuple-element.143), channel_id=1, source_target_pairs={{0,1},{1,0},{2,3},{3,2},{4,8},{5,9},{6,10},{7,11},{8,4},{9,5},{10,... | collective-permute-start | bytes 688136 | tf_op jit(solution)/shard_map/ppermute | solution.py:511
  52.6 8.9 %collective-permute-start.18 = (bf16[16,3584]{1,0:T(8,128)(2,1)S(1)}, bf16[16,3584]{1,0:T(8,128)(2,1)S(1)}, u32[]{:S(2)}, u32[]{:S(2)}) collective-permute-start(bf16[16,3584]{1,0:T(8,128)(2,1)S(1)} %get-tuple-element.141), channel_id=1, source_target_pairs={{0,6},{1,7},{2,4},{3,5},{4,2},{5,3},{6,0},{7,1},{8,14},{9,15},{10,... | collective-permute-start | bytes 344072 | tf_op jit(solution)/shard_map/ppermute | solution.py:511
  55.1 8.8 %collective-permute-start.16 = (bf16[16,3584]{1,0:T(8,128)(2,1)S(1)}, bf16[16,3584]{1,0:T(8,128)(2,1)S(1)}, u32[]{:S(2)}, u32[]{:S(2)}) collective-permute-start(bf16[16,3584]{1,0:T(8,128)(2,1)S(1)} %get-tuple-element.141), channel_id=1, source_target_pairs={{0,4},{1,5},{2,6},{3,7},{4,0},{5,1},{6,2},{7,3},{8,12},{9,13},{10,... | collective-permute-start | bytes 344072 | tf_op jit(solution)/shard_map/ppermute | solution.py:511
  55.4 8.4 %collective-permute-start.19 = (bf16[16,3584]{1,0:T(8,128)(2,1)S(1)}, bf16[16,3584]{1,0:T(8,128)(2,1)S(1)}, u32[]{:S(2)}, u32[]{:S(2)}) collective-permute-start(bf16[16,3584]{1,0:T(8,128)(2,1)S(1)} %get-tuple-element.142), channel_id=1, source_target_pairs={{0,10},{1,11},{2,8},{3,9},{4,14},{5,15},{6,12},{7,13},{8,2},{9,3},... | collective-permute-start | bytes 344072 | tf_op jit(solution)/shard_map/ppermute | solution.py:511
  57.2 7.4 %collective-permute-start.17 = (bf16[16,3584]{1,0:T(8,128)(2,1)S(1)}, bf16[16,3584]{1,0:T(8,128)(2,1)S(1)}, u32[]{:S(2)}, u32[]{:S(2)}) collective-permute-start(bf16[16,3584]{1,0:T(8,128)(2,1)S(1)} %get-tuple-element.142), channel_id=1, source_target_pairs={{0,8},{1,9},{2,10},{3,11},{4,12},{5,13},{6,14},{7,15},{8,0},{9,1},... | collective-permute-start | bytes 344072 | tf_op jit(solution)/shard_map/ppermute | solution.py:511
  64.6 1.6 %collective-permute-start.21 = (bf16[32,3584]{1,0:T(8,128)(2,1)S(1)}, bf16[32,3584]{1,0:T(8,128)(2,1)S(1)}, u32[]{:S(2)}, u32[]{:S(2)}) collective-permute-start(bf16[32,3584]{1,0:T(8,128)(2,1)S(1)} %total.9.um_ref.base_ref), channel_id=1, source_target_pairs={{0,1},{1,0},{2,3},{3,2},{4,5},{5,4},{6,7},{7,6},{8,9},{9,8},{10,11... | collective-permute-start | bytes 688136 | tf_op jit(solution)/shard_map/ppermute | solution.py:468
  68.3 1.6 %collective-permute-start.22 = (bf16[32,3584]{1,0:T(8,128)(2,1)S(1)}, bf16[32,3584]{1,0:T(8,128)(2,1)S(1)}, u32[]{:S(2)}, u32[]{:S(2)}) collective-permute-start(bf16[32,3584]{1,0:T(8,128)(2,1)S(1)} %get-tuple-element.151), channel_id=1, source_target_pairs={{0,1},{1,0},{2,3},{3,2},{4,5},{5,4},{6,7},{7,6},{8,9},{9,8},{10,11... | collective-permute-start | bytes 688136 | tf_op jit(solution)/shard_map/ppermute | solution.py:468
  68.5 9.6 %collective-permute-start.26 = (bf16[64,3584]{1,0:T(8,128)(2,1)S(1)}, bf16[64,3584]{1,0:T(8,128)(2,1)S(1)}, u32[]{:S(2)}, u32[]{:S(2)}) collective-permute-start(bf16[64,3584]{1,0:T(8,128)(2,1)S(1)} %stack.114), channel_id=1, source_target_pairs={{0,1},{1,0},{2,3},{3,2},{4,20},{5,21},{6,22},{7,23},{8,24},{9,25},... | collective-permute-start | bytes 1376264 | tf_op jit(solution)/shard_map/ppermute | solution.py:511
  70.2 7.7 %collective-permute-start.23 = (bf16[32,3584]{1,0:T(8,128)(2,1)S(1)}, bf16[32,3584]{1,0:T(8,128)(2,1)S(1)}, u32[]{:S(2)}, u32[]{:S(2)}) collective-permute-start(bf16[32,3584]{1,0:T(8,128)(2,1)S(1)} %hold.10.refs_0_), channel_id=1, source_target_pairs={{0,2},{1,3},{2,0},{3,1},{4,6},{5,7},{6,4},{7,5},{8,10},{9,11},{10,... | collective-permute-start | bytes 688136 | tf_op jit(solution)/shard_map/ppermute | solution.py:471
  71.6 16.8 %collective-permute-start.25 = (bf16[32,3584]{1,0:T(8,128)(2,1)S(1)}, bf16[32,3584]{1,0:T(8,128)(2,1)S(1)}, u32[]{:S(2)}, u32[]{:S(2)}) collective-permute-start(bf16[32,3584]{1,0:T(8,128)(2,1)S(1)} %get-tuple-element.154.refs_0_), channel_id=1, source_target_pairs={{0,12},{1,13},{2,14},{3,15},{4,8},{5,9},{6,10},{7,11},{8,4},{9,5},... | collective-permute-start | bytes 688136 | tf_op jit(solution)/shard_map/ppermute | solution.py:511
  78.0 10.4 %collective-permute-start.24 = (bf16[32,3584]{1,0:T(8,128)(2,1)S(1)}, bf16[32,3584]{1,0:T(8,128)(2,1)S(1)}, u32[]{:S(2)}, u32[]{:S(2)}) collective-permute-start(bf16[32,3584]{1,0:T(8,128)(2,1)S(1)} %total.10.um_ref.base_ref), channel_id=1, source_target_pairs={{0,1},{1,0},{2,3},{3,2},{4,5},{5,4},{6,7},{7,6},{8,9},{9,8},{10,11... | collective-permute-start | bytes 688136 | tf_op jit(solution)/shard_map/ppermute | solution.py:468
  88.4 4.1 %collective-permute-start.29 = (bf16[64,3584]{1,0:T(8,128)(2,1)S(1)}, bf16[64,3584]{1,0:T(8,128)(2,1)S(1)}, u32[]{:S(2)}, u32[]{:S(2)}) collective-permute-start(bf16[64,3584]{1,0:T(8,128)(2,1)S(1)} %collective-permute-done.26.p1), channel_id=1, source_target_pairs={{0,1},{1,0},{2,3},{3,2},{4,5},{5,4},{6,7},{7,6},{8,9},{9,8},{10,11... | collective-permute-start | bytes 1376264 | tf_op jit(solution)/shard_map/ppermute | solution.py:468
  90.4 1.7 %collective-permute-start.27 = (bf16[32,3584]{1,0:T(8,128)(2,1)S(1)}, bf16[32,3584]{1,0:T(8,128)(2,1)S(1)}, u32[]{:S(2)}, u32[]{:S(2)}) collective-permute-start(bf16[32,3584]{1,0:T(8,128)(2,1)S(1)} %get-tuple-element.161), channel_id=1, source_target_pairs={{0,1},{1,0},{2,3},{3,2},{4,5},{5,4},{6,7},{7,6},{8,9},{9,8},{10,11... | collective-permute-start | bytes 688136 | tf_op jit(solution)/shard_map/ppermute | solution.py:468
  91.0 1.5 %collective-permute-start.28 = (bf16[32,3584]{1,0:T(8,128)(2,1)S(1)}, bf16[32,3584]{1,0:T(8,128)(2,1)S(1)}, u32[]{:S(2)}, u32[]{:S(2)}) collective-permute-start(bf16[32,3584]{1,0:T(8,128)(2,1)S(1)} %collective-permute-done.20.refs_1_.p0), channel_id=1, source_target_pairs={{0,1},{1,0},{2,3},{3,2},{4,5},{5,4},{6,7},{7,6},{8,9},{9,8},{10,11... | collective-permute-start | bytes 688136 | tf_op jit(solution)/shard_map/ppermute | solution.py:468
  91.1 9.4 %collective-permute-start.35 = (bf16[64,3584]{1,0:T(8,128)(2,1)S(1)}, bf16[64,3584]{1,0:T(8,128)(2,1)S(1)}, u32[]{:S(2)}, u32[]{:S(2)}) collective-permute-start(bf16[64,3584]{1,0:T(8,128)(2,1)S(1)} %stack.115), channel_id=1, source_target_pairs={{0,1},{1,0},{2,3},{3,2},{4,5},{5,4},{6,7},{7,6},{8,24},{9,25},{10,... | collective-permute-start | bytes 1376264 | tf_op jit(solution)/shard_map/ppermute | solution.py:511
  92.5 7.9 %collective-permute-start.30 = (bf16[32,3584]{1,0:T(8,128)(2,1)S(1)}, bf16[32,3584]{1,0:T(8,128)(2,1)S(1)}, u32[]{:S(2)}, u32[]{:S(2)}) collective-permute-start(bf16[32,3584]{1,0:T(8,128)(2,1)S(1)} %hold.11.refs_0_), channel_id=1, source_target_pairs={{0,2},{1,3},{2,0},{3,1},{4,6},{5,7},{6,4},{7,5},{8,10},{9,11},{10,... | collective-permute-start | bytes 688136 | tf_op jit(solution)/shard_map/ppermute | solution.py:471
  100.5 6.1 %collective-permute-start.37 = (bf16[64,3584]{1,0:T(8,128)(2,1)S(1)}, bf16[64,3584]{1,0:T(8,128)(2,1)S(1)}, u32[]{:S(2)}, u32[]{:S(2)}) collective-permute-start(bf16[64,3584]{1,0:T(8,128)(2,1)S(1)} %collective-permute-done.35.q1.refs_7_), channel_id=1, source_target_pairs={{0,1},{1,0},{2,3},{3,2},{4,5},{5,4},{6,7},{7,6},{8,9},{9,8},{10,11... | collective-permute-start | bytes 1376264 | tf_op jit(solution)/shard_map/ppermute | solution.py:468
  100.6 4.8 %collective-permute-start.36 = (bf16[32,3584]{1,0:T(8,128)(2,1)S(1)}, bf16[32,3584]{1,0:T(8,128)(2,1)S(1)}, u32[]{:S(2)}, u32[]{:S(2)}) collective-permute-start(bf16[32,3584]{1,0:T(8,128)(2,1)S(1)} %collective-permute-done.25.refs_1_.q0.refs_6_), channel_id=1, source_target_pairs={{0,1},{1,0},{2,3},{3,2},{4,5},{5,4},{6,7},{7,6},{8,9},{9,8},{10,11... | collective-permute-start | bytes 688136 | tf_op jit(solution)/shard_map/ppermute | solution.py:468
  101.4 11.8 %collective-permute-start.33 = (bf16[32,3584]{1,0:T(8,128)(2,1)S(1)}, bf16[32,3584]{1,0:T(8,128)(2,1)S(1)}, u32[]{:S(2)}, u32[]{:S(2)}) collective-permute-start(bf16[32,3584]{1,0:T(8,128)(2,1)S(1)} %get-tuple-element.165), channel_id=1, source_target_pairs={{20,0},{21,1},{22,2},{23,3},{24,4},{25,5},{26,6},{27,7},{4,16},{5,... | collective-permute-start | bytes 688136 | tf_op jit(solution)/shard_map/ppermute | solution.py:511
  102.7 14.9 %collective-permute-start.31 = (bf16[32,3584]{1,0:T(8,128)(2,1)S(1)}, bf16[32,3584]{1,0:T(8,128)(2,1)S(1)}, u32[]{:S(2)}, u32[]{:S(2)}) collective-permute-start(bf16[32,3584]{1,0:T(8,128)(2,1)S(1)} %get-tuple-element.165), channel_id=1, source_target_pairs={{4,0},{5,1},{6,2},{7,3},{8,4},{9,5},{10,6},{11,7},{20,16},{21,17},... | collective-permute-start | bytes 688136 | tf_op jit(solution)/shard_map/ppermute | solution.py:511
  104.0 21.8 %collective-permute-start.34 = (bf16[32,3584]{1,0:T(8,128)(2,1)S(1)}, bf16[32,3584]{1,0:T(8,128)(2,1)S(1)}, u32[]{:S(2)}, u32[]{:S(2)}) collective-permute-start(bf16[32,3584]{1,0:T(8,128)(2,1)S(1)} %get-tuple-element.166), channel_id=1, source_target_pairs={{24,0},{25,1},{26,2},{27,3},{20,4},{21,5},{22,6},{23,7},{8,16},{9,... | collective-permute-start | bytes 688136 | tf_op jit(solution)/shard_map/ppermute | solution.py:511
  105.3 23.6 %collective-permute-start.32 = (bf16[32,3584]{1,0:T(8,128)(2,1)S(1)}, bf16[32,3584]{1,0:T(8,128)(2,1)S(1)}, u32[]{:S(2)}, u32[]{:S(2)}) collective-permute-start(bf16[32,3584]{1,0:T(8,128)(2,1)S(1)} %get-tuple-element.166), channel_id=1, source_target_pairs={{8,0},{9,1},{10,2},{11,3},{24,16},{25,17},{26,18},{27,19}} | collective-permute-start | bytes 688136 | tf_op jit(solution)/shard_map/ppermute | solution.py:511
  129.0 2.5 %collective-permute-start.38 = (bf16[128,3584]{1,0:T(8,128)(2,1)S(1)}, bf16[128,3584]{1,0:T(8,128)(2,1)S(1)}, u32[]{:S(2)}, u32[]{:S(2)}) collective-permute-start(bf16[128,3584]{1,0:T(8,128)(2,1)S(1)} %stack.116.refs_0_), channel_id=1, source_target_pairs={{0,1},{1,0},{2,3},{3,2},{4,5},{5,4},{6,7},{7,6},{8,9},{9,8},{10,11... | collective-permute-start | bytes 2752520 | tf_op jit(solution)/shard_map/ppermute | solution.py:468

commit v2 on v1

--- a/solution.py
+++ b/solution.py
@@ -677,11 +677,10 @@
             mine = total([held, swap_chip(held)])
         elif step == middle:
             held, mixed = lax.optimization_barrier((held, kept[2]))
-            up_mine = total([held, swap_chip(held)])
+            crossed, state_second = lax.optimization_barrier((swap_chip(held), state_second))
+            up_mine = total([held, crossed])
             mixed_first = flow(mixed, 0, far)
-            up_other, mixed_first, state_second = lax.optimization_barrier(
-                (swap_core(up_mine), mixed_first, state_second)
-            )
+            up_other, mixed_first = lax.optimization_barrier((swap_core(up_mine), mixed_first))
             middle_arrived = with_other_core([state_first, state_second])
             mixed_second = flow(joined(mixed, mixed_first), 1, far)
         else:
@@ -690,7 +689,6 @@
             if step == sections - 1:
                 (state_first,) = during
                 state_second = flow(joined(same, state_first), 1, middle_class)
-    _, mixed_second = lax.optimization_barrier((mine, mixed_second))
     def last_route(shift, source):
         return lambda copy, end, c: ((copy + shift) % REPL, source, 1, False) if c == 0 and end == 0 else None
 
@@ -701,6 +699,7 @@
         send(payloads[0], last_route(1, 0), flow_route(2, middle_near), whole=False),
         send(payloads[1], last_route(1, 1), flow_route(1, middle_near), whole=False),
     ]
+    straight, mixed_second = lax.optimization_barrier((straight, mixed_second))
     mixed_arrived = with_other_core([mixed_first, mixed_second])
     prepared = call(
         own_first_kernel,
@@ -722,7 +721,6 @@
         8 * features * narrow,
         hbm=(15,),
     )
-    straight, prepared = lax.optimization_barrier((straight, prepared))
     direct = with_other_core([joined(*straight)])
     return call(
         own_last_kernel,

time: 136 us -> 139 us (1.022)
  waiting for transfers between devices: 72.1 us -> 74.7 us
    ppermute x20, waiting for transfers between devices: 40.2 us -> 42.2 us  [send(): lax.ppermute(block, ('pipe', 'tensor'), completed(moves) if whole else mo...]
where the time goes in v2:
time: 139 us; the launch traced here: 138 us
  waiting for transfers between devices  74.7 us (54%)
  Pallas kernels  31.6 us (23%)
  starting transfers between devices  31.4 us (23%)
    ppermute x20, waiting for transfers between devices, send(): lax.ppermute(block, ('pipe', 'tensor'), completed(moves) if whole else mo...  42.2 us
    pallas_call x28, Pallas kernels, call(): pl.pallas_call(kernel, out_shape=outs, in_specs=specs, out_specs=[out_spe...  31.6 us
    ppermute x20, starting transfers between devices, send(): lax.ppermute(block, ('pipe', 'tensor'), completed(moves) if whole else mo...  23.8 us
    ppermute x3, waiting for transfers between devices, swap_chip(): return lax.ppermute(block, 'tensor', chip_swap)  17.2 us
    ppermute x16, waiting for transfers between devices, swap_core(): return lax.ppermute(block, 'tensor', core_swap)  15.2 us
    ppermute x3, starting transfers between devices, swap_chip(): return lax.ppermute(block, 'tensor', chip_swap)  4.24 us
    ppermute x16, starting transfers between devices, swap_core(): return lax.ppermute(block, 'tensor', core_swap)  3.4 us
  transfers between devices with their start and end apart: 39, of which 28 were waited for; matrix products, arithmetic and copies ran while one was open for 0% of the time, Pallas kernels for 10%

profile of v2, /device:TPU:0, one launch (start us, length us, event | category | flops | bytes accessed | tf_op | source)
XLA Modules:
  0.0 138.3 jit_solution(8224984752659341113)
XLA Ops:
  0.1 5.5 %first_layer.1 = (bf16[32,3584]{1,0:T(8,128)(2,1)S(1)}, bf16[32,3584]{1,0:T(8,128)(2,1)S(1)}, f32[64,256]{1,0:T(8,128)S(1)}, f32[64,256]{1,0:T(8,128)S(1)}, bf16...) custom-call(s32[29]{0:T(128)S(1)} %stack.110.flags_ref, ...), custom_call_target="tpu_custom_call" | custom-call | flops 352321536 | bytes 5505024 | tf_op jit(solution)/shard_map/first_layer/pallas_call | solution.py:418
  6.1 1.1 collective-permute-done.recv_ref
  7.4 3.9 %collective-permute-start.3 = (bf16[16,3584]{1,0:T(8,128)(2,1)S(1)}, bf16[16,3584]{1,0:T(8,128)(2,1)S(1)}, u32[]{:S(2)}, u32[]{:S(2)}) collective-permute-start(bf16[16,3584]{1,0:T(8,128)(2,1)S(1)} %get-tuple-element.99), channel_id=1, source_target_pairs={{0,6},{1,7},{2,4},{3,5},{4,2},{5,3},{6,0},{7,1},{8,14},{9,15},{10,... | collective-permute-start | bytes 344072 | tf_op jit(solution)/shard_map/ppermute | solution.py:511
  11.8 1.5 %collective-permute-start.4 = (bf16[16,3584]{1,0:T(8,128)(2,1)S(1)}, bf16[16,3584]{1,0:T(8,128)(2,1)S(1)}, u32[]{:S(2)}, u32[]{:S(2)}) collective-permute-start(bf16[16,3584]{1,0:T(8,128)(2,1)S(1)} %get-tuple-element.100), channel_id=1, source_target_pairs={{0,10},{1,11},{2,8},{3,9},{4,14},{5,15},{6,12},{7,13},{8,2},{9,3},... | collective-permute-start | bytes 344072 | tf_op jit(solution)/shard_map/ppermute | solution.py:511
  13.4 3.4 %load_late.1 = (bf16[3,3584,256]{2,1,0:T(8,128)(2,1)S(1)}, bf16[32,3584]{1,0:T(8,128)(2,1)S(1)}, bf16[32,3584]{1,0:T(8,128)(2,1)S(1)}) custom-call(s32[29]{0:T(128)S(1)} %stack.110.flags_ref, bf16[8,32,3584]{2,1,0:T(8,128)(2,1)} %bitcast.36, bf16[2,3,3584,256]{3,2,1,0:T(8,128)(2,1)} %bitcast.34), custom_call_target="tpu_custom_call" | custom-call | bytes 11010048 | tf_op jit(solution)/shard_map/load_late/pallas_call | solution.py:418
  17.5 1.2 collective-permute-done.4.refs_3_
  19.2 1.5 %collective-permute-done.5.xo_ref = bf16[32,3584]{1,0:T(8,128)(2,1)S(1)} collective-permute-done((bf16[32,3584]{1,0:T(8,128)(2,1)S(1)}, bf16[32,3584]{1,0:T(8,128)(2,1)S(1)}, u32[]{:S(2)}, u32[]{:S(2)}) %collective-permute-start.5) | collective-permute-done | bytes 229408 | tf_op jit(solution)/shard_map/ppermute | solution.py:468
  20.7 1.6 %forward_layer.2 = (bf16[32,3584]{1,0:T(8,128)(2,1)S(1)}, bf16[32,3584]{1,0:T(8,128)(2,1)S(1)}, f32[64,256]{1,0:T(8,128)S(1)}, f32[64,256]{1,0:T(8,128)S(1)}, bf...) custom-call(s32[8,128]{1,0:T(8,128)S(1)} %get-tuple-element.95.flags_ref.marks_ref, ...), custom_call_target="tpu_custom_call" | custom-call | flops 352321536 | bytes 5505024 | tf_op jit(solution)/shard_map/forward_layer/pallas_call | solution.py:418
  22.5 1.3 collective-permute-done.6.recv_ref
  24.0 1.4 %collective-permute-start.7 = (bf16[32,3584]{1,0:T(8,128)(2,1)S(1)}, bf16[32,3584]{1,0:T(8,128)(2,1)S(1)}, u32[]{:S(2)}, u32[]{:S(2)}) collective-permute-start(bf16[32,3584]{1,0:T(8,128)(2,1)S(1)} %hold.7.refs_0_), channel_id=1, source_target_pairs={{0,2},{1,3},{2,0},{3,1},{4,6},{5,7},{6,4},{7,5},{8,10},{9,11},{10,... | collective-permute-start | bytes 688136 | tf_op jit(solution)/shard_map/ppermute | solution.py:471
  25.5 6.3 %collective-permute-done.7.refs_1_ = bf16[32,3584]{1,0:T(8,128)(2,1)S(1)} collective-permute-done((bf16[32,3584]{1,0:T(8,128)(2,1)S(1)}, bf16[32,3584]{1,0:T(8,128)(2,1)S(1)}, u32[]{:S(2)}, u32[]{:S(2)}) %collective-permute-start.7) | collective-permute-done | bytes 229408 | tf_op jit(solution)/shard_map/ppermute | solution.py:471
  31.9 1.5 %collective-permute-done.8.xo_ref = bf16[32,3584]{1,0:T(8,128)(2,1)S(1)} collective-permute-done((bf16[32,3584]{1,0:T(8,128)(2,1)S(1)}, bf16[32,3584]{1,0:T(8,128)(2,1)S(1)}, u32[]{:S(2)}, u32[]{:S(2)}) %collective-permute-start.8) | collective-permute-done | bytes 229408 | tf_op jit(solution)/shard_map/ppermute | solution.py:468
  33.4 1.5 %forward_layer.3 = (bf16[32,3584]{1,0:T(8,128)(2,1)S(1)}, bf16[32,3584]{1,0:T(8,128)(2,1)S(1)}, f32[64,256]{1,0:T(8,128)S(1)}, f32[64,256]{1,0:T(8,128)S(1)}, bf...) custom-call(s32[8,128]{1,0:T(8,128)S(1)} %get-tuple-element.95.flags_ref.marks_ref, ...), custom_call_target="tpu_custom_call" | custom-call | flops 352321536 | bytes 5505024 | tf_op jit(solution)/shard_map/forward_layer/pallas_call | solution.py:418
  35.1 1.4 collective-permute-done.9.recv_ref
  36.6 2.4 %collective-permute-start.12 = (bf16[16,3584]{1,0:T(8,128)(2,1)S(1)}, bf16[16,3584]{1,0:T(8,128)(2,1)S(1)}, u32[]{:S(2)}, u32[]{:S(2)}) collective-permute-start(bf16[16,3584]{1,0:T(8,128)(2,1)S(1)} %get-tuple-element.117), channel_id=1, source_target_pairs={{0,6},{1,7},{2,4},{3,5},{4,2},{5,3},{6,0},{7,1},{8,14},{9,15},{10,... | collective-permute-start | bytes 344072 | tf_op jit(solution)/shard_map/ppermute | solution.py:511
  39.5 1.6 %collective-permute-start.13 = (bf16[16,3584]{1,0:T(8,128)(2,1)S(1)}, bf16[16,3584]{1,0:T(8,128)(2,1)S(1)}, u32[]{:S(2)}, u32[]{:S(2)}) collective-permute-start(bf16[16,3584]{1,0:T(8,128)(2,1)S(1)} %get-tuple-element.118), channel_id=1, source_target_pairs={{0,10},{1,11},{2,8},{3,9},{4,14},{5,15},{6,12},{7,13},{8,2},{9,3},... | collective-permute-start | bytes 344072 | tf_op jit(solution)/shard_map/ppermute | solution.py:511
  41.6 2.9 %load_rows.1 = (bf16[8,32,3584]{2,1,0:T(8,128)(2,1)S(1)}, bf16[8,32,3584]{2,1,0:T(8,128)(2,1)S(1)}) custom-call(s32[29]{0:T(128)S(1)} %stack.110.flags_ref, bf16[8,32,3584]{2,1,0:T(8,128)(2,1)} %bitcast.39, bf16[8,32,3584]{2,1,0:T(8,128)(2,1)} %bitcast.37), custom_call_target="tpu_custom_call" | custom-call | bytes 5505024 | tf_op jit(solution)/shard_map/load_rows/pallas_call | solution.py:418
  45.1 1.2 collective-permute-done.13.refs_3_
  47.1 1.3 collective-permute-done.14.xo_ref
  48.4 2.2 %turn_layer.1 = (bf16[32,3584]{1,0:T(8,128)(2,1)S(1)}, bf16[32,3584]{1,0:T(8,128)(2,1)S(1)}, bf16[32,3584]{1,0:T(8,128)(2,1)S(1)}, bf16[32,3584]{1,0:T(8,128)(2,1)S(1)}) custom-call(s32[8,128]{1,0:T(8,128)S(1)} %get-tuple-element.95.flags_ref.marks_ref, f32[64,256]{1,0:T(8,128)S(1)} %cotangent.1.d_ref, bf16[32,3584]{1,0:T(8,128)(2,1)S(1)} %total.8.xm_ref, ...), custom_call_target="tpu_custom_call" | custom-call | flops 352321536 | bytes 5505024 | tf_op jit(solution)/shard_map/turn_layer/pallas_call | solution.py:418
  51.2 1.0 collective-permute-done.15.recv_ref
  52.6 2.5 %collective-permute-start.18 = (bf16[16,3584]{1,0:T(8,128)(2,1)S(1)}, bf16[16,3584]{1,0:T(8,128)(2,1)S(1)}, u32[]{:S(2)}, u32[]{:S(2)}) collective-permute-start(bf16[16,3584]{1,0:T(8,128)(2,1)S(1)} %get-tuple-element.138), channel_id=1, source_target_pairs={{0,6},{1,7},{2,4},{3,5},{4,2},{5,3},{6,0},{7,1},{8,14},{9,15},{10,... | collective-permute-start | bytes 344072 | tf_op jit(solution)/shard_map/ppermute | solution.py:511
  55.4 1.7 %collective-permute-start.19 = (bf16[16,3584]{1,0:T(8,128)(2,1)S(1)}, bf16[16,3584]{1,0:T(8,128)(2,1)S(1)}, u32[]{:S(2)}, u32[]{:S(2)}) collective-permute-start(bf16[16,3584]{1,0:T(8,128)(2,1)S(1)} %get-tuple-element.139), channel_id=1, source_target_pairs={{0,10},{1,11},{2,8},{3,9},{4,14},{5,15},{6,12},{7,13},{8,2},{9,3},... | collective-permute-start | bytes 344072 | tf_op jit(solution)/shard_map/ppermute | solution.py:511
  57.6 3.9 %collective-permute-done.18.refs_2_ = bf16[16,3584]{1,0:T(8,128)(2,1)S(1)} collective-permute-done((bf16[16,3584]{1,0:T(8,128)(2,1)S(1)}, bf16[16,3584]{1,0:T(8,128)(2,1)S(1)}, u32[]{:S(2)}, u32[]{:S(2)}) %collective-permute-start.18) | collective-permute-done | bytes 114720 | tf_op jit(solution)/shard_map/ppermute | solution.py:511
  61.5 2.4 %collective-permute-done.16.refs_0_ = bf16[16,3584]{1,0:T(8,128)(2,1)S(1)} collective-permute-done((bf16[16,3584]{1,0:T(8,128)(2,1)S(1)}, bf16[16,3584]{1,0:T(8,128)(2,1)S(1)}, u32[]{:S(2)}, u32[]{:S(2)}) %collective-permute-start.16) | collective-permute-done | bytes 114720 | tf_op jit(solution)/shard_map/ppermute | solution.py:511
  63.9 0.7 collective-permute-done.17.refs_1_
  64.7 1.5 %collective-permute-done.21.uo_ref = bf16[32,3584]{1,0:T(8,128)(2,1)S(1)} collective-permute-done((bf16[32,3584]{1,0:T(8,128)(2,1)S(1)}, bf16[32,3584]{1,0:T(8,128)(2,1)S(1)}, u32[]{:S(2)}, u32[]{:S(2)}) %collective-permute-start.21) | collective-permute-done | bytes 229408 | tf_op jit(solution)/shard_map/ppermute | solution.py:468
  66.2 2.1 %backward_layer.2 = (bf16[32,3584]{1,0:T(8,128)(2,1)S(1)}, bf16[32,3584]{1,0:T(8,128)(2,1)S(1)}, bf16[32,3584]{1,0:T(8,128)(2,1)S(1)}, bf16[32,3584]{1,0:T(8,128)(2,1)S(1)}, bf16[32,3584]{1,0:T(8,128)(2,1)S(1)}) custom-call(s32[8,128]{1,0:T(8,128)S(1)} %get-tuple-element.95.flags_ref.marks_ref, bf16[32,3584]{1,0:T(8,128)(2,1)S(1)} %total.9.um_ref.base_ref, ...), custom_call_target="tpu_custom_call" | custom-call | flops 352321536 | bytes 5505024 | tf_op jit(solution)/shard_map/backward_layer/pallas_call | solution.py:418
  68.9 0.9 collective-permute-done.22.recv_ref
  70.2 1.4 %collective-permute-start.23 = (bf16[32,3584]{1,0:T(8,128)(2,1)S(1)}, bf16[32,3584]{1,0:T(8,128)(2,1)S(1)}, u32[]{:S(2)}, u32[]{:S(2)}) collective-permute-start(bf16[32,3584]{1,0:T(8,128)(2,1)S(1)} %hold.10.refs_0_), channel_id=1, source_target_pairs={{0,2},{1,3},{2,0},{3,1},{4,6},{5,7},{6,4},{7,5},{8,10},{9,11},{10,... | collective-permute-start | bytes 688136 | tf_op jit(solution)/shard_map/ppermute | solution.py:471
  71.6 1.6 %collective-permute-start.26 = (bf16[32,3584]{1,0:T(8,128)(2,1)S(1)}, bf16[32,3584]{1,0:T(8,128)(2,1)S(1)}, u32[]{:S(2)}, u32[]{:S(2)}) collective-permute-start(bf16[32,3584]{1,0:T(8,128)(2,1)S(1)} %get-tuple-element.154.refs_0_), channel_id=1, source_target_pairs={{0,12},{1,13},{2,14},{3,15},{4,8},{5,9},{6,10},{7,11},{8,4},{9,5},... | collective-permute-start | bytes 688136 | tf_op jit(solution)/shard_map/ppermute | solution.py:511
  73.2 4.8 %collective-permute-done.23.refs_1_ = bf16[32,3584]{1,0:T(8,128)(2,1)S(1)} collective-permute-done((bf16[32,3584]{1,0:T(8,128)(2,1)S(1)}, bf16[32,3584]{1,0:T(8,128)(2,1)S(1)}, u32[]{:S(2)}, u32[]{:S(2)}) %collective-permute-start.23) | collective-permute-done | bytes 229408 | tf_op jit(solution)/shard_map/ppermute | solution.py:471
  78.6 9.8 %collective-permute-done.26.refs_1_.q0.refs_6_ = bf16[32,3584]{1,0:T(8,128)(2,1)S(1)} collective-permute-done((bf16[32,3584]{1,0:T(8,128)(2,1)S(1)}, bf16[32,3584]{1,0:T(8,128)(2,1)S(1)}, u32[]{:S(2)}, u32[]{:S(2)}) %collective-permute-start.26) | collective-permute-done | bytes 229408 | tf_op jit(solution)/shard_map/ppermute | solution.py:511
  88.4 1.9 %backward_layer.3 = (bf16[32,3584]{1,0:T(8,128)(2,1)S(1)}, bf16[32,3584]{1,0:T(8,128)(2,1)S(1)}, bf16[32,3584]{1,0:T(8,128)(2,1)S(1)}, bf16[32,3584]{1,0:T(8,128)(2,1)S(1)}) custom-call(s32[8,128]{1,0:T(8,128)S(1)} %get-tuple-element.95.flags_ref.marks_ref, bf16[32,3584]{1,0:T(8,128)(2,1)S(1)} %total.10.um_ref.base_ref, ...), custom_call_target="tpu_custom_call" | custom-call | flops 352321536 | bytes 5505024 | tf_op jit(solution)/shard_map/backward_layer/pallas_call | solution.py:418
  90.9 1.0 collective-permute-done.27.recv_ref
  92.3 1.4 %collective-permute-start.30 = (bf16[32,3584]{1,0:T(8,128)(2,1)S(1)}, bf16[32,3584]{1,0:T(8,128)(2,1)S(1)}, u32[]{:S(2)}, u32[]{:S(2)}) collective-permute-start(bf16[32,3584]{1,0:T(8,128)(2,1)S(1)} %hold.11.refs_0_), channel_id=1, source_target_pairs={{0,2},{1,3},{2,0},{3,1},{4,6},{5,7},{6,4},{7,5},{8,10},{9,11},{10,... | collective-permute-start | bytes 688136 | tf_op jit(solution)/shard_map/ppermute | solution.py:471
  93.8 6.2 %collective-permute-done.30.refs_1_ = bf16[32,3584]{1,0:T(8,128)(2,1)S(1)} collective-permute-done((bf16[32,3584]{1,0:T(8,128)(2,1)S(1)}, bf16[32,3584]{1,0:T(8,128)(2,1)S(1)}, u32[]{:S(2)}, u32[]{:S(2)}) %collective-permute-start.30) | collective-permute-done | bytes 229408 | tf_op jit(solution)/shard_map/ppermute | solution.py:471
  100.3 1.5 %collective-permute-start.33 = (bf16[32,3584]{1,0:T(8,128)(2,1)S(1)}, bf16[32,3584]{1,0:T(8,128)(2,1)S(1)}, u32[]{:S(2)}, u32[]{:S(2)}) collective-permute-start(bf16[32,3584]{1,0:T(8,128)(2,1)S(1)} %get-tuple-element.163), channel_id=1, source_target_pairs={{20,0},{21,1},{22,2},{23,3},{24,4},{25,5},{26,6},{27,7},{4,16},{5,... | collective-permute-start | bytes 688136 | tf_op jit(solution)/shard_map/ppermute | solution.py:511
  101.8 1.3 collective-permute-start.31
  103.1 1.3 collective-permute-start.34
  104.4 1.3 collective-permute-start.32
  105.7 7.3 %collective-permute-done.33.refs_2_ = bf16[32,3584]{1,0:T(8,128)(2,1)S(1)} collective-permute-done((bf16[32,3584]{1,0:T(8,128)(2,1)S(1)}, bf16[32,3584]{1,0:T(8,128)(2,1)S(1)}, u32[]{:S(2)}, u32[]{:S(2)}) %collective-permute-start.33) | collective-permute-done | bytes 229408 | tf_op jit(solution)/shard_map/ppermute | solution.py:511
  113.0 3.2 %collective-permute-done.31.refs_0_ = bf16[32,3584]{1,0:T(8,128)(2,1)S(1)} collective-permute-done((bf16[32,3584]{1,0:T(8,128)(2,1)S(1)}, bf16[32,3584]{1,0:T(8,128)(2,1)S(1)}, u32[]{:S(2)}, u32[]{:S(2)}) %collective-permute-start.31) | collective-permute-done | bytes 229408 | tf_op jit(solution)/shard_map/ppermute | solution.py:511
  116.2 7.8 %collective-permute-done.34.refs_3_ = bf16[32,3584]{1,0:T(8,128)(2,1)S(1)} collective-permute-done((bf16[32,3584]{1,0:T(8,128)(2,1)S(1)}, bf16[32,3584]{1,0:T(8,128)(2,1)S(1)}, u32[]{:S(2)}, u32[]{:S(2)}) %collective-permute-start.34) | collective-permute-done | bytes 229408 | tf_op jit(solution)/shard_map/ppermute | solution.py:511
  124.0 2.9 %collective-permute-done.32.refs_1_ = bf16[32,3584]{1,0:T(8,128)(2,1)S(1)} collective-permute-done((bf16[32,3584]{1,0:T(8,128)(2,1)S(1)}, bf16[32,3584]{1,0:T(8,128)(2,1)S(1)}, u32[]{:S(2)}, u32[]{:S(2)}) %collective-permute-start.32) | collective-permute-done | bytes 229408 | tf_op jit(solution)/shard_map/ppermute | solution.py:511
  127.7 2.9 %collective-permute-done.37.q2.refs_8_ = bf16[32,3584]{1,0:T(8,128)(2,1)S(1)} collective-permute-done((bf16[32,3584]{1,0:T(8,128)(2,1)S(1)}, bf16[32,3584]{1,0:T(8,128)(2,1)S(1)}, u32[]{:S(2)}, u32[]{:S(2)}) %collective-permute-start.37) | collective-permute-done | bytes 229408 | tf_op jit(solution)/shard_map/ppermute | solution.py:468
  130.5 3.5 %own_first.1 = (bf16[3584,256]{1,0:T(8,128)(2,1)S(1)}, f32[256,256]{1,0:T(8,128)S(1)}, f32[256,256]{1,0:T(8,128)S(1)}, bf16[256,256]{1,0:T(8,128)(2,1)S(1)}) custom-call(s32[29]{0:T(128)S(1)} %stack.110.flags_ref, bf16[8,32,3584]{2,1,0:T(8,128)(2,1)S(1)} %get-tuple-element.174.xs_ref, bf16[32,3584]{1,0:T(8,128)(2,1)S(1)} %get-tuple-element.129.early_ref.refs_0_.em_ref, ...), custom_call_target="tpu_custom_call" | custom-call | flops 939524096 | bytes 7340032 | tf_op jit(solution)/shard_map/own_first/pallas_call | solution.py:418
  134.0 4.1 %own_last.1 = bf16[1,3,3584,256]{3,2,1,0:T(8,128)(2,1)} custom-call(s32[29]{0:T(128)S(1)} %stack.110.flags_ref, bf16[8,32,3584]{2,1,0:T(8,128)(2,1)S(1)} %get-tuple-element.123.us_ref, bf16[128,3584]{1,0:T(8,128)(2,1)S(1)} %stack.116.refs_0_, bf16[128,3584]{1,0:T(8,128)(2,1)S(1)} %collective-permute-done.36.refs_1_, ...), custom_call_target="tpu_custom_call" | custom-call | flops 1879048192 | bytes 7340032 | tf_op jit(solution)/shard_map/own_last/pallas_call | solution.py:418
  (61 shorter events, 11.4 us)
Async XLA Ops:
  5.6 1.6 %collective-permute-start = (bf16[32,3584]{1,0:T(8,128)(2,1)S(1)}, bf16[32,3584]{1,0:T(8,128)(2,1)S(1)}, u32[]{:S(2)}, u32[]{:S(2)}) collective-permute-start(bf16[32,3584]{1,0:T(8,128)(2,1)S(1)} %get-tuple-element.97), channel_id=1, source_target_pairs={{0,1},{1,0},{2,3},{3,2},{4,5},{5,4},{6,7},{7,6},{8,9},{9,8},{10,11... | collective-permute-start | bytes 688136 | tf_op jit(solution)/shard_map/ppermute | solution.py:468
  7.4 9.4 %collective-permute-start.3 = (bf16[16,3584]{1,0:T(8,128)(2,1)S(1)}, bf16[16,3584]{1,0:T(8,128)(2,1)S(1)}, u32[]{:S(2)}, u32[]{:S(2)}) collective-permute-start(bf16[16,3584]{1,0:T(8,128)(2,1)S(1)} %get-tuple-element.99), channel_id=1, source_target_pairs={{0,6},{1,7},{2,4},{3,5},{4,2},{5,3},{6,0},{7,1},{8,14},{9,15},{10,... | collective-permute-start | bytes 344072 | tf_op jit(solution)/shard_map/ppermute | solution.py:511
  11.3 6.2 %collective-permute-start.1 = (bf16[16,3584]{1,0:T(8,128)(2,1)S(1)}, bf16[16,3584]{1,0:T(8,128)(2,1)S(1)}, u32[]{:S(2)}, u32[]{:S(2)}) collective-permute-start(bf16[16,3584]{1,0:T(8,128)(2,1)S(1)} %get-tuple-element.99), channel_id=1, source_target_pairs={{0,4},{1,5},{2,6},{3,7},{4,0},{5,1},{6,2},{7,3},{8,12},{9,13},{10,... | collective-permute-start | bytes 344072 | tf_op jit(solution)/shard_map/ppermute | solution.py:511
  11.8 6.8 %collective-permute-start.4 = (bf16[16,3584]{1,0:T(8,128)(2,1)S(1)}, bf16[16,3584]{1,0:T(8,128)(2,1)S(1)}, u32[]{:S(2)}, u32[]{:S(2)}) collective-permute-start(bf16[16,3584]{1,0:T(8,128)(2,1)S(1)} %get-tuple-element.100), channel_id=1, source_target_pairs={{0,10},{1,11},{2,8},{3,9},{4,14},{5,15},{6,12},{7,13},{8,2},{9,3},... | collective-permute-start | bytes 344072 | tf_op jit(solution)/shard_map/ppermute | solution.py:511
  13.4 5.7 %collective-permute-start.2 = (bf16[16,3584]{1,0:T(8,128)(2,1)S(1)}, bf16[16,3584]{1,0:T(8,128)(2,1)S(1)}, u32[]{:S(2)}, u32[]{:S(2)}) collective-permute-start(bf16[16,3584]{1,0:T(8,128)(2,1)S(1)} %get-tuple-element.100), channel_id=1, source_target_pairs={{0,8},{1,9},{2,10},{3,11},{4,12},{5,13},{6,14},{7,15},{8,0},{9,1},... | collective-permute-start | bytes 344072 | tf_op jit(solution)/shard_map/ppermute | solution.py:511
  13.4 7.3 %copy-start = (f32[1,2,3584]{2,1,0:T(2,128)S(1)}, f32[1,2,3584]{2,1,0:T(2,128)}, u32[]{:S(2)}) copy-start(f32[1,2,3584]{2,1,0:T(2,128)} %param.7) | copy-start | bytes 86020
  19.2 1.6 %collective-permute-start.5 = (bf16[32,3584]{1,0:T(8,128)(2,1)S(1)}, bf16[32,3584]{1,0:T(8,128)(2,1)S(1)}, u32[]{:S(2)}, u32[]{:S(2)}) collective-permute-start(bf16[32,3584]{1,0:T(8,128)(2,1)S(1)} %total.6.xm_ref.base_ref), channel_id=1, source_target_pairs={{0,1},{1,0},{2,3},{3,2},{4,5},{5,4},{6,7},{7,6},{8,9},{9,8},{10,11... | collective-permute-start | bytes 688136 | tf_op jit(solution)/shard_map/ppermute | solution.py:468
  22.3 1.6 %collective-permute-start.6 = (bf16[32,3584]{1,0:T(8,128)(2,1)S(1)}, bf16[32,3584]{1,0:T(8,128)(2,1)S(1)}, u32[]{:S(2)}, u32[]{:S(2)}) collective-permute-start(bf16[32,3584]{1,0:T(8,128)(2,1)S(1)} %get-tuple-element.113), channel_id=1, source_target_pairs={{0,1},{1,0},{2,3},{3,2},{4,5},{5,4},{6,7},{7,6},{8,9},{9,8},{10,11... | collective-permute-start | bytes 688136 | tf_op jit(solution)/shard_map/ppermute | solution.py:468
  24.0 7.7 %collective-permute-start.7 = (bf16[32,3584]{1,0:T(8,128)(2,1)S(1)}, bf16[32,3584]{1,0:T(8,128)(2,1)S(1)}, u32[]{:S(2)}, u32[]{:S(2)}) collective-permute-start(bf16[32,3584]{1,0:T(8,128)(2,1)S(1)} %hold.7.refs_0_), channel_id=1, source_target_pairs={{0,2},{1,3},{2,0},{3,1},{4,6},{5,7},{6,4},{7,5},{8,10},{9,11},{10,... | collective-permute-start | bytes 688136 | tf_op jit(solution)/shard_map/ppermute | solution.py:471
  31.8 1.6 %collective-permute-start.8 = (bf16[32,3584]{1,0:T(8,128)(2,1)S(1)}, bf16[32,3584]{1,0:T(8,128)(2,1)S(1)}, u32[]{:S(2)}, u32[]{:S(2)}) collective-permute-start(bf16[32,3584]{1,0:T(8,128)(2,1)S(1)} %total.7.xm_ref.base_ref), channel_id=1, source_target_pairs={{0,1},{1,0},{2,3},{3,2},{4,5},{5,4},{6,7},{7,6},{8,9},{9,8},{10,11... | collective-permute-start | bytes 688136 | tf_op jit(solution)/shard_map/ppermute | solution.py:468
  34.9 1.6 %collective-permute-start.9 = (bf16[32,3584]{1,0:T(8,128)(2,1)S(1)}, bf16[32,3584]{1,0:T(8,128)(2,1)S(1)}, u32[]{:S(2)}, u32[]{:S(2)}) collective-permute-start(bf16[32,3584]{1,0:T(8,128)(2,1)S(1)} %get-tuple-element.116), channel_id=1, source_target_pairs={{0,1},{1,0},{2,3},{3,2},{4,5},{5,4},{6,7},{7,6},{8,9},{9,8},{10,11... | collective-permute-start | bytes 688136 | tf_op jit(solution)/shard_map/ppermute | solution.py:468
  36.6 8.3 %collective-permute-start.12 = (bf16[16,3584]{1,0:T(8,128)(2,1)S(1)}, bf16[16,3584]{1,0:T(8,128)(2,1)S(1)}, u32[]{:S(2)}, u32[]{:S(2)}) collective-permute-start(bf16[16,3584]{1,0:T(8,128)(2,1)S(1)} %get-tuple-element.117), channel_id=1, source_target_pairs={{0,6},{1,7},{2,4},{3,5},{4,2},{5,3},{6,0},{7,1},{8,14},{9,15},{10,... | collective-permute-start | bytes 344072 | tf_op jit(solution)/shard_map/ppermute | solution.py:511
  39.0 6.2 %collective-permute-start.10 = (bf16[16,3584]{1,0:T(8,128)(2,1)S(1)}, bf16[16,3584]{1,0:T(8,128)(2,1)S(1)}, u32[]{:S(2)}, u32[]{:S(2)}) collective-permute-start(bf16[16,3584]{1,0:T(8,128)(2,1)S(1)} %get-tuple-element.117), channel_id=1, source_target_pairs={{0,4},{1,5},{2,6},{3,7},{4,0},{5,1},{6,2},{7,3},{8,12},{9,13},{10,... | collective-permute-start | bytes 344072 | tf_op jit(solution)/shard_map/ppermute | solution.py:511
  39.5 6.8 %collective-permute-start.13 = (bf16[16,3584]{1,0:T(8,128)(2,1)S(1)}, bf16[16,3584]{1,0:T(8,128)(2,1)S(1)}, u32[]{:S(2)}, u32[]{:S(2)}) collective-permute-start(bf16[16,3584]{1,0:T(8,128)(2,1)S(1)} %get-tuple-element.118), channel_id=1, source_target_pairs={{0,10},{1,11},{2,8},{3,9},{4,14},{5,15},{6,12},{7,13},{8,2},{9,3},... | collective-permute-start | bytes 344072 | tf_op jit(solution)/shard_map/ppermute | solution.py:511
  41.1 5.7 %collective-permute-start.11 = (bf16[16,3584]{1,0:T(8,128)(2,1)S(1)}, bf16[16,3584]{1,0:T(8,128)(2,1)S(1)}, u32[]{:S(2)}, u32[]{:S(2)}) collective-permute-start(bf16[16,3584]{1,0:T(8,128)(2,1)S(1)} %get-tuple-element.118), channel_id=1, source_target_pairs={{0,8},{1,9},{2,10},{3,11},{4,12},{5,13},{6,14},{7,15},{8,0},{9,1},... | collective-permute-start | bytes 344072 | tf_op jit(solution)/shard_map/ppermute | solution.py:511
  46.9 1.6 %collective-permute-start.14 = (bf16[32,3584]{1,0:T(8,128)(2,1)S(1)}, bf16[32,3584]{1,0:T(8,128)(2,1)S(1)}, u32[]{:S(2)}, u32[]{:S(2)}) collective-permute-start(bf16[32,3584]{1,0:T(8,128)(2,1)S(1)} %total.8.xm_ref), channel_id=1, source_target_pairs={{0,1},{1,0},{2,3},{3,2},{4,5},{5,4},{6,7},{7,6},{8,9},{9,8},{10,11... | collective-permute-start | bytes 688136 | tf_op jit(solution)/shard_map/ppermute | solution.py:468
  50.6 1.6 %collective-permute-start.15 = (bf16[32,3584]{1,0:T(8,128)(2,1)S(1)}, bf16[32,3584]{1,0:T(8,128)(2,1)S(1)}, u32[]{:S(2)}, u32[]{:S(2)}) collective-permute-start(bf16[32,3584]{1,0:T(8,128)(2,1)S(1)} %get-tuple-element.136), channel_id=1, source_target_pairs={{0,1},{1,0},{2,3},{3,2},{4,5},{5,4},{6,7},{7,6},{8,9},{9,8},{10,11... | collective-permute-start | bytes 688136 | tf_op jit(solution)/shard_map/ppermute | solution.py:468
  50.8 6.8 %collective-permute-start.20 = (bf16[32,3584]{1,0:T(8,128)(2,1)S(1)}, bf16[32,3584]{1,0:T(8,128)(2,1)S(1)}, u32[]{:S(2)}, u32[]{:S(2)}) collective-permute-start(bf16[32,3584]{1,0:T(8,128)(2,1)S(1)} %get-tuple-element.140), channel_id=1, source_target_pairs={{0,1},{1,0},{2,3},{3,2},{4,8},{5,9},{6,10},{7,11},{8,4},{9,5},{10,... | collective-permute-start | bytes 688136 | tf_op jit(solution)/shard_map/ppermute | solution.py:511
  52.6 8.9 %collective-permute-start.18 = (bf16[16,3584]{1,0:T(8,128)(2,1)S(1)}, bf16[16,3584]{1,0:T(8,128)(2,1)S(1)}, u32[]{:S(2)}, u32[]{:S(2)}) collective-permute-start(bf16[16,3584]{1,0:T(8,128)(2,1)S(1)} %get-tuple-element.138), channel_id=1, source_target_pairs={{0,6},{1,7},{2,4},{3,5},{4,2},{5,3},{6,0},{7,1},{8,14},{9,15},{10,... | collective-permute-start | bytes 344072 | tf_op jit(solution)/shard_map/ppermute | solution.py:511
  55.1 8.8 %collective-permute-start.16 = (bf16[16,3584]{1,0:T(8,128)(2,1)S(1)}, bf16[16,3584]{1,0:T(8,128)(2,1)S(1)}, u32[]{:S(2)}, u32[]{:S(2)}) collective-permute-start(bf16[16,3584]{1,0:T(8,128)(2,1)S(1)} %get-tuple-element.138), channel_id=1, source_target_pairs={{0,4},{1,5},{2,6},{3,7},{4,0},{5,1},{6,2},{7,3},{8,12},{9,13},{10,... | collective-permute-start | bytes 344072 | tf_op jit(solution)/shard_map/ppermute | solution.py:511
  55.4 8.4 %collective-permute-start.19 = (bf16[16,3584]{1,0:T(8,128)(2,1)S(1)}, bf16[16,3584]{1,0:T(8,128)(2,1)S(1)}, u32[]{:S(2)}, u32[]{:S(2)}) collective-permute-start(bf16[16,3584]{1,0:T(8,128)(2,1)S(1)} %get-tuple-element.139), channel_id=1, source_target_pairs={{0,10},{1,11},{2,8},{3,9},{4,14},{5,15},{6,12},{7,13},{8,2},{9,3},... | collective-permute-start | bytes 344072 | tf_op jit(solution)/shard_map/ppermute | solution.py:511
  57.1 7.4 %collective-permute-start.17 = (bf16[16,3584]{1,0:T(8,128)(2,1)S(1)}, bf16[16,3584]{1,0:T(8,128)(2,1)S(1)}, u32[]{:S(2)}, u32[]{:S(2)}) collective-permute-start(bf16[16,3584]{1,0:T(8,128)(2,1)S(1)} %get-tuple-element.139), channel_id=1, source_target_pairs={{0,8},{1,9},{2,10},{3,11},{4,12},{5,13},{6,14},{7,15},{8,0},{9,1},... | collective-permute-start | bytes 344072 | tf_op jit(solution)/shard_map/ppermute | solution.py:511
  64.6 1.6 %collective-permute-start.21 = (bf16[32,3584]{1,0:T(8,128)(2,1)S(1)}, bf16[32,3584]{1,0:T(8,128)(2,1)S(1)}, u32[]{:S(2)}, u32[]{:S(2)}) collective-permute-start(bf16[32,3584]{1,0:T(8,128)(2,1)S(1)} %total.9.um_ref.base_ref), channel_id=1, source_target_pairs={{0,1},{1,0},{2,3},{3,2},{4,5},{5,4},{6,7},{7,6},{8,9},{9,8},{10,11... | collective-permute-start | bytes 688136 | tf_op jit(solution)/shard_map/ppermute | solution.py:468
  68.3 1.6 %collective-permute-start.22 = (bf16[32,3584]{1,0:T(8,128)(2,1)S(1)}, bf16[32,3584]{1,0:T(8,128)(2,1)S(1)}, u32[]{:S(2)}, u32[]{:S(2)}) collective-permute-start(bf16[32,3584]{1,0:T(8,128)(2,1)S(1)} %get-tuple-element.148), channel_id=1, source_target_pairs={{0,1},{1,0},{2,3},{3,2},{4,5},{5,4},{6,7},{7,6},{8,9},{9,8},{10,11... | collective-permute-start | bytes 688136 | tf_op jit(solution)/shard_map/ppermute | solution.py:468
  68.5 4.7 %collective-permute-start.24 = (bf16[64,3584]{1,0:T(8,128)(2,1)S(1)}, bf16[64,3584]{1,0:T(8,128)(2,1)S(1)}, u32[]{:S(2)}, u32[]{:S(2)}) collective-permute-start(bf16[64,3584]{1,0:T(8,128)(2,1)S(1)} %stack.114), channel_id=1, source_target_pairs={{0,1},{1,0},{2,3},{3,2},{4,20},{5,21},{6,22},{7,23},{8,24},{9,25},... | collective-permute-start | bytes 1376264 | tf_op jit(solution)/shard_map/ppermute | solution.py:511
  70.2 7.7 %collective-permute-start.23 = (bf16[32,3584]{1,0:T(8,128)(2,1)S(1)}, bf16[32,3584]{1,0:T(8,128)(2,1)S(1)}, u32[]{:S(2)}, u32[]{:S(2)}) collective-permute-start(bf16[32,3584]{1,0:T(8,128)(2,1)S(1)} %hold.10.refs_0_), channel_id=1, source_target_pairs={{0,2},{1,3},{2,0},{3,1},{4,6},{5,7},{6,4},{7,5},{8,10},{9,11},{10,... | collective-permute-start | bytes 688136 | tf_op jit(solution)/shard_map/ppermute | solution.py:471
  71.6 16.8 %collective-permute-start.26 = (bf16[32,3584]{1,0:T(8,128)(2,1)S(1)}, bf16[32,3584]{1,0:T(8,128)(2,1)S(1)}, u32[]{:S(2)}, u32[]{:S(2)}) collective-permute-start(bf16[32,3584]{1,0:T(8,128)(2,1)S(1)} %get-tuple-element.154.refs_0_), channel_id=1, source_target_pairs={{0,12},{1,13},{2,14},{3,15},{4,8},{5,9},{6,10},{7,11},{8,4},{9,5},... | collective-permute-start | bytes 688136 | tf_op jit(solution)/shard_map/ppermute | solution.py:511
  78.0 10.4 %collective-permute-start.25 = (bf16[32,3584]{1,0:T(8,128)(2,1)S(1)}, bf16[32,3584]{1,0:T(8,128)(2,1)S(1)}, u32[]{:S(2)}, u32[]{:S(2)}) collective-permute-start(bf16[32,3584]{1,0:T(8,128)(2,1)S(1)} %total.10.um_ref.base_ref), channel_id=1, source_target_pairs={{0,1},{1,0},{2,3},{3,2},{4,5},{5,4},{6,7},{7,6},{8,9},{9,8},{10,11... | collective-permute-start | bytes 688136 | tf_op jit(solution)/shard_map/ppermute | solution.py:468
  78.1 14.2 %collective-permute-start.29 = (bf16[64,3584]{1,0:T(8,128)(2,1)S(1)}, bf16[64,3584]{1,0:T(8,128)(2,1)S(1)}, u32[]{:S(2)}, u32[]{:S(2)}) collective-permute-start(bf16[64,3584]{1,0:T(8,128)(2,1)S(1)} %collective-permute-done.24.p1), channel_id=1, source_target_pairs={{0,1},{1,0},{2,3},{3,2},{4,5},{5,4},{6,7},{7,6},{8,9},{9,8},{10,11... | collective-permute-start | bytes 1376264 | tf_op jit(solution)/shard_map/ppermute | solution.py:468
  90.4 1.6 %collective-permute-start.27 = (bf16[32,3584]{1,0:T(8,128)(2,1)S(1)}, bf16[32,3584]{1,0:T(8,128)(2,1)S(1)}, u32[]{:S(2)}, u32[]{:S(2)}) collective-permute-start(bf16[32,3584]{1,0:T(8,128)(2,1)S(1)} %get-tuple-element.159), channel_id=1, source_target_pairs={{0,1},{1,0},{2,3},{3,2},{4,5},{5,4},{6,7},{7,6},{8,9},{9,8},{10,11... | collective-permute-start | bytes 688136 | tf_op jit(solution)/shard_map/ppermute | solution.py:468
  90.5 1.9 %collective-permute-start.28 = (bf16[32,3584]{1,0:T(8,128)(2,1)S(1)}, bf16[32,3584]{1,0:T(8,128)(2,1)S(1)}, u32[]{:S(2)}, u32[]{:S(2)}) collective-permute-start(bf16[32,3584]{1,0:T(8,128)(2,1)S(1)} %collective-permute-done.20.refs_1_.p0), channel_id=1, source_target_pairs={{0,1},{1,0},{2,3},{3,2},{4,5},{5,4},{6,7},{7,6},{8,9},{9,8},{10,11... | collective-permute-start | bytes 688136 | tf_op jit(solution)/shard_map/ppermute | solution.py:468
  92.3 7.7 %collective-permute-start.30 = (bf16[32,3584]{1,0:T(8,128)(2,1)S(1)}, bf16[32,3584]{1,0:T(8,128)(2,1)S(1)}, u32[]{:S(2)}, u32[]{:S(2)}) collective-permute-start(bf16[32,3584]{1,0:T(8,128)(2,1)S(1)} %hold.11.refs_0_), channel_id=1, source_target_pairs={{0,2},{1,3},{2,0},{3,1},{4,6},{5,7},{6,4},{7,5},{8,10},{9,11},{10,... | collective-permute-start | bytes 688136 | tf_op jit(solution)/shard_map/ppermute | solution.py:471
  93.8 11.9 %collective-permute-start.35 = (bf16[64,3584]{1,0:T(8,128)(2,1)S(1)}, bf16[64,3584]{1,0:T(8,128)(2,1)S(1)}, u32[]{:S(2)}, u32[]{:S(2)}) collective-permute-start(bf16[64,3584]{1,0:T(8,128)(2,1)S(1)} %stack.115), channel_id=1, source_target_pairs={{0,1},{1,0},{2,3},{3,2},{4,5},{5,4},{6,7},{7,6},{8,24},{9,25},{10,... | collective-permute-start | bytes 1376264 | tf_op jit(solution)/shard_map/ppermute | solution.py:511
  100.3 12.7 %collective-permute-start.33 = (bf16[32,3584]{1,0:T(8,128)(2,1)S(1)}, bf16[32,3584]{1,0:T(8,128)(2,1)S(1)}, u32[]{:S(2)}, u32[]{:S(2)}) collective-permute-start(bf16[32,3584]{1,0:T(8,128)(2,1)S(1)} %get-tuple-element.163), channel_id=1, source_target_pairs={{20,0},{21,1},{22,2},{23,3},{24,4},{25,5},{26,6},{27,7},{4,16},{5,... | collective-permute-start | bytes 688136 | tf_op jit(solution)/shard_map/ppermute | solution.py:511
  101.8 14.4 %collective-permute-start.31 = (bf16[32,3584]{1,0:T(8,128)(2,1)S(1)}, bf16[32,3584]{1,0:T(8,128)(2,1)S(1)}, u32[]{:S(2)}, u32[]{:S(2)}) collective-permute-start(bf16[32,3584]{1,0:T(8,128)(2,1)S(1)} %get-tuple-element.163), channel_id=1, source_target_pairs={{4,0},{5,1},{6,2},{7,3},{8,4},{9,5},{10,6},{11,7},{20,16},{21,17},... | collective-permute-start | bytes 688136 | tf_op jit(solution)/shard_map/ppermute | solution.py:511
  103.1 20.9 %collective-permute-start.34 = (bf16[32,3584]{1,0:T(8,128)(2,1)S(1)}, bf16[32,3584]{1,0:T(8,128)(2,1)S(1)}, u32[]{:S(2)}, u32[]{:S(2)}) collective-permute-start(bf16[32,3584]{1,0:T(8,128)(2,1)S(1)} %get-tuple-element.164), channel_id=1, source_target_pairs={{24,0},{25,1},{26,2},{27,3},{20,4},{21,5},{22,6},{23,7},{8,16},{9,... | collective-permute-start | bytes 688136 | tf_op jit(solution)/shard_map/ppermute | solution.py:511
  104.4 22.6 %collective-permute-start.32 = (bf16[32,3584]{1,0:T(8,128)(2,1)S(1)}, bf16[32,3584]{1,0:T(8,128)(2,1)S(1)}, u32[]{:S(2)}, u32[]{:S(2)}) collective-permute-start(bf16[32,3584]{1,0:T(8,128)(2,1)S(1)} %get-tuple-element.164), channel_id=1, source_target_pairs={{8,0},{9,1},{10,2},{11,3},{24,16},{25,17},{26,18},{27,19}} | collective-permute-start | bytes 688136 | tf_op jit(solution)/shard_map/ppermute | solution.py:511
  127.0 7.0 %collective-permute-start.36 = (bf16[128,3584]{1,0:T(8,128)(2,1)S(1)}, bf16[128,3584]{1,0:T(8,128)(2,1)S(1)}, u32[]{:S(2)}, u32[]{:S(2)}) collective-permute-start(bf16[128,3584]{1,0:T(8,128)(2,1)S(1)} %stack.116.refs_0_), channel_id=1, source_target_pairs={{0,1},{1,0},{2,3},{3,2},{4,5},{5,4},{6,7},{7,6},{8,9},{9,8},{10,11... | collective-permute-start | bytes 2752520 | tf_op jit(solution)/shard_map/ppermute | solution.py:468
  127.1 3.4 %collective-permute-start.38 = (bf16[64,3584]{1,0:T(8,128)(2,1)S(1)}, bf16[64,3584]{1,0:T(8,128)(2,1)S(1)}, u32[]{:S(2)}, u32[]{:S(2)}) collective-permute-start(bf16[64,3584]{1,0:T(8,128)(2,1)S(1)} %collective-permute-done.35.q1.refs_7_), channel_id=1, source_target_pairs={{0,1},{1,0},{2,3},{3,2},{4,5},{5,4},{6,7},{7,6},{8,9},{9,8},{10,11... | collective-permute-start | bytes 1376264 | tf_op jit(solution)/shard_map/ppermute | solution.py:468
  127.6 2.9 %collective-permute-start.37 = (bf16[32,3584]{1,0:T(8,128)(2,1)S(1)}, bf16[32,3584]{1,0:T(8,128)(2,1)S(1)}, u32[]{:S(2)}, u32[]{:S(2)}) collective-permute-start(bf16[32,3584]{1,0:T(8,128)(2,1)S(1)} %collective-permute-done.26.refs_1_.q0.refs_6_), channel_id=1, source_target_pairs={{0,1},{1,0},{2,3},{3,2},{4,5},{5,4},{6,7},{7,6},{8,9},{9,8},{10,11... | collective-permute-start | bytes 688136 | tf_op jit(solution)/shard_map/ppermute | solution.py:468

commit v3 on v1

--- a/solution.py
+++ b/solution.py
@@ -126,13 +126,14 @@
         move.start()
     for i in range(marks_ref.shape[0]):
         marks_ref[i : i + 1] = jnp.full((1, marks_ref.shape[1]), flags_ref[i], jnp.int32)
+    copies = weight_copies(own_index(flags_ref, 0), w_ref, w_buf, sems, size)
+    ordered = [(matrix, k) for group in ((0, 1), (2,)) for k in range(w_buf.shape[1] // size) for matrix in group]
+    for key in ordered[:4]:
+        copies[key].start()
     for move in moves:
         move.wait()
-    copies = weight_copies(own_index(flags_ref, 0), w_ref, w_buf, sems, size)
-    for group in ((0, 1), (2,)):
-        for k in range(w_buf.shape[1] // size):
-            for matrix in group:
-                copies[matrix, k].start()
+    for key in ordered[4:]:
+        copies[key].start()
     gain = gain_at(flags_ref, gains_buf, 0)
     gate_ref[...], upper_ref[...] = forward_math(copies, xm_ref, xo_ref, gain, w_buf, pm_ref, po_ref, normed)
 
@@ -273,11 +274,11 @@
         start += rows.shape[0]
 
 
-def last_kernel(marks_ref, mine_ref, early_ref, first_ref, second_ref):
+def last_kernel(marks_ref, mine_ref, early_ref, arrived_ref, first_ref, second_ref):
     is_near = is_set(marks_ref, NEAR)
-    mine, early = mine_ref[...], early_ref[...]
-    first_ref[...] = choose(is_near, mine, early)
-    second_ref[...] = choose(is_near, early, mine)
+    mine = mine_ref[...]
+    first_ref[...] = choose(is_near, arrived_ref[...], mine)
+    second_ref[...] = choose(is_near, early_ref[...], mine)
 
 
 def sum_kernel(*refs):
@@ -346,7 +347,7 @@
     def take(count):
         return [refs.pop(0) for _ in range(count)]
 
-    direct, early, late, arrived = take(2), take(2), take(2), take(4)
+    direct, near_in, early, late, arrived = take(2), take(2), take(2), take(2), take(4)
     turned_ref, left_ref, right_ref, active_ref, early_ref, late_ref = take(6)
     out_ref, u_buf, d_act, out_buf, sems = take(5)
     features = turned_ref.shape[0]
@@ -370,7 +371,7 @@
     def lanes(source, *places):
         return [source.at[pl.ds(i * half, half)] for i in places]
 
-    near_sources = early + lanes(direct[0], 0, 3, 2) + lanes(direct[1], 0, 3, 2)
+    near_sources = early + near_in[:1] + lanes(direct[0], 3, 1) + near_in[1:] + lanes(direct[1], 3, 1)
     cases = (
         (True, True, direct, early_ref),
         (True, False, [us_ref.at[i] for i in range(pieces)], late_ref),
@@ -674,7 +675,11 @@
         held = hold(part, True, [pm, swap_core(po), up_mine, state_mine[part], gains], step not in (middle, 1))
         if step == 1:
             held, middle_arrived = lax.optimization_barrier((held, middle_arrived))
-            mine = total([held, swap_chip(held)])
+            held, near_up = lax.optimization_barrier((held, ups[0][0]))
+            crossed = swap_chip(held)
+            near_first = flow(near_up, 0, middle_near)
+            crossed, near_first = lax.optimization_barrier((crossed, near_first))
+            mine = total([held, crossed])
         elif step == middle:
             held, mixed = lax.optimization_barrier((held, kept[2]))
             up_mine = total([held, swap_chip(held)])
@@ -694,11 +699,11 @@
     def last_route(shift, source):
         return lambda copy, end, c: ((copy + shift) % REPL, source, 1, False) if c == 0 and end == 0 else None
 
-    payloads = call(last_kernel, "last", [marks, mine, ups[0][0]], [row] * 2, [], 4, 0, 0, smem=())
+    payloads = call(last_kernel, "last", [marks, mine, ups[0][0], near_first], [row] * 2, [], 4, 0, 0, smem=())
     straight = [
-        send(payloads[0], last_route(0, 0), flow_route(0, middle_near), whole=False),
-        send(payloads[1], last_route(0, 1), whole=False),
-        send(payloads[0], last_route(1, 0), flow_route(2, middle_near), whole=False),
+        send(mine, last_route(0, 0), whole=False),
+        send(payloads[0], last_route(0, 1), flow_route(1, middle_near), whole=False),
+        send(mine, last_route(1, 0), whole=False),
         send(payloads[1], last_route(1, 1), flow_route(1, middle_near), whole=False),
     ]
     mixed_arrived = with_other_core([mixed_first, mixed_second])
@@ -727,7 +732,7 @@
     return call(
         own_last_kernel,
         "own_last",
-        [flags, cot_rows, *direct, *ups[0], *ups[1], *mixed_arrived]
+        [flags, cot_rows, *direct, *with_other_core([near_first]), *ups[0], *ups[1], *mixed_arrived]
         + [*prepared, held_early, held_late],
         [shape(1, 3, features, narrow)],
         [

time: 136 us -> 135 us (level)
  waiting for transfers between devices: 72.1 us -> 70.7 us
    ppermute x20 -> x21, waiting for transfers between devices: 40.2 us -> 39.1 us  [send(): lax.ppermute(block, ('pipe', 'tensor'), completed(moves) if whole else mo...]
    ppermute x16 -> x17, starting transfers between devices: 3.01 us -> 3.46 us  [swap_core(): return lax.ppermute(block, 'tensor', core_swap)]
    ppermute x20 -> x21, starting transfers between devices: 24.1 us -> 24.5 us  [send(): lax.ppermute(block, ('pipe', 'tensor'), completed(moves) if whole else mo...]
    ppermute x16 -> x17, waiting for transfers between devices: 14.3 us -> 14.2 us  [swap_core(): return lax.ppermute(block, 'tensor', core_swap)]
  transfers between devices with their start and end apart: 39 -> 41, of which waited for: 28 -> 26; matrix products, arithmetic and copies ran while one was open for 0% -> 0% of each run, Pallas kernels for 10% -> 10%
where the time goes in v3:
time: 135 us
  waiting for transfers between devices  70.7 us (52%)
  starting transfers between devices  32.1 us (24%)
  Pallas kernels  31.4 us (23%)
    ppermute x21, waiting for transfers between devices, send(): lax.ppermute(block, ('pipe', 'tensor'), completed(moves) if whole else mo...  39.1 us
    pallas_call x28, Pallas kernels, call(): pl.pallas_call(kernel, out_shape=outs, in_specs=specs, out_specs=[out_spe...  31.4 us
    ppermute x21, starting transfers between devices, send(): lax.ppermute(block, ('pipe', 'tensor'), completed(moves) if whole else mo...  24.5 us
    ppermute x3, waiting for transfers between devices, swap_chip(): return lax.ppermute(block, 'tensor', chip_swap)  17.3 us
    ppermute x17, waiting for transfers between devices, swap_core(): return lax.ppermute(block, 'tensor', core_swap)  14.2 us
    ppermute x3, starting transfers between devices, swap_chip(): return lax.ppermute(block, 'tensor', chip_swap)  4.16 us
    ppermute x17, starting transfers between devices, swap_core(): return lax.ppermute(block, 'tensor', core_swap)  3.46 us
  transfers between devices with their start and end apart: 41, of which 26 were waited for; matrix products, arithmetic and copies ran while one was open for 0% of the time, Pallas kernels for 10%

profile of v3, /device:TPU:0, one launch (start us, length us, event | category | flops | bytes accessed | tf_op | source)
XLA Modules:
  0.0 134.8 jit_solution(5225637681849054086)
XLA Ops:
  0.1 5.3 %first_layer.1 = (bf16[32,3584]{1,0:T(8,128)(2,1)S(1)}, bf16[32,3584]{1,0:T(8,128)(2,1)S(1)}, f32[64,256]{1,0:T(8,128)S(1)}, f32[64,256]{1,0:T(8,128)S(1)}, bf16...) custom-call(s32[29]{0:T(128)S(1)} %stack.110.flags_ref, ...), custom_call_target="tpu_custom_call" | custom-call | flops 352321536 | bytes 5505024 | tf_op jit(solution)/shard_map/first_layer/pallas_call | solution.py:419
  6.0 1.1 collective-permute-done.recv_ref
  7.3 3.9 %collective-permute-start.3 = (bf16[16,3584]{1,0:T(8,128)(2,1)S(1)}, bf16[16,3584]{1,0:T(8,128)(2,1)S(1)}, u32[]{:S(2)}, u32[]{:S(2)}) collective-permute-start(bf16[16,3584]{1,0:T(8,128)(2,1)S(1)} %get-tuple-element.106), channel_id=1, source_target_pairs={{0,6},{1,7},{2,4},{3,5},{4,2},{5,3},{6,0},{7,1},{8,14},{9,15},{10,... | collective-permute-start | bytes 344072 | tf_op jit(solution)/shard_map/ppermute | solution.py:512
  11.2 0.5 collective-permute-start.1
  11.7 1.5 %collective-permute-start.4 = (bf16[16,3584]{1,0:T(8,128)(2,1)S(1)}, bf16[16,3584]{1,0:T(8,128)(2,1)S(1)}, u32[]{:S(2)}, u32[]{:S(2)}) collective-permute-start(bf16[16,3584]{1,0:T(8,128)(2,1)S(1)} %get-tuple-element.107), channel_id=1, source_target_pairs={{0,10},{1,11},{2,8},{3,9},{4,14},{5,15},{6,12},{7,13},{8,2},{9,3},... | collective-permute-start | bytes 344072 | tf_op jit(solution)/shard_map/ppermute | solution.py:512
  13.3 3.4 %load_late.1 = (bf16[3,3584,256]{2,1,0:T(8,128)(2,1)S(1)}, bf16[32,3584]{1,0:T(8,128)(2,1)S(1)}, bf16[32,3584]{1,0:T(8,128)(2,1)S(1)}) custom-call(s32[29]{0:T(128)S(1)} %stack.110.flags_ref, bf16[8,32,3584]{2,1,0:T(8,128)(2,1)} %bitcast.36, bf16[2,3,3584,256]{3,2,1,0:T(8,128)(2,1)} %bitcast.34), custom_call_target="tpu_custom_call" | custom-call | bytes 11010048 | tf_op jit(solution)/shard_map/load_late/pallas_call | solution.py:419
  16.7 0.6 collective-permute-done.1.refs_0_
  17.3 1.2 collective-permute-done.4.refs_3_
  19.1 1.5 %collective-permute-done.5.xo_ref = bf16[32,3584]{1,0:T(8,128)(2,1)S(1)} collective-permute-done((bf16[32,3584]{1,0:T(8,128)(2,1)S(1)}, bf16[32,3584]{1,0:T(8,128)(2,1)S(1)}, u32[]{:S(2)}, u32[]{:S(2)}) %collective-permute-start.5) | collective-permute-done | bytes 229408 | tf_op jit(solution)/shard_map/ppermute | solution.py:469
  20.6 1.6 %forward_layer.2 = (bf16[32,3584]{1,0:T(8,128)(2,1)S(1)}, bf16[32,3584]{1,0:T(8,128)(2,1)S(1)}, f32[64,256]{1,0:T(8,128)S(1)}, f32[64,256]{1,0:T(8,128)S(1)}, bf...) custom-call(s32[8,128]{1,0:T(8,128)S(1)} %get-tuple-element.102.flags_ref.marks_ref, ...), custom_call_target="tpu_custom_call" | custom-call | flops 352321536 | bytes 5505024 | tf_op jit(solution)/shard_map/forward_layer/pallas_call | solution.py:419
  22.4 1.4 %collective-permute-done.6.recv_ref = bf16[32,3584]{1,0:T(8,128)(2,1)S(1)} collective-permute-done((bf16[32,3584]{1,0:T(8,128)(2,1)S(1)}, bf16[32,3584]{1,0:T(8,128)(2,1)S(1)}, u32[]{:S(2)}, u32[]{:S(2)}) %collective-permute-start.6) | collective-permute-done | bytes 229408 | tf_op jit(solution)/shard_map/ppermute | solution.py:469
  23.9 1.4 %collective-permute-start.7 = (bf16[32,3584]{1,0:T(8,128)(2,1)S(1)}, bf16[32,3584]{1,0:T(8,128)(2,1)S(1)}, u32[]{:S(2)}, u32[]{:S(2)}) collective-permute-start(bf16[32,3584]{1,0:T(8,128)(2,1)S(1)} %hold.7.refs_0_), channel_id=1, source_target_pairs={{0,2},{1,3},{2,0},{3,1},{4,6},{5,7},{6,4},{7,5},{8,10},{9,11},{10,... | collective-permute-start | bytes 688136 | tf_op jit(solution)/shard_map/ppermute | solution.py:472
  25.3 6.3 %collective-permute-done.7.refs_1_ = bf16[32,3584]{1,0:T(8,128)(2,1)S(1)} collective-permute-done((bf16[32,3584]{1,0:T(8,128)(2,1)S(1)}, bf16[32,3584]{1,0:T(8,128)(2,1)S(1)}, u32[]{:S(2)}, u32[]{:S(2)}) %collective-permute-start.7) | collective-permute-done | bytes 229408 | tf_op jit(solution)/shard_map/ppermute | solution.py:472
  31.7 1.5 %collective-permute-done.8.xo_ref = bf16[32,3584]{1,0:T(8,128)(2,1)S(1)} collective-permute-done((bf16[32,3584]{1,0:T(8,128)(2,1)S(1)}, bf16[32,3584]{1,0:T(8,128)(2,1)S(1)}, u32[]{:S(2)}, u32[]{:S(2)}) %collective-permute-start.8) | collective-permute-done | bytes 229408 | tf_op jit(solution)/shard_map/ppermute | solution.py:469
  33.2 1.5 %forward_layer.3 = (bf16[32,3584]{1,0:T(8,128)(2,1)S(1)}, bf16[32,3584]{1,0:T(8,128)(2,1)S(1)}, f32[64,256]{1,0:T(8,128)S(1)}, f32[64,256]{1,0:T(8,128)S(1)}, bf...) custom-call(s32[8,128]{1,0:T(8,128)S(1)} %get-tuple-element.102.flags_ref.marks_ref, ...), custom_call_target="tpu_custom_call" | custom-call | flops 352321536 | bytes 5505024 | tf_op jit(solution)/shard_map/forward_layer/pallas_call | solution.py:419
  34.9 1.4 %collective-permute-done.9.recv_ref = bf16[32,3584]{1,0:T(8,128)(2,1)S(1)} collective-permute-done((bf16[32,3584]{1,0:T(8,128)(2,1)S(1)}, bf16[32,3584]{1,0:T(8,128)(2,1)S(1)}, u32[]{:S(2)}, u32[]{:S(2)}) %collective-permute-start.9) | collective-permute-done | bytes 229408 | tf_op jit(solution)/shard_map/ppermute | solution.py:469
  36.5 2.4 %collective-permute-start.12 = (bf16[16,3584]{1,0:T(8,128)(2,1)S(1)}, bf16[16,3584]{1,0:T(8,128)(2,1)S(1)}, u32[]{:S(2)}, u32[]{:S(2)}) collective-permute-start(bf16[16,3584]{1,0:T(8,128)(2,1)S(1)} %get-tuple-element.124), channel_id=1, source_target_pairs={{0,6},{1,7},{2,4},{3,5},{4,2},{5,3},{6,0},{7,1},{8,14},{9,15},{10,... | collective-permute-start | bytes 344072 | tf_op jit(solution)/shard_map/ppermute | solution.py:512
  39.4 1.6 %collective-permute-start.13 = (bf16[16,3584]{1,0:T(8,128)(2,1)S(1)}, bf16[16,3584]{1,0:T(8,128)(2,1)S(1)}, u32[]{:S(2)}, u32[]{:S(2)}) collective-permute-start(bf16[16,3584]{1,0:T(8,128)(2,1)S(1)} %get-tuple-element.125), channel_id=1, source_target_pairs={{0,10},{1,11},{2,8},{3,9},{4,14},{5,15},{6,12},{7,13},{8,2},{9,3},... | collective-permute-start | bytes 344072 | tf_op jit(solution)/shard_map/ppermute | solution.py:512
  41.5 2.9 %load_rows.1 = (bf16[8,32,3584]{2,1,0:T(8,128)(2,1)S(1)}, bf16[8,32,3584]{2,1,0:T(8,128)(2,1)S(1)}) custom-call(s32[29]{0:T(128)S(1)} %stack.110.flags_ref, bf16[8,32,3584]{2,1,0:T(8,128)(2,1)} %bitcast.39, bf16[8,32,3584]{2,1,0:T(8,128)(2,1)} %bitcast.37), custom_call_target="tpu_custom_call" | custom-call | bytes 5505024 | tf_op jit(solution)/shard_map/load_rows/pallas_call | solution.py:419
  45.0 1.2 collective-permute-done.13.refs_3_
  47.0 1.3 collective-permute-done.14.xo_ref
  48.3 2.2 %turn_layer.1 = (bf16[32,3584]{1,0:T(8,128)(2,1)S(1)}, bf16[32,3584]{1,0:T(8,128)(2,1)S(1)}, bf16[32,3584]{1,0:T(8,128)(2,1)S(1)}, bf16[32,3584]{1,0:T(8,128)(2,1)S(1)}) custom-call(s32[8,128]{1,0:T(8,128)S(1)} %get-tuple-element.102.flags_ref.marks_ref, f32[64,256]{1,0:T(8,128)S(1)} %cotangent.1.d_ref, bf16[32,3584]{1,0:T(8,128)(2,1)S(1)} %total.8.xm_ref, ...), custom_call_target="tpu_custom_call" | custom-call | flops 352321536 | bytes 5505024 | tf_op jit(solution)/shard_map/turn_layer/pallas_call | solution.py:419
  51.0 1.0 collective-permute-done.15.recv_ref
  52.4 2.5 %collective-permute-start.18 = (bf16[16,3584]{1,0:T(8,128)(2,1)S(1)}, bf16[16,3584]{1,0:T(8,128)(2,1)S(1)}, u32[]{:S(2)}, u32[]{:S(2)}) collective-permute-start(bf16[16,3584]{1,0:T(8,128)(2,1)S(1)} %get-tuple-element.145), channel_id=1, source_target_pairs={{0,6},{1,7},{2,4},{3,5},{4,2},{5,3},{6,0},{7,1},{8,14},{9,15},{10,... | collective-permute-start | bytes 344072 | tf_op jit(solution)/shard_map/ppermute | solution.py:512
  55.3 1.7 %collective-permute-start.19 = (bf16[16,3584]{1,0:T(8,128)(2,1)S(1)}, bf16[16,3584]{1,0:T(8,128)(2,1)S(1)}, u32[]{:S(2)}, u32[]{:S(2)}) collective-permute-start(bf16[16,3584]{1,0:T(8,128)(2,1)S(1)} %get-tuple-element.146), channel_id=1, source_target_pairs={{0,10},{1,11},{2,8},{3,9},{4,14},{5,15},{6,12},{7,13},{8,2},{9,3},... | collective-permute-start | bytes 344072 | tf_op jit(solution)/shard_map/ppermute | solution.py:512
  57.4 3.9 %collective-permute-done.18.refs_2_ = bf16[16,3584]{1,0:T(8,128)(2,1)S(1)} collective-permute-done((bf16[16,3584]{1,0:T(8,128)(2,1)S(1)}, bf16[16,3584]{1,0:T(8,128)(2,1)S(1)}, u32[]{:S(2)}, u32[]{:S(2)}) %collective-permute-start.18) | collective-permute-done | bytes 114720 | tf_op jit(solution)/shard_map/ppermute | solution.py:512
  61.3 2.4 %collective-permute-done.16.refs_0_ = bf16[16,3584]{1,0:T(8,128)(2,1)S(1)} collective-permute-done((bf16[16,3584]{1,0:T(8,128)(2,1)S(1)}, bf16[16,3584]{1,0:T(8,128)(2,1)S(1)}, u32[]{:S(2)}, u32[]{:S(2)}) %collective-permute-start.16) | collective-permute-done | bytes 114720 | tf_op jit(solution)/shard_map/ppermute | solution.py:512
  63.7 0.7 collective-permute-done.17.refs_1_
  64.6 1.5 %collective-permute-done.21.uo_ref = bf16[32,3584]{1,0:T(8,128)(2,1)S(1)} collective-permute-done((bf16[32,3584]{1,0:T(8,128)(2,1)S(1)}, bf16[32,3584]{1,0:T(8,128)(2,1)S(1)}, u32[]{:S(2)}, u32[]{:S(2)}) %collective-permute-start.21) | collective-permute-done | bytes 229408 | tf_op jit(solution)/shard_map/ppermute | solution.py:469
  66.0 2.1 %backward_layer.2 = (bf16[32,3584]{1,0:T(8,128)(2,1)S(1)}, bf16[32,3584]{1,0:T(8,128)(2,1)S(1)}, bf16[32,3584]{1,0:T(8,128)(2,1)S(1)}, bf16[32,3584]{1,0:T(8,128)(2,1)S(1)}, bf16[32,3584]{1,0:T(8,128)(2,1)S(1)}) custom-call(s32[8,128]{1,0:T(8,128)S(1)} %get-tuple-element.102.flags_ref.marks_ref, bf16[32,3584]{1,0:T(8,128)(2,1)S(1)} %total.9.um_ref.base_ref, ...), custom_call_target="tpu_custom_call" | custom-call | flops 352321536 | bytes 5505024 | tf_op jit(solution)/shard_map/backward_layer/pallas_call | solution.py:419
  68.8 0.9 collective-permute-done.22.recv_ref
  70.1 1.4 %collective-permute-start.23 = (bf16[32,3584]{1,0:T(8,128)(2,1)S(1)}, bf16[32,3584]{1,0:T(8,128)(2,1)S(1)}, u32[]{:S(2)}, u32[]{:S(2)}) collective-permute-start(bf16[32,3584]{1,0:T(8,128)(2,1)S(1)} %hold.10.refs_0_), channel_id=1, source_target_pairs={{0,2},{1,3},{2,0},{3,1},{4,6},{5,7},{6,4},{7,5},{8,10},{9,11},{10,... | collective-permute-start | bytes 688136 | tf_op jit(solution)/shard_map/ppermute | solution.py:472
  71.5 1.6 %collective-permute-start.25 = (bf16[32,3584]{1,0:T(8,128)(2,1)S(1)}, bf16[32,3584]{1,0:T(8,128)(2,1)S(1)}, u32[]{:S(2)}, u32[]{:S(2)}) collective-permute-start(bf16[32,3584]{1,0:T(8,128)(2,1)S(1)} %get-tuple-element.158.refs_0_), channel_id=1, source_target_pairs={{0,12},{1,13},{2,14},{3,15},{4,8},{5,9},{6,10},{7,11},{8,4},{9,5},... | collective-permute-start | bytes 688136 | tf_op jit(solution)/shard_map/ppermute | solution.py:512
  73.0 4.8 %collective-permute-done.23.refs_1_ = bf16[32,3584]{1,0:T(8,128)(2,1)S(1)} collective-permute-done((bf16[32,3584]{1,0:T(8,128)(2,1)S(1)}, bf16[32,3584]{1,0:T(8,128)(2,1)S(1)}, u32[]{:S(2)}, u32[]{:S(2)}) %collective-permute-start.23) | collective-permute-done | bytes 229408 | tf_op jit(solution)/shard_map/ppermute | solution.py:472
  77.9 10.3 %collective-permute-done.25.refs_1_.q0.refs_8_ = bf16[32,3584]{1,0:T(8,128)(2,1)S(1)} collective-permute-done((bf16[32,3584]{1,0:T(8,128)(2,1)S(1)}, bf16[32,3584]{1,0:T(8,128)(2,1)S(1)}, u32[]{:S(2)}, u32[]{:S(2)}) %collective-permute-start.25) | collective-permute-done | bytes 229408 | tf_op jit(solution)/shard_map/ppermute | solution.py:512
  88.3 1.9 %backward_layer.3 = (bf16[32,3584]{1,0:T(8,128)(2,1)S(1)}, bf16[32,3584]{1,0:T(8,128)(2,1)S(1)}, bf16[32,3584]{1,0:T(8,128)(2,1)S(1)}, bf16[32,3584]{1,0:T(8,128)(2,1)S(1)}) custom-call(s32[8,128]{1,0:T(8,128)S(1)} %get-tuple-element.102.flags_ref.marks_ref, bf16[32,3584]{1,0:T(8,128)(2,1)S(1)} %total.10.um_ref.base_ref, ...), custom_call_target="tpu_custom_call" | custom-call | flops 352321536 | bytes 5505024 | tf_op jit(solution)/shard_map/backward_layer/pallas_call | solution.py:419
  90.2 0.6 collective-permute-start.27
  92.8 1.3 collective-permute-start.30
  94.1 6.3 %collective-permute-done.30.refs_1_ = bf16[32,3584]{1,0:T(8,128)(2,1)S(1)} collective-permute-done((bf16[32,3584]{1,0:T(8,128)(2,1)S(1)}, bf16[32,3584]{1,0:T(8,128)(2,1)S(1)}, u32[]{:S(2)}, u32[]{:S(2)}) %collective-permute-start.30) | collective-permute-done | bytes 229408 | tf_op jit(solution)/shard_map/ppermute | solution.py:472
  101.1 1.3 collective-permute-start.34
  102.4 1.3 collective-permute-start.32
  103.8 1.3 collective-permute-start.33
  105.2 1.3 collective-permute-start.35
  106.5 3.5 %own_first.1 = (bf16[3584,256]{1,0:T(8,128)(2,1)S(1)}, f32[256,256]{1,0:T(8,128)S(1)}, f32[256,256]{1,0:T(8,128)S(1)}, bf16[256,256]{1,0:T(8,128)(2,1)S(1)}) custom-call(s32[29]{0:T(128)S(1)} %stack.110.flags_ref, bf16[8,32,3584]{2,1,0:T(8,128)(2,1)S(1)} %get-tuple-element.175.xs_ref, bf16[32,3584]{1,0:T(8,128)(2,1)S(1)} %get-tuple-element.136.early_ref.refs_0_.em_ref, ...), custom_call_target="tpu_custom_call" | custom-call | flops 939524096 | bytes 7340032 | tf_op jit(solution)/shard_map/own_first/pallas_call | solution.py:419
  110.0 10.6 %collective-permute-done.34.refs_2_ = bf16[32,3584]{1,0:T(8,128)(2,1)S(1)} collective-permute-done((bf16[32,3584]{1,0:T(8,128)(2,1)S(1)}, bf16[32,3584]{1,0:T(8,128)(2,1)S(1)}, u32[]{:S(2)}, u32[]{:S(2)}) %collective-permute-start.34) | collective-permute-done | bytes 229408 | tf_op jit(solution)/shard_map/ppermute | solution.py:512
  120.5 7.1 %collective-permute-done.35.refs_3_ = bf16[32,3584]{1,0:T(8,128)(2,1)S(1)} collective-permute-done((bf16[32,3584]{1,0:T(8,128)(2,1)S(1)}, bf16[32,3584]{1,0:T(8,128)(2,1)S(1)}, u32[]{:S(2)}, u32[]{:S(2)}) %collective-permute-start.35) | collective-permute-done | bytes 229408 | tf_op jit(solution)/shard_map/ppermute | solution.py:512
  128.3 2.3 %collective-permute-done.40.refs_3_ = bf16[32,3584]{1,0:T(8,128)(2,1)S(1)} collective-permute-done((bf16[32,3584]{1,0:T(8,128)(2,1)S(1)}, bf16[32,3584]{1,0:T(8,128)(2,1)S(1)}, u32[]{:S(2)}, u32[]{:S(2)}) %collective-permute-start.40) | collective-permute-done | bytes 229408 | tf_op jit(solution)/shard_map/ppermute | solution.py:469
  130.6 4.1 %own_last.1 = bf16[1,3,3584,256]{3,2,1,0:T(8,128)(2,1)} custom-call(s32[29]{0:T(128)S(1)} %stack.110.flags_ref, bf16[8,32,3584]{2,1,0:T(8,128)(2,1)S(1)} %get-tuple-element.130.us_ref, bf16[128,3584]{1,0:T(8,128)(2,1)S(1)} %stack.116.refs_0_, bf16[128,3584]{1,0:T(8,128)(2,1)S(1)} %collective-permute-done.39.refs_1_, ...), custom_call_target="tpu_custom_call" | custom-call | flops 1879048192 | bytes 7340032 | tf_op jit(solution)/shard_map/own_last/pallas_call | solution.py:419
  (65 shorter events, 11.1 us)
Async XLA Ops:
  5.5 1.6 %collective-permute-start = (bf16[32,3584]{1,0:T(8,128)(2,1)S(1)}, bf16[32,3584]{1,0:T(8,128)(2,1)S(1)}, u32[]{:S(2)}, u32[]{:S(2)}) collective-permute-start(bf16[32,3584]{1,0:T(8,128)(2,1)S(1)} %get-tuple-element.104), channel_id=1, source_target_pairs={{0,1},{1,0},{2,3},{3,2},{4,5},{5,4},{6,7},{7,6},{8,9},{9,8},{10,11... | collective-permute-start | bytes 688136 | tf_op jit(solution)/shard_map/ppermute | solution.py:469
  7.3 9.4 %collective-permute-start.3 = (bf16[16,3584]{1,0:T(8,128)(2,1)S(1)}, bf16[16,3584]{1,0:T(8,128)(2,1)S(1)}, u32[]{:S(2)}, u32[]{:S(2)}) collective-permute-start(bf16[16,3584]{1,0:T(8,128)(2,1)S(1)} %get-tuple-element.106), channel_id=1, source_target_pairs={{0,6},{1,7},{2,4},{3,5},{4,2},{5,3},{6,0},{7,1},{8,14},{9,15},{10,... | collective-permute-start | bytes 344072 | tf_op jit(solution)/shard_map/ppermute | solution.py:512
  11.2 6.2 %collective-permute-start.1 = (bf16[16,3584]{1,0:T(8,128)(2,1)S(1)}, bf16[16,3584]{1,0:T(8,128)(2,1)S(1)}, u32[]{:S(2)}, u32[]{:S(2)}) collective-permute-start(bf16[16,3584]{1,0:T(8,128)(2,1)S(1)} %get-tuple-element.106), channel_id=1, source_target_pairs={{0,4},{1,5},{2,6},{3,7},{4,0},{5,1},{6,2},{7,3},{8,12},{9,13},{10,... | collective-permute-start | bytes 344072 | tf_op jit(solution)/shard_map/ppermute | solution.py:512
  11.7 6.8 %collective-permute-start.4 = (bf16[16,3584]{1,0:T(8,128)(2,1)S(1)}, bf16[16,3584]{1,0:T(8,128)(2,1)S(1)}, u32[]{:S(2)}, u32[]{:S(2)}) collective-permute-start(bf16[16,3584]{1,0:T(8,128)(2,1)S(1)} %get-tuple-element.107), channel_id=1, source_target_pairs={{0,10},{1,11},{2,8},{3,9},{4,14},{5,15},{6,12},{7,13},{8,2},{9,3},... | collective-permute-start | bytes 344072 | tf_op jit(solution)/shard_map/ppermute | solution.py:512
  13.2 5.7 %collective-permute-start.2 = (bf16[16,3584]{1,0:T(8,128)(2,1)S(1)}, bf16[16,3584]{1,0:T(8,128)(2,1)S(1)}, u32[]{:S(2)}, u32[]{:S(2)}) collective-permute-start(bf16[16,3584]{1,0:T(8,128)(2,1)S(1)} %get-tuple-element.107), channel_id=1, source_target_pairs={{0,8},{1,9},{2,10},{3,11},{4,12},{5,13},{6,14},{7,15},{8,0},{9,1},... | collective-permute-start | bytes 344072 | tf_op jit(solution)/shard_map/ppermute | solution.py:512
  13.3 7.3 %copy-start = (f32[1,2,3584]{2,1,0:T(2,128)S(1)}, f32[1,2,3584]{2,1,0:T(2,128)}, u32[]{:S(2)}) copy-start(f32[1,2,3584]{2,1,0:T(2,128)} %param.7) | copy-start | bytes 86020
  19.0 1.6 %collective-permute-start.5 = (bf16[32,3584]{1,0:T(8,128)(2,1)S(1)}, bf16[32,3584]{1,0:T(8,128)(2,1)S(1)}, u32[]{:S(2)}, u32[]{:S(2)}) collective-permute-start(bf16[32,3584]{1,0:T(8,128)(2,1)S(1)} %total.6.xm_ref.base_ref), channel_id=1, source_target_pairs={{0,1},{1,0},{2,3},{3,2},{4,5},{5,4},{6,7},{7,6},{8,9},{9,8},{10,11... | collective-permute-start | bytes 688136 | tf_op jit(solution)/shard_map/ppermute | solution.py:469
  22.2 1.6 %collective-permute-start.6 = (bf16[32,3584]{1,0:T(8,128)(2,1)S(1)}, bf16[32,3584]{1,0:T(8,128)(2,1)S(1)}, u32[]{:S(2)}, u32[]{:S(2)}) collective-permute-start(bf16[32,3584]{1,0:T(8,128)(2,1)S(1)} %get-tuple-element.120), channel_id=1, source_target_pairs={{0,1},{1,0},{2,3},{3,2},{4,5},{5,4},{6,7},{7,6},{8,9},{9,8},{10,11... | collective-permute-start | bytes 688136 | tf_op jit(solution)/shard_map/ppermute | solution.py:469
  23.9 7.7 %collective-permute-start.7 = (bf16[32,3584]{1,0:T(8,128)(2,1)S(1)}, bf16[32,3584]{1,0:T(8,128)(2,1)S(1)}, u32[]{:S(2)}, u32[]{:S(2)}) collective-permute-start(bf16[32,3584]{1,0:T(8,128)(2,1)S(1)} %hold.7.refs_0_), channel_id=1, source_target_pairs={{0,2},{1,3},{2,0},{3,1},{4,6},{5,7},{6,4},{7,5},{8,10},{9,11},{10,... | collective-permute-start | bytes 688136 | tf_op jit(solution)/shard_map/ppermute | solution.py:472
  31.7 1.6 %collective-permute-start.8 = (bf16[32,3584]{1,0:T(8,128)(2,1)S(1)}, bf16[32,3584]{1,0:T(8,128)(2,1)S(1)}, u32[]{:S(2)}, u32[]{:S(2)}) collective-permute-start(bf16[32,3584]{1,0:T(8,128)(2,1)S(1)} %total.7.xm_ref.base_ref), channel_id=1, source_target_pairs={{0,1},{1,0},{2,3},{3,2},{4,5},{5,4},{6,7},{7,6},{8,9},{9,8},{10,11... | collective-permute-start | bytes 688136 | tf_op jit(solution)/shard_map/ppermute | solution.py:469
  34.7 1.6 %collective-permute-start.9 = (bf16[32,3584]{1,0:T(8,128)(2,1)S(1)}, bf16[32,3584]{1,0:T(8,128)(2,1)S(1)}, u32[]{:S(2)}, u32[]{:S(2)}) collective-permute-start(bf16[32,3584]{1,0:T(8,128)(2,1)S(1)} %get-tuple-element.123), channel_id=1, source_target_pairs={{0,1},{1,0},{2,3},{3,2},{4,5},{5,4},{6,7},{7,6},{8,9},{9,8},{10,11... | collective-permute-start | bytes 688136 | tf_op jit(solution)/shard_map/ppermute | solution.py:469
  36.5 8.3 %collective-permute-start.12 = (bf16[16,3584]{1,0:T(8,128)(2,1)S(1)}, bf16[16,3584]{1,0:T(8,128)(2,1)S(1)}, u32[]{:S(2)}, u32[]{:S(2)}) collective-permute-start(bf16[16,3584]{1,0:T(8,128)(2,1)S(1)} %get-tuple-element.124), channel_id=1, source_target_pairs={{0,6},{1,7},{2,4},{3,5},{4,2},{5,3},{6,0},{7,1},{8,14},{9,15},{10,... | collective-permute-start | bytes 344072 | tf_op jit(solution)/shard_map/ppermute | solution.py:512
  38.8 6.2 %collective-permute-start.10 = (bf16[16,3584]{1,0:T(8,128)(2,1)S(1)}, bf16[16,3584]{1,0:T(8,128)(2,1)S(1)}, u32[]{:S(2)}, u32[]{:S(2)}) collective-permute-start(bf16[16,3584]{1,0:T(8,128)(2,1)S(1)} %get-tuple-element.124), channel_id=1, source_target_pairs={{0,4},{1,5},{2,6},{3,7},{4,0},{5,1},{6,2},{7,3},{8,12},{9,13},{10,... | collective-permute-start | bytes 344072 | tf_op jit(solution)/shard_map/ppermute | solution.py:512
  39.4 6.8 %collective-permute-start.13 = (bf16[16,3584]{1,0:T(8,128)(2,1)S(1)}, bf16[16,3584]{1,0:T(8,128)(2,1)S(1)}, u32[]{:S(2)}, u32[]{:S(2)}) collective-permute-start(bf16[16,3584]{1,0:T(8,128)(2,1)S(1)} %get-tuple-element.125), channel_id=1, source_target_pairs={{0,10},{1,11},{2,8},{3,9},{4,14},{5,15},{6,12},{7,13},{8,2},{9,3},... | collective-permute-start | bytes 344072 | tf_op jit(solution)/shard_map/ppermute | solution.py:512
  41.0 5.7 %collective-permute-start.11 = (bf16[16,3584]{1,0:T(8,128)(2,1)S(1)}, bf16[16,3584]{1,0:T(8,128)(2,1)S(1)}, u32[]{:S(2)}, u32[]{:S(2)}) collective-permute-start(bf16[16,3584]{1,0:T(8,128)(2,1)S(1)} %get-tuple-element.125), channel_id=1, source_target_pairs={{0,8},{1,9},{2,10},{3,11},{4,12},{5,13},{6,14},{7,15},{8,0},{9,1},... | collective-permute-start | bytes 344072 | tf_op jit(solution)/shard_map/ppermute | solution.py:512
  46.7 1.6 %collective-permute-start.14 = (bf16[32,3584]{1,0:T(8,128)(2,1)S(1)}, bf16[32,3584]{1,0:T(8,128)(2,1)S(1)}, u32[]{:S(2)}, u32[]{:S(2)}) collective-permute-start(bf16[32,3584]{1,0:T(8,128)(2,1)S(1)} %total.8.xm_ref), channel_id=1, source_target_pairs={{0,1},{1,0},{2,3},{3,2},{4,5},{5,4},{6,7},{7,6},{8,9},{9,8},{10,11... | collective-permute-start | bytes 688136 | tf_op jit(solution)/shard_map/ppermute | solution.py:469
  50.5 1.6 %collective-permute-start.15 = (bf16[32,3584]{1,0:T(8,128)(2,1)S(1)}, bf16[32,3584]{1,0:T(8,128)(2,1)S(1)}, u32[]{:S(2)}, u32[]{:S(2)}) collective-permute-start(bf16[32,3584]{1,0:T(8,128)(2,1)S(1)} %get-tuple-element.143), channel_id=1, source_target_pairs={{0,1},{1,0},{2,3},{3,2},{4,5},{5,4},{6,7},{7,6},{8,9},{9,8},{10,11... | collective-permute-start | bytes 688136 | tf_op jit(solution)/shard_map/ppermute | solution.py:469
  50.6 6.8 %collective-permute-start.20 = (bf16[32,3584]{1,0:T(8,128)(2,1)S(1)}, bf16[32,3584]{1,0:T(8,128)(2,1)S(1)}, u32[]{:S(2)}, u32[]{:S(2)}) collective-permute-start(bf16[32,3584]{1,0:T(8,128)(2,1)S(1)} %get-tuple-element.147), channel_id=1, source_target_pairs={{0,1},{1,0},{2,3},{3,2},{4,8},{5,9},{6,10},{7,11},{8,4},{9,5},{10,... | collective-permute-start | bytes 688136 | tf_op jit(solution)/shard_map/ppermute | solution.py:512
  52.4 8.9 %collective-permute-start.18 = (bf16[16,3584]{1,0:T(8,128)(2,1)S(1)}, bf16[16,3584]{1,0:T(8,128)(2,1)S(1)}, u32[]{:S(2)}, u32[]{:S(2)}) collective-permute-start(bf16[16,3584]{1,0:T(8,128)(2,1)S(1)} %get-tuple-element.145), channel_id=1, source_target_pairs={{0,6},{1,7},{2,4},{3,5},{4,2},{5,3},{6,0},{7,1},{8,14},{9,15},{10,... | collective-permute-start | bytes 344072 | tf_op jit(solution)/shard_map/ppermute | solution.py:512
  54.9 8.8 %collective-permute-start.16 = (bf16[16,3584]{1,0:T(8,128)(2,1)S(1)}, bf16[16,3584]{1,0:T(8,128)(2,1)S(1)}, u32[]{:S(2)}, u32[]{:S(2)}) collective-permute-start(bf16[16,3584]{1,0:T(8,128)(2,1)S(1)} %get-tuple-element.145), channel_id=1, source_target_pairs={{0,4},{1,5},{2,6},{3,7},{4,0},{5,1},{6,2},{7,3},{8,12},{9,13},{10,... | collective-permute-start | bytes 344072 | tf_op jit(solution)/shard_map/ppermute | solution.py:512
  55.3 8.5 %collective-permute-start.19 = (bf16[16,3584]{1,0:T(8,128)(2,1)S(1)}, bf16[16,3584]{1,0:T(8,128)(2,1)S(1)}, u32[]{:S(2)}, u32[]{:S(2)}) collective-permute-start(bf16[16,3584]{1,0:T(8,128)(2,1)S(1)} %get-tuple-element.146), channel_id=1, source_target_pairs={{0,10},{1,11},{2,8},{3,9},{4,14},{5,15},{6,12},{7,13},{8,2},{9,3},... | collective-permute-start | bytes 344072 | tf_op jit(solution)/shard_map/ppermute | solution.py:512
  57.0 7.4 %collective-permute-start.17 = (bf16[16,3584]{1,0:T(8,128)(2,1)S(1)}, bf16[16,3584]{1,0:T(8,128)(2,1)S(1)}, u32[]{:S(2)}, u32[]{:S(2)}) collective-permute-start(bf16[16,3584]{1,0:T(8,128)(2,1)S(1)} %get-tuple-element.146), channel_id=1, source_target_pairs={{0,8},{1,9},{2,10},{3,11},{4,12},{5,13},{6,14},{7,15},{8,0},{9,1},... | collective-permute-start | bytes 344072 | tf_op jit(solution)/shard_map/ppermute | solution.py:512
  64.5 1.6 %collective-permute-start.21 = (bf16[32,3584]{1,0:T(8,128)(2,1)S(1)}, bf16[32,3584]{1,0:T(8,128)(2,1)S(1)}, u32[]{:S(2)}, u32[]{:S(2)}) collective-permute-start(bf16[32,3584]{1,0:T(8,128)(2,1)S(1)} %total.9.um_ref.base_ref), channel_id=1, source_target_pairs={{0,1},{1,0},{2,3},{3,2},{4,5},{5,4},{6,7},{7,6},{8,9},{9,8},{10,11... | collective-permute-start | bytes 688136 | tf_op jit(solution)/shard_map/ppermute | solution.py:469
  68.1 1.6 %collective-permute-start.22 = (bf16[32,3584]{1,0:T(8,128)(2,1)S(1)}, bf16[32,3584]{1,0:T(8,128)(2,1)S(1)}, u32[]{:S(2)}, u32[]{:S(2)}) collective-permute-start(bf16[32,3584]{1,0:T(8,128)(2,1)S(1)} %get-tuple-element.155), channel_id=1, source_target_pairs={{0,1},{1,0},{2,3},{3,2},{4,5},{5,4},{6,7},{7,6},{8,9},{9,8},{10,11... | collective-permute-start | bytes 688136 | tf_op jit(solution)/shard_map/ppermute | solution.py:469
  68.4 9.6 %collective-permute-start.26 = (bf16[64,3584]{1,0:T(8,128)(2,1)S(1)}, bf16[64,3584]{1,0:T(8,128)(2,1)S(1)}, u32[]{:S(2)}, u32[]{:S(2)}) collective-permute-start(bf16[64,3584]{1,0:T(8,128)(2,1)S(1)} %stack.114), channel_id=1, source_target_pairs={{0,1},{1,0},{2,3},{3,2},{4,20},{5,21},{6,22},{7,23},{8,24},{9,25},... | collective-permute-start | bytes 1376264 | tf_op jit(solution)/shard_map/ppermute | solution.py:512
  70.1 7.7 %collective-permute-start.23 = (bf16[32,3584]{1,0:T(8,128)(2,1)S(1)}, bf16[32,3584]{1,0:T(8,128)(2,1)S(1)}, u32[]{:S(2)}, u32[]{:S(2)}) collective-permute-start(bf16[32,3584]{1,0:T(8,128)(2,1)S(1)} %hold.10.refs_0_), channel_id=1, source_target_pairs={{0,2},{1,3},{2,0},{3,1},{4,6},{5,7},{6,4},{7,5},{8,10},{9,11},{10,... | collective-permute-start | bytes 688136 | tf_op jit(solution)/shard_map/ppermute | solution.py:472
  71.5 16.8 %collective-permute-start.25 = (bf16[32,3584]{1,0:T(8,128)(2,1)S(1)}, bf16[32,3584]{1,0:T(8,128)(2,1)S(1)}, u32[]{:S(2)}, u32[]{:S(2)}) collective-permute-start(bf16[32,3584]{1,0:T(8,128)(2,1)S(1)} %get-tuple-element.158.refs_0_), channel_id=1, source_target_pairs={{0,12},{1,13},{2,14},{3,15},{4,8},{5,9},{6,10},{7,11},{8,4},{9,5},... | collective-permute-start | bytes 688136 | tf_op jit(solution)/shard_map/ppermute | solution.py:512
  77.9 10.4 %collective-permute-start.24 = (bf16[32,3584]{1,0:T(8,128)(2,1)S(1)}, bf16[32,3584]{1,0:T(8,128)(2,1)S(1)}, u32[]{:S(2)}, u32[]{:S(2)}) collective-permute-start(bf16[32,3584]{1,0:T(8,128)(2,1)S(1)} %total.10.um_ref.base_ref), channel_id=1, source_target_pairs={{0,1},{1,0},{2,3},{3,2},{4,5},{5,4},{6,7},{7,6},{8,9},{9,8},{10,11... | collective-permute-start | bytes 688136 | tf_op jit(solution)/shard_map/ppermute | solution.py:469
  88.3 4.0 %collective-permute-start.29 = (bf16[64,3584]{1,0:T(8,128)(2,1)S(1)}, bf16[64,3584]{1,0:T(8,128)(2,1)S(1)}, u32[]{:S(2)}, u32[]{:S(2)}) collective-permute-start(bf16[64,3584]{1,0:T(8,128)(2,1)S(1)} %collective-permute-done.26.p1), channel_id=1, source_target_pairs={{0,1},{1,0},{2,3},{3,2},{4,5},{5,4},{6,7},{7,6},{8,9},{9,8},{10,11... | collective-permute-start | bytes 1376264 | tf_op jit(solution)/shard_map/ppermute | solution.py:469
  90.2 1.7 %collective-permute-start.27 = (bf16[32,3584]{1,0:T(8,128)(2,1)S(1)}, bf16[32,3584]{1,0:T(8,128)(2,1)S(1)}, u32[]{:S(2)}, u32[]{:S(2)}) collective-permute-start(bf16[32,3584]{1,0:T(8,128)(2,1)S(1)} %get-tuple-element.165), channel_id=1, source_target_pairs={{0,1},{1,0},{2,3},{3,2},{4,5},{5,4},{6,7},{7,6},{8,9},{9,8},{10,11... | collective-permute-start | bytes 688136 | tf_op jit(solution)/shard_map/ppermute | solution.py:469
  90.8 1.5 %collective-permute-start.28 = (bf16[32,3584]{1,0:T(8,128)(2,1)S(1)}, bf16[32,3584]{1,0:T(8,128)(2,1)S(1)}, u32[]{:S(2)}, u32[]{:S(2)}) collective-permute-start(bf16[32,3584]{1,0:T(8,128)(2,1)S(1)} %collective-permute-done.20.refs_1_.p0), channel_id=1, source_target_pairs={{0,1},{1,0},{2,3},{3,2},{4,5},{5,4},{6,7},{7,6},{8,9},{9,8},{10,11... | collective-permute-start | bytes 688136 | tf_op jit(solution)/shard_map/ppermute | solution.py:469
  90.9 9.6 %collective-permute-start.36 = (bf16[64,3584]{1,0:T(8,128)(2,1)S(1)}, bf16[64,3584]{1,0:T(8,128)(2,1)S(1)}, u32[]{:S(2)}, u32[]{:S(2)}) collective-permute-start(bf16[64,3584]{1,0:T(8,128)(2,1)S(1)} %stack.115), channel_id=1, source_target_pairs={{0,1},{1,0},{2,3},{3,2},{4,5},{5,4},{6,7},{7,6},{8,24},{9,25},{10,... | collective-permute-start | bytes 1376264 | tf_op jit(solution)/shard_map/ppermute | solution.py:512
  92.3 1.8 %collective-permute-start.31 = (bf16[32,3584]{1,0:T(8,128)(2,1)S(1)}, bf16[32,3584]{1,0:T(8,128)(2,1)S(1)}, u32[]{:S(2)}, u32[]{:S(2)}) collective-permute-start(bf16[32,3584]{1,0:T(8,128)(2,1)S(1)} %get-tuple-element.170.early_ref.refs_4_), channel_id=1, source_target_pairs={{0,1},{1,0},{2,3},{3,2},{4,8},{5,9},{6,10},{7,11},{8,4},{9,5},{10,... | collective-permute-start | bytes 688136 | tf_op jit(solution)/shard_map/ppermute | solution.py:512
  92.8 7.6 %collective-permute-start.30 = (bf16[32,3584]{1,0:T(8,128)(2,1)S(1)}, bf16[32,3584]{1,0:T(8,128)(2,1)S(1)}, u32[]{:S(2)}, u32[]{:S(2)}) collective-permute-start(bf16[32,3584]{1,0:T(8,128)(2,1)S(1)} %hold.11.refs_0_), channel_id=1, source_target_pairs={{0,2},{1,3},{2,0},{3,1},{4,6},{5,7},{6,4},{7,5},{8,10},{9,11},{10,... | collective-permute-start | bytes 688136 | tf_op jit(solution)/shard_map/ppermute | solution.py:472
  100.5 6.0 %collective-permute-start.38 = (bf16[64,3584]{1,0:T(8,128)(2,1)S(1)}, bf16[64,3584]{1,0:T(8,128)(2,1)S(1)}, u32[]{:S(2)}, u32[]{:S(2)}) collective-permute-start(bf16[64,3584]{1,0:T(8,128)(2,1)S(1)} %collective-permute-done.36.q1.refs_9_), channel_id=1, source_target_pairs={{0,1},{1,0},{2,3},{3,2},{4,5},{5,4},{6,7},{7,6},{8,9},{9,8},{10,11... | collective-permute-start | bytes 1376264 | tf_op jit(solution)/shard_map/ppermute | solution.py:469
  100.6 4.6 %collective-permute-start.37 = (bf16[32,3584]{1,0:T(8,128)(2,1)S(1)}, bf16[32,3584]{1,0:T(8,128)(2,1)S(1)}, u32[]{:S(2)}, u32[]{:S(2)}) collective-permute-start(bf16[32,3584]{1,0:T(8,128)(2,1)S(1)} %collective-permute-done.25.refs_1_.q0.refs_8_), channel_id=1, source_target_pairs={{0,1},{1,0},{2,3},{3,2},{4,5},{5,4},{6,7},{7,6},{8,9},{9,8},{10,11... | collective-permute-start | bytes 688136 | tf_op jit(solution)/shard_map/ppermute | solution.py:469
  101.1 19.5 %collective-permute-start.34 = (bf16[32,3584]{1,0:T(8,128)(2,1)S(1)}, bf16[32,3584]{1,0:T(8,128)(2,1)S(1)}, u32[]{:S(2)}, u32[]{:S(2)}) collective-permute-start(bf16[32,3584]{1,0:T(8,128)(2,1)S(1)} %total.11.mine_ref), channel_id=1, source_target_pairs={{20,0},{21,1},{22,2},{23,3},{4,16},{5,17},{6,18},{7,19}} | collective-permute-start | bytes 688136 | tf_op jit(solution)/shard_map/ppermute | solution.py:512
  102.4 18.2 %collective-permute-start.32 = (bf16[32,3584]{1,0:T(8,128)(2,1)S(1)}, bf16[32,3584]{1,0:T(8,128)(2,1)S(1)}, u32[]{:S(2)}, u32[]{:S(2)}) collective-permute-start(bf16[32,3584]{1,0:T(8,128)(2,1)S(1)} %total.11.mine_ref), channel_id=1, source_target_pairs={{4,0},{5,1},{6,2},{7,3},{20,16},{21,17},{22,18},{23,19}} | collective-permute-start | bytes 688136 | tf_op jit(solution)/shard_map/ppermute | solution.py:512
  103.8 16.7 %collective-permute-start.33 = (bf16[32,3584]{1,0:T(8,128)(2,1)S(1)}, bf16[32,3584]{1,0:T(8,128)(2,1)S(1)}, u32[]{:S(2)}, u32[]{:S(2)}) collective-permute-start(bf16[32,3584]{1,0:T(8,128)(2,1)S(1)} %get-tuple-element.173), channel_id=1, source_target_pairs={{8,0},{9,1},{10,2},{11,3},{20,4},{21,5},{22,6},{23,7},{24,16},{25,... | collective-permute-start | bytes 688136 | tf_op jit(solution)/shard_map/ppermute | solution.py:512
  105.2 22.5 %collective-permute-start.35 = (bf16[32,3584]{1,0:T(8,128)(2,1)S(1)}, bf16[32,3584]{1,0:T(8,128)(2,1)S(1)}, u32[]{:S(2)}, u32[]{:S(2)}) collective-permute-start(bf16[32,3584]{1,0:T(8,128)(2,1)S(1)} %get-tuple-element.174), channel_id=1, source_target_pairs={{24,0},{25,1},{26,2},{27,3},{20,4},{21,5},{22,6},{23,7},{8,16},{9,... | collective-permute-start | bytes 688136 | tf_op jit(solution)/shard_map/ppermute | solution.py:512
  127.7 2.9 %collective-permute-start.39 = (bf16[128,3584]{1,0:T(8,128)(2,1)S(1)}, bf16[128,3584]{1,0:T(8,128)(2,1)S(1)}, u32[]{:S(2)}, u32[]{:S(2)}) collective-permute-start(bf16[128,3584]{1,0:T(8,128)(2,1)S(1)} %stack.116.refs_0_), channel_id=1, source_target_pairs={{0,1},{1,0},{2,3},{3,2},{4,5},{5,4},{6,7},{7,6},{8,9},{9,8},{10,11... | collective-permute-start | bytes 2752520 | tf_op jit(solution)/shard_map/ppermute | solution.py:469
  127.8 2.8 %collective-permute-start.40 = (bf16[32,3584]{1,0:T(8,128)(2,1)S(1)}, bf16[32,3584]{1,0:T(8,128)(2,1)S(1)}, u32[]{:S(2)}, u32[]{:S(2)}) collective-permute-start(bf16[32,3584]{1,0:T(8,128)(2,1)S(1)} %collective-permute-done.31.arrived_ref.refs_2_), channel_id=1, source_target_pairs={{0,1},{1,0},{2,3},{3,2},{4,5},{5,4},{6,7},{7,6},{8,9},{9,8},{10,11... | collective-permute-start | bytes 688136 | tf_op jit(solution)/shard_map/ppermute | solution.py:469

commit v4 on v3

--- a/solution.py
+++ b/solution.py
@@ -700,6 +700,7 @@
         return lambda copy, end, c: ((copy + shift) % REPL, source, 1, False) if c == 0 and end == 0 else None
 
     payloads = call(last_kernel, "last", [marks, mine, ups[0][0], near_first], [row] * 2, [], 4, 0, 0, smem=())
+    mine, payloads = lax.optimization_barrier((mine, payloads))
     straight = [
         send(mine, last_route(0, 0), whole=False),
         send(payloads[0], last_route(0, 1), flow_route(1, middle_near), whole=False),

time: 135 us -> 138 us (1.022)
  waiting for transfers between devices: 70.7 us -> 73.9 us
    ppermute x21, waiting for transfers between devices: 39.1 us -> 42.3 us  [send(): lax.ppermute(block, ('pipe', 'tensor'), completed(moves) if whole else mo...]
  transfers between devices with their start and end apart: 41 -> 41, of which waited for: 26 -> 27; matrix products, arithmetic and copies ran while one was open for 0% -> 0% of each run, Pallas kernels for 10% -> 10%
where the time goes in v4:
time: 138 us
  waiting for transfers between devices  73.9 us (54%)
  starting transfers between devices  32.1 us (23%)
  Pallas kernels  31.4 us (23%)
    ppermute x21, waiting for transfers between devices, send(): lax.ppermute(block, ('pipe', 'tensor'), completed(moves) if whole else mo...  42.3 us
    pallas_call x28, Pallas kernels, call(): pl.pallas_call(kernel, out_shape=outs, in_specs=specs, out_specs=[out_spe...  31.4 us
    ppermute x21, starting transfers between devices, send(): lax.ppermute(block, ('pipe', 'tensor'), completed(moves) if whole else mo...  24.5 us
    ppermute x3, waiting for transfers between devices, swap_chip(): return lax.ppermute(block, 'tensor', chip_swap)  17.3 us
    ppermute x17, waiting for transfers between devices, swap_core(): return lax.ppermute(block, 'tensor', core_swap)  14.2 us
    ppermute x3, starting transfers between devices, swap_chip(): return lax.ppermute(block, 'tensor', chip_swap)  4.16 us
    ppermute x17, starting transfers between devices, swap_core(): return lax.ppermute(block, 'tensor', core_swap)  3.46 us
  transfers between devices with their start and end apart: 41, of which 27 were waited for; matrix products, arithmetic and copies ran while one was open for 0% of the time, Pallas kernels for 10%

profile of v4, /device:TPU:0, one launch (start us, length us, event | category | flops | bytes accessed | tf_op | source)
XLA Modules:
  0.0 138.0 jit_solution(3338543527395193025)
XLA Ops:
  0.1 5.3 %first_layer.1 = (bf16[32,3584]{1,0:T(8,128)(2,1)S(1)}, bf16[32,3584]{1,0:T(8,128)(2,1)S(1)}, f32[64,256]{1,0:T(8,128)S(1)}, f32[64,256]{1,0:T(8,128)S(1)}, bf16...) custom-call(s32[29]{0:T(128)S(1)} %stack.110.flags_ref, ...), custom_call_target="tpu_custom_call" | custom-call | flops 352321536 | bytes 5505024 | tf_op jit(solution)/shard_map/first_layer/pallas_call | solution.py:419
  6.0 1.1 collective-permute-done.recv_ref
  7.3 3.9 %collective-permute-start.3 = (bf16[16,3584]{1,0:T(8,128)(2,1)S(1)}, bf16[16,3584]{1,0:T(8,128)(2,1)S(1)}, u32[]{:S(2)}, u32[]{:S(2)}) collective-permute-start(bf16[16,3584]{1,0:T(8,128)(2,1)S(1)} %get-tuple-element.109), channel_id=1, source_target_pairs={{0,6},{1,7},{2,4},{3,5},{4,2},{5,3},{6,0},{7,1},{8,14},{9,15},{10,... | collective-permute-start | bytes 344072 | tf_op jit(solution)/shard_map/ppermute | solution.py:512
  11.7 1.5 %collective-permute-start.4 = (bf16[16,3584]{1,0:T(8,128)(2,1)S(1)}, bf16[16,3584]{1,0:T(8,128)(2,1)S(1)}, u32[]{:S(2)}, u32[]{:S(2)}) collective-permute-start(bf16[16,3584]{1,0:T(8,128)(2,1)S(1)} %get-tuple-element.110), channel_id=1, source_target_pairs={{0,10},{1,11},{2,8},{3,9},{4,14},{5,15},{6,12},{7,13},{8,2},{9,3},... | collective-permute-start | bytes 344072 | tf_op jit(solution)/shard_map/ppermute | solution.py:512
  13.3 3.4 %load_late.1 = (bf16[3,3584,256]{2,1,0:T(8,128)(2,1)S(1)}, bf16[32,3584]{1,0:T(8,128)(2,1)S(1)}, bf16[32,3584]{1,0:T(8,128)(2,1)S(1)}) custom-call(s32[29]{0:T(128)S(1)} %stack.110.flags_ref, bf16[8,32,3584]{2,1,0:T(8,128)(2,1)} %bitcast.36, bf16[2,3,3584,256]{3,2,1,0:T(8,128)(2,1)} %bitcast.34), custom_call_target="tpu_custom_call" | custom-call | bytes 11010048 | tf_op jit(solution)/shard_map/load_late/pallas_call | solution.py:419
  16.7 0.6 collective-permute-done.1.refs_0_
  17.3 1.2 collective-permute-done.4.refs_3_
  19.1 1.5 %collective-permute-done.5.xo_ref = bf16[32,3584]{1,0:T(8,128)(2,1)S(1)} collective-permute-done((bf16[32,3584]{1,0:T(8,128)(2,1)S(1)}, bf16[32,3584]{1,0:T(8,128)(2,1)S(1)}, u32[]{:S(2)}, u32[]{:S(2)}) %collective-permute-start.5) | collective-permute-done | bytes 229408 | tf_op jit(solution)/shard_map/ppermute | solution.py:469
  20.6 1.6 %forward_layer.2 = (bf16[32,3584]{1,0:T(8,128)(2,1)S(1)}, bf16[32,3584]{1,0:T(8,128)(2,1)S(1)}, f32[64,256]{1,0:T(8,128)S(1)}, f32[64,256]{1,0:T(8,128)S(1)}, bf...) custom-call(s32[8,128]{1,0:T(8,128)S(1)} %get-tuple-element.105.flags_ref.marks_ref, ...), custom_call_target="tpu_custom_call" | custom-call | flops 352321536 | bytes 5505024 | tf_op jit(solution)/shard_map/forward_layer/pallas_call | solution.py:419
  22.4 1.4 collective-permute-done.6.recv_ref
  23.9 1.4 %collective-permute-start.7 = (bf16[32,3584]{1,0:T(8,128)(2,1)S(1)}, bf16[32,3584]{1,0:T(8,128)(2,1)S(1)}, u32[]{:S(2)}, u32[]{:S(2)}) collective-permute-start(bf16[32,3584]{1,0:T(8,128)(2,1)S(1)} %hold.7.refs_0_), channel_id=1, source_target_pairs={{0,2},{1,3},{2,0},{3,1},{4,6},{5,7},{6,4},{7,5},{8,10},{9,11},{10,... | collective-permute-start | bytes 688136 | tf_op jit(solution)/shard_map/ppermute | solution.py:472
  25.3 6.3 %collective-permute-done.7.refs_1_ = bf16[32,3584]{1,0:T(8,128)(2,1)S(1)} collective-permute-done((bf16[32,3584]{1,0:T(8,128)(2,1)S(1)}, bf16[32,3584]{1,0:T(8,128)(2,1)S(1)}, u32[]{:S(2)}, u32[]{:S(2)}) %collective-permute-start.7) | collective-permute-done | bytes 229408 | tf_op jit(solution)/shard_map/ppermute | solution.py:472
  31.7 1.5 %collective-permute-done.8.xo_ref = bf16[32,3584]{1,0:T(8,128)(2,1)S(1)} collective-permute-done((bf16[32,3584]{1,0:T(8,128)(2,1)S(1)}, bf16[32,3584]{1,0:T(8,128)(2,1)S(1)}, u32[]{:S(2)}, u32[]{:S(2)}) %collective-permute-start.8) | collective-permute-done | bytes 229408 | tf_op jit(solution)/shard_map/ppermute | solution.py:469
  33.2 1.5 %forward_layer.3 = (bf16[32,3584]{1,0:T(8,128)(2,1)S(1)}, bf16[32,3584]{1,0:T(8,128)(2,1)S(1)}, f32[64,256]{1,0:T(8,128)S(1)}, f32[64,256]{1,0:T(8,128)S(1)}, bf...) custom-call(s32[8,128]{1,0:T(8,128)S(1)} %get-tuple-element.105.flags_ref.marks_ref, ...), custom_call_target="tpu_custom_call" | custom-call | flops 352321536 | bytes 5505024 | tf_op jit(solution)/shard_map/forward_layer/pallas_call | solution.py:419
  34.9 1.4 collective-permute-done.9.recv_ref
  36.5 2.4 %collective-permute-start.12 = (bf16[16,3584]{1,0:T(8,128)(2,1)S(1)}, bf16[16,3584]{1,0:T(8,128)(2,1)S(1)}, u32[]{:S(2)}, u32[]{:S(2)}) collective-permute-start(bf16[16,3584]{1,0:T(8,128)(2,1)S(1)} %get-tuple-element.127), channel_id=1, source_target_pairs={{0,6},{1,7},{2,4},{3,5},{4,2},{5,3},{6,0},{7,1},{8,14},{9,15},{10,... | collective-permute-start | bytes 344072 | tf_op jit(solution)/shard_map/ppermute | solution.py:512
  39.4 1.6 %collective-permute-start.13 = (bf16[16,3584]{1,0:T(8,128)(2,1)S(1)}, bf16[16,3584]{1,0:T(8,128)(2,1)S(1)}, u32[]{:S(2)}, u32[]{:S(2)}) collective-permute-start(bf16[16,3584]{1,0:T(8,128)(2,1)S(1)} %get-tuple-element.128), channel_id=1, source_target_pairs={{0,10},{1,11},{2,8},{3,9},{4,14},{5,15},{6,12},{7,13},{8,2},{9,3},... | collective-permute-start | bytes 344072 | tf_op jit(solution)/shard_map/ppermute | solution.py:512
  41.5 2.9 %load_rows.1 = (bf16[8,32,3584]{2,1,0:T(8,128)(2,1)S(1)}, bf16[8,32,3584]{2,1,0:T(8,128)(2,1)S(1)}) custom-call(s32[29]{0:T(128)S(1)} %stack.110.flags_ref, bf16[8,32,3584]{2,1,0:T(8,128)(2,1)} %bitcast.39, bf16[8,32,3584]{2,1,0:T(8,128)(2,1)} %bitcast.37), custom_call_target="tpu_custom_call" | custom-call | bytes 5505024 | tf_op jit(solution)/shard_map/load_rows/pallas_call | solution.py:419
  45.0 1.2 collective-permute-done.13.refs_3_
  47.0 1.3 collective-permute-done.14.xo_ref
  48.3 2.2 %turn_layer.1 = (bf16[32,3584]{1,0:T(8,128)(2,1)S(1)}, bf16[32,3584]{1,0:T(8,128)(2,1)S(1)}, bf16[32,3584]{1,0:T(8,128)(2,1)S(1)}, bf16[32,3584]{1,0:T(8,128)(2,1)S(1)}) custom-call(s32[8,128]{1,0:T(8,128)S(1)} %get-tuple-element.105.flags_ref.marks_ref, f32[64,256]{1,0:T(8,128)S(1)} %cotangent.1.d_ref, bf16[32,3584]{1,0:T(8,128)(2,1)S(1)} %total.8.xm_ref, ...), custom_call_target="tpu_custom_call" | custom-call | flops 352321536 | bytes 5505024 | tf_op jit(solution)/shard_map/turn_layer/pallas_call | solution.py:419
  51.0 1.0 collective-permute-done.15.recv_ref
  52.4 2.5 %collective-permute-start.18 = (bf16[16,3584]{1,0:T(8,128)(2,1)S(1)}, bf16[16,3584]{1,0:T(8,128)(2,1)S(1)}, u32[]{:S(2)}, u32[]{:S(2)}) collective-permute-start(bf16[16,3584]{1,0:T(8,128)(2,1)S(1)} %get-tuple-element.148), channel_id=1, source_target_pairs={{0,6},{1,7},{2,4},{3,5},{4,2},{5,3},{6,0},{7,1},{8,14},{9,15},{10,... | collective-permute-start | bytes 344072 | tf_op jit(solution)/shard_map/ppermute | solution.py:512
  55.3 1.7 %collective-permute-start.19 = (bf16[16,3584]{1,0:T(8,128)(2,1)S(1)}, bf16[16,3584]{1,0:T(8,128)(2,1)S(1)}, u32[]{:S(2)}, u32[]{:S(2)}) collective-permute-start(bf16[16,3584]{1,0:T(8,128)(2,1)S(1)} %get-tuple-element.149), channel_id=1, source_target_pairs={{0,10},{1,11},{2,8},{3,9},{4,14},{5,15},{6,12},{7,13},{8,2},{9,3},... | collective-permute-start | bytes 344072 | tf_op jit(solution)/shard_map/ppermute | solution.py:512
  57.4 3.9 %collective-permute-done.18.refs_2_ = bf16[16,3584]{1,0:T(8,128)(2,1)S(1)} collective-permute-done((bf16[16,3584]{1,0:T(8,128)(2,1)S(1)}, bf16[16,3584]{1,0:T(8,128)(2,1)S(1)}, u32[]{:S(2)}, u32[]{:S(2)}) %collective-permute-start.18) | collective-permute-done | bytes 114720 | tf_op jit(solution)/shard_map/ppermute | solution.py:512
  61.3 2.4 %collective-permute-done.16.refs_0_ = bf16[16,3584]{1,0:T(8,128)(2,1)S(1)} collective-permute-done((bf16[16,3584]{1,0:T(8,128)(2,1)S(1)}, bf16[16,3584]{1,0:T(8,128)(2,1)S(1)}, u32[]{:S(2)}, u32[]{:S(2)}) %collective-permute-start.16) | collective-permute-done | bytes 114720 | tf_op jit(solution)/shard_map/ppermute | solution.py:512
  63.7 0.7 collective-permute-done.17.refs_1_
  64.6 1.5 %collective-permute-done.21.uo_ref = bf16[32,3584]{1,0:T(8,128)(2,1)S(1)} collective-permute-done((bf16[32,3584]{1,0:T(8,128)(2,1)S(1)}, bf16[32,3584]{1,0:T(8,128)(2,1)S(1)}, u32[]{:S(2)}, u32[]{:S(2)}) %collective-permute-start.21) | collective-permute-done | bytes 229408 | tf_op jit(solution)/shard_map/ppermute | solution.py:469
  66.0 2.1 %backward_layer.2 = (bf16[32,3584]{1,0:T(8,128)(2,1)S(1)}, bf16[32,3584]{1,0:T(8,128)(2,1)S(1)}, bf16[32,3584]{1,0:T(8,128)(2,1)S(1)}, bf16[32,3584]{1,0:T(8,128)(2,1)S(1)}, bf16[32,3584]{1,0:T(8,128)(2,1)S(1)}) custom-call(s32[8,128]{1,0:T(8,128)S(1)} %get-tuple-element.105.flags_ref.marks_ref, bf16[32,3584]{1,0:T(8,128)(2,1)S(1)} %total.9.um_ref.base_ref, ...), custom_call_target="tpu_custom_call" | custom-call | flops 352321536 | bytes 5505024 | tf_op jit(solution)/shard_map/backward_layer/pallas_call | solution.py:419
  68.8 0.9 collective-permute-done.22.recv_ref
  70.1 1.4 %collective-permute-start.23 = (bf16[32,3584]{1,0:T(8,128)(2,1)S(1)}, bf16[32,3584]{1,0:T(8,128)(2,1)S(1)}, u32[]{:S(2)}, u32[]{:S(2)}) collective-permute-start(bf16[32,3584]{1,0:T(8,128)(2,1)S(1)} %hold.10.refs_0_), channel_id=1, source_target_pairs={{0,2},{1,3},{2,0},{3,1},{4,6},{5,7},{6,4},{7,5},{8,10},{9,11},{10,... | collective-permute-start | bytes 688136 | tf_op jit(solution)/shard_map/ppermute | solution.py:472
  71.5 1.6 %collective-permute-start.25 = (bf16[32,3584]{1,0:T(8,128)(2,1)S(1)}, bf16[32,3584]{1,0:T(8,128)(2,1)S(1)}, u32[]{:S(2)}, u32[]{:S(2)}) collective-permute-start(bf16[32,3584]{1,0:T(8,128)(2,1)S(1)} %get-tuple-element.161.refs_0_), channel_id=1, source_target_pairs={{0,12},{1,13},{2,14},{3,15},{4,8},{5,9},{6,10},{7,11},{8,4},{9,5},... | collective-permute-start | bytes 688136 | tf_op jit(solution)/shard_map/ppermute | solution.py:512
  73.0 4.8 %collective-permute-done.23.refs_1_ = bf16[32,3584]{1,0:T(8,128)(2,1)S(1)} collective-permute-done((bf16[32,3584]{1,0:T(8,128)(2,1)S(1)}, bf16[32,3584]{1,0:T(8,128)(2,1)S(1)}, u32[]{:S(2)}, u32[]{:S(2)}) %collective-permute-start.23) | collective-permute-done | bytes 229408 | tf_op jit(solution)/shard_map/ppermute | solution.py:472
  77.9 10.3 %collective-permute-done.25.refs_1_.q0.refs_8_ = bf16[32,3584]{1,0:T(8,128)(2,1)S(1)} collective-permute-done((bf16[32,3584]{1,0:T(8,128)(2,1)S(1)}, bf16[32,3584]{1,0:T(8,128)(2,1)S(1)}, u32[]{:S(2)}, u32[]{:S(2)}) %collective-permute-start.25) | collective-permute-done | bytes 229408 | tf_op jit(solution)/shard_map/ppermute | solution.py:512
  88.3 1.9 %backward_layer.3 = (bf16[32,3584]{1,0:T(8,128)(2,1)S(1)}, bf16[32,3584]{1,0:T(8,128)(2,1)S(1)}, bf16[32,3584]{1,0:T(8,128)(2,1)S(1)}, bf16[32,3584]{1,0:T(8,128)(2,1)S(1)}) custom-call(s32[8,128]{1,0:T(8,128)S(1)} %get-tuple-element.105.flags_ref.marks_ref, bf16[32,3584]{1,0:T(8,128)(2,1)S(1)} %total.10.um_ref.base_ref, ...), custom_call_target="tpu_custom_call" | custom-call | flops 352321536 | bytes 5505024 | tf_op jit(solution)/shard_map/backward_layer/pallas_call | solution.py:419
  90.2 0.6 collective-permute-start.27
  92.8 1.3 collective-permute-start.30
  94.1 6.3 %collective-permute-done.30.refs_1_ = bf16[32,3584]{1,0:T(8,128)(2,1)S(1)} collective-permute-done((bf16[32,3584]{1,0:T(8,128)(2,1)S(1)}, bf16[32,3584]{1,0:T(8,128)(2,1)S(1)}, u32[]{:S(2)}, u32[]{:S(2)}) %collective-permute-start.30) | collective-permute-done | bytes 229408 | tf_op jit(solution)/shard_map/ppermute | solution.py:472
  101.2 1.3 collective-permute-start.33
  102.5 1.3 collective-permute-start.35
  103.8 1.3 collective-permute-start.34
  105.2 1.3 collective-permute-start.32
  106.5 3.5 %own_first.1 = (bf16[3584,256]{1,0:T(8,128)(2,1)S(1)}, f32[256,256]{1,0:T(8,128)S(1)}, f32[256,256]{1,0:T(8,128)S(1)}, bf16[256,256]{1,0:T(8,128)(2,1)S(1)}) custom-call(s32[29]{0:T(128)S(1)} %stack.110.flags_ref, bf16[8,32,3584]{2,1,0:T(8,128)(2,1)S(1)} %get-tuple-element.181.xs_ref, bf16[32,3584]{1,0:T(8,128)(2,1)S(1)} %get-tuple-element.139.early_ref.refs_0_.em_ref, ...), custom_call_target="tpu_custom_call" | custom-call | flops 939524096 | bytes 7340032 | tf_op jit(solution)/shard_map/own_first/pallas_call | solution.py:419
  110.0 4.6 %collective-permute-done.33.refs_1_ = bf16[32,3584]{1,0:T(8,128)(2,1)S(1)} collective-permute-done((bf16[32,3584]{1,0:T(8,128)(2,1)S(1)}, bf16[32,3584]{1,0:T(8,128)(2,1)S(1)}, u32[]{:S(2)}, u32[]{:S(2)}) %collective-permute-start.33) | collective-permute-done | bytes 229408 | tf_op jit(solution)/shard_map/ppermute | solution.py:512
  114.6 11.6 %collective-permute-done.35.refs_3_ = bf16[32,3584]{1,0:T(8,128)(2,1)S(1)} collective-permute-done((bf16[32,3584]{1,0:T(8,128)(2,1)S(1)}, bf16[32,3584]{1,0:T(8,128)(2,1)S(1)}, u32[]{:S(2)}, u32[]{:S(2)}) %collective-permute-start.35) | collective-permute-done | bytes 229408 | tf_op jit(solution)/shard_map/ppermute | solution.py:512
  126.3 4.6 %collective-permute-done.34.refs_2_ = bf16[32,3584]{1,0:T(8,128)(2,1)S(1)} collective-permute-done((bf16[32,3584]{1,0:T(8,128)(2,1)S(1)}, bf16[32,3584]{1,0:T(8,128)(2,1)S(1)}, u32[]{:S(2)}, u32[]{:S(2)}) %collective-permute-start.34) | collective-permute-done | bytes 229408 | tf_op jit(solution)/shard_map/ppermute | solution.py:512
  131.5 2.3 %collective-permute-done.40.refs_3_ = bf16[32,3584]{1,0:T(8,128)(2,1)S(1)} collective-permute-done((bf16[32,3584]{1,0:T(8,128)(2,1)S(1)}, bf16[32,3584]{1,0:T(8,128)(2,1)S(1)}, u32[]{:S(2)}, u32[]{:S(2)}) %collective-permute-start.40) | collective-permute-done | bytes 229408 | tf_op jit(solution)/shard_map/ppermute | solution.py:469
  133.8 4.1 %own_last.1 = bf16[1,3,3584,256]{3,2,1,0:T(8,128)(2,1)} custom-call(s32[29]{0:T(128)S(1)} %stack.110.flags_ref, bf16[8,32,3584]{2,1,0:T(8,128)(2,1)S(1)} %get-tuple-element.133.us_ref, bf16[128,3584]{1,0:T(8,128)(2,1)S(1)} %stack.116.refs_0_, bf16[128,3584]{1,0:T(8,128)(2,1)S(1)} %collective-permute-done.39.refs_1_, ...), custom_call_target="tpu_custom_call" | custom-call | flops 1879048192 | bytes 7340032 | tf_op jit(solution)/shard_map/own_last/pallas_call | solution.py:419
  (65 shorter events, 11.6 us)
Async XLA Ops:
  5.5 1.6 %collective-permute-start = (bf16[32,3584]{1,0:T(8,128)(2,1)S(1)}, bf16[32,3584]{1,0:T(8,128)(2,1)S(1)}, u32[]{:S(2)}, u32[]{:S(2)}) collective-permute-start(bf16[32,3584]{1,0:T(8,128)(2,1)S(1)} %get-tuple-element.107), channel_id=1, source_target_pairs={{0,1},{1,0},{2,3},{3,2},{4,5},{5,4},{6,7},{7,6},{8,9},{9,8},{10,11... | collective-permute-start | bytes 688136 | tf_op jit(solution)/shard_map/ppermute | solution.py:469
  7.3 9.4 %collective-permute-start.3 = (bf16[16,3584]{1,0:T(8,128)(2,1)S(1)}, bf16[16,3584]{1,0:T(8,128)(2,1)S(1)}, u32[]{:S(2)}, u32[]{:S(2)}) collective-permute-start(bf16[16,3584]{1,0:T(8,128)(2,1)S(1)} %get-tuple-element.109), channel_id=1, source_target_pairs={{0,6},{1,7},{2,4},{3,5},{4,2},{5,3},{6,0},{7,1},{8,14},{9,15},{10,... | collective-permute-start | bytes 344072 | tf_op jit(solution)/shard_map/ppermute | solution.py:512
  11.2 6.2 %collective-permute-start.1 = (bf16[16,3584]{1,0:T(8,128)(2,1)S(1)}, bf16[16,3584]{1,0:T(8,128)(2,1)S(1)}, u32[]{:S(2)}, u32[]{:S(2)}) collective-permute-start(bf16[16,3584]{1,0:T(8,128)(2,1)S(1)} %get-tuple-element.109), channel_id=1, source_target_pairs={{0,4},{1,5},{2,6},{3,7},{4,0},{5,1},{6,2},{7,3},{8,12},{9,13},{10,... | collective-permute-start | bytes 344072 | tf_op jit(solution)/shard_map/ppermute | solution.py:512
  11.7 6.8 %collective-permute-start.4 = (bf16[16,3584]{1,0:T(8,128)(2,1)S(1)}, bf16[16,3584]{1,0:T(8,128)(2,1)S(1)}, u32[]{:S(2)}, u32[]{:S(2)}) collective-permute-start(bf16[16,3584]{1,0:T(8,128)(2,1)S(1)} %get-tuple-element.110), channel_id=1, source_target_pairs={{0,10},{1,11},{2,8},{3,9},{4,14},{5,15},{6,12},{7,13},{8,2},{9,3},... | collective-permute-start | bytes 344072 | tf_op jit(solution)/shard_map/ppermute | solution.py:512
  13.2 5.7 %collective-permute-start.2 = (bf16[16,3584]{1,0:T(8,128)(2,1)S(1)}, bf16[16,3584]{1,0:T(8,128)(2,1)S(1)}, u32[]{:S(2)}, u32[]{:S(2)}) collective-permute-start(bf16[16,3584]{1,0:T(8,128)(2,1)S(1)} %get-tuple-element.110), channel_id=1, source_target_pairs={{0,8},{1,9},{2,10},{3,11},{4,12},{5,13},{6,14},{7,15},{8,0},{9,1},... | collective-permute-start | bytes 344072 | tf_op jit(solution)/shard_map/ppermute | solution.py:512
  13.3 7.3 %copy-start = (f32[1,2,3584]{2,1,0:T(2,128)S(1)}, f32[1,2,3584]{2,1,0:T(2,128)}, u32[]{:S(2)}) copy-start(f32[1,2,3584]{2,1,0:T(2,128)} %param.7) | copy-start | bytes 86020
  19.0 1.6 %collective-permute-start.5 = (bf16[32,3584]{1,0:T(8,128)(2,1)S(1)}, bf16[32,3584]{1,0:T(8,128)(2,1)S(1)}, u32[]{:S(2)}, u32[]{:S(2)}) collective-permute-start(bf16[32,3584]{1,0:T(8,128)(2,1)S(1)} %total.6.xm_ref.base_ref), channel_id=1, source_target_pairs={{0,1},{1,0},{2,3},{3,2},{4,5},{5,4},{6,7},{7,6},{8,9},{9,8},{10,11... | collective-permute-start | bytes 688136 | tf_op jit(solution)/shard_map/ppermute | solution.py:469
  22.2 1.6 %collective-permute-start.6 = (bf16[32,3584]{1,0:T(8,128)(2,1)S(1)}, bf16[32,3584]{1,0:T(8,128)(2,1)S(1)}, u32[]{:S(2)}, u32[]{:S(2)}) collective-permute-start(bf16[32,3584]{1,0:T(8,128)(2,1)S(1)} %get-tuple-element.123), channel_id=1, source_target_pairs={{0,1},{1,0},{2,3},{3,2},{4,5},{5,4},{6,7},{7,6},{8,9},{9,8},{10,11... | collective-permute-start | bytes 688136 | tf_op jit(solution)/shard_map/ppermute | solution.py:469
  23.9 7.7 %collective-permute-start.7 = (bf16[32,3584]{1,0:T(8,128)(2,1)S(1)}, bf16[32,3584]{1,0:T(8,128)(2,1)S(1)}, u32[]{:S(2)}, u32[]{:S(2)}) collective-permute-start(bf16[32,3584]{1,0:T(8,128)(2,1)S(1)} %hold.7.refs_0_), channel_id=1, source_target_pairs={{0,2},{1,3},{2,0},{3,1},{4,6},{5,7},{6,4},{7,5},{8,10},{9,11},{10,... | collective-permute-start | bytes 688136 | tf_op jit(solution)/shard_map/ppermute | solution.py:472
  31.7 1.6 %collective-permute-start.8 = (bf16[32,3584]{1,0:T(8,128)(2,1)S(1)}, bf16[32,3584]{1,0:T(8,128)(2,1)S(1)}, u32[]{:S(2)}, u32[]{:S(2)}) collective-permute-start(bf16[32,3584]{1,0:T(8,128)(2,1)S(1)} %total.7.xm_ref.base_ref), channel_id=1, source_target_pairs={{0,1},{1,0},{2,3},{3,2},{4,5},{5,4},{6,7},{7,6},{8,9},{9,8},{10,11... | collective-permute-start | bytes 688136 | tf_op jit(solution)/shard_map/ppermute | solution.py:469
  34.7 1.6 %collective-permute-start.9 = (bf16[32,3584]{1,0:T(8,128)(2,1)S(1)}, bf16[32,3584]{1,0:T(8,128)(2,1)S(1)}, u32[]{:S(2)}, u32[]{:S(2)}) collective-permute-start(bf16[32,3584]{1,0:T(8,128)(2,1)S(1)} %get-tuple-element.126), channel_id=1, source_target_pairs={{0,1},{1,0},{2,3},{3,2},{4,5},{5,4},{6,7},{7,6},{8,9},{9,8},{10,11... | collective-permute-start | bytes 688136 | tf_op jit(solution)/shard_map/ppermute | solution.py:469
  36.5 8.3 %collective-permute-start.12 = (bf16[16,3584]{1,0:T(8,128)(2,1)S(1)}, bf16[16,3584]{1,0:T(8,128)(2,1)S(1)}, u32[]{:S(2)}, u32[]{:S(2)}) collective-permute-start(bf16[16,3584]{1,0:T(8,128)(2,1)S(1)} %get-tuple-element.127), channel_id=1, source_target_pairs={{0,6},{1,7},{2,4},{3,5},{4,2},{5,3},{6,0},{7,1},{8,14},{9,15},{10,... | collective-permute-start | bytes 344072 | tf_op jit(solution)/shard_map/ppermute | solution.py:512
  38.8 6.2 %collective-permute-start.10 = (bf16[16,3584]{1,0:T(8,128)(2,1)S(1)}, bf16[16,3584]{1,0:T(8,128)(2,1)S(1)}, u32[]{:S(2)}, u32[]{:S(2)}) collective-permute-start(bf16[16,3584]{1,0:T(8,128)(2,1)S(1)} %get-tuple-element.127), channel_id=1, source_target_pairs={{0,4},{1,5},{2,6},{3,7},{4,0},{5,1},{6,2},{7,3},{8,12},{9,13},{10,... | collective-permute-start | bytes 344072 | tf_op jit(solution)/shard_map/ppermute | solution.py:512
  39.4 6.8 %collective-permute-start.13 = (bf16[16,3584]{1,0:T(8,128)(2,1)S(1)}, bf16[16,3584]{1,0:T(8,128)(2,1)S(1)}, u32[]{:S(2)}, u32[]{:S(2)}) collective-permute-start(bf16[16,3584]{1,0:T(8,128)(2,1)S(1)} %get-tuple-element.128), channel_id=1, source_target_pairs={{0,10},{1,11},{2,8},{3,9},{4,14},{5,15},{6,12},{7,13},{8,2},{9,3},... | collective-permute-start | bytes 344072 | tf_op jit(solution)/shard_map/ppermute | solution.py:512
  41.0 5.7 %collective-permute-start.11 = (bf16[16,3584]{1,0:T(8,128)(2,1)S(1)}, bf16[16,3584]{1,0:T(8,128)(2,1)S(1)}, u32[]{:S(2)}, u32[]{:S(2)}) collective-permute-start(bf16[16,3584]{1,0:T(8,128)(2,1)S(1)} %get-tuple-element.128), channel_id=1, source_target_pairs={{0,8},{1,9},{2,10},{3,11},{4,12},{5,13},{6,14},{7,15},{8,0},{9,1},... | collective-permute-start | bytes 344072 | tf_op jit(solution)/shard_map/ppermute | solution.py:512
  46.7 1.6 %collective-permute-start.14 = (bf16[32,3584]{1,0:T(8,128)(2,1)S(1)}, bf16[32,3584]{1,0:T(8,128)(2,1)S(1)}, u32[]{:S(2)}, u32[]{:S(2)}) collective-permute-start(bf16[32,3584]{1,0:T(8,128)(2,1)S(1)} %total.8.xm_ref), channel_id=1, source_target_pairs={{0,1},{1,0},{2,3},{3,2},{4,5},{5,4},{6,7},{7,6},{8,9},{9,8},{10,11... | collective-permute-start | bytes 688136 | tf_op jit(solution)/shard_map/ppermute | solution.py:469
  50.5 1.6 %collective-permute-start.15 = (bf16[32,3584]{1,0:T(8,128)(2,1)S(1)}, bf16[32,3584]{1,0:T(8,128)(2,1)S(1)}, u32[]{:S(2)}, u32[]{:S(2)}) collective-permute-start(bf16[32,3584]{1,0:T(8,128)(2,1)S(1)} %get-tuple-element.146), channel_id=1, source_target_pairs={{0,1},{1,0},{2,3},{3,2},{4,5},{5,4},{6,7},{7,6},{8,9},{9,8},{10,11... | collective-permute-start | bytes 688136 | tf_op jit(solution)/shard_map/ppermute | solution.py:469
  50.6 6.8 %collective-permute-start.20 = (bf16[32,3584]{1,0:T(8,128)(2,1)S(1)}, bf16[32,3584]{1,0:T(8,128)(2,1)S(1)}, u32[]{:S(2)}, u32[]{:S(2)}) collective-permute-start(bf16[32,3584]{1,0:T(8,128)(2,1)S(1)} %get-tuple-element.150), channel_id=1, source_target_pairs={{0,1},{1,0},{2,3},{3,2},{4,8},{5,9},{6,10},{7,11},{8,4},{9,5},{10,... | collective-permute-start | bytes 688136 | tf_op jit(solution)/shard_map/ppermute | solution.py:512
  52.4 8.9 %collective-permute-start.18 = (bf16[16,3584]{1,0:T(8,128)(2,1)S(1)}, bf16[16,3584]{1,0:T(8,128)(2,1)S(1)}, u32[]{:S(2)}, u32[]{:S(2)}) collective-permute-start(bf16[16,3584]{1,0:T(8,128)(2,1)S(1)} %get-tuple-element.148), channel_id=1, source_target_pairs={{0,6},{1,7},{2,4},{3,5},{4,2},{5,3},{6,0},{7,1},{8,14},{9,15},{10,... | collective-permute-start | bytes 344072 | tf_op jit(solution)/shard_map/ppermute | solution.py:512
  54.9 8.8 %collective-permute-start.16 = (bf16[16,3584]{1,0:T(8,128)(2,1)S(1)}, bf16[16,3584]{1,0:T(8,128)(2,1)S(1)}, u32[]{:S(2)}, u32[]{:S(2)}) collective-permute-start(bf16[16,3584]{1,0:T(8,128)(2,1)S(1)} %get-tuple-element.148), channel_id=1, source_target_pairs={{0,4},{1,5},{2,6},{3,7},{4,0},{5,1},{6,2},{7,3},{8,12},{9,13},{10,... | collective-permute-start | bytes 344072 | tf_op jit(solution)/shard_map/ppermute | solution.py:512
  55.3 8.5 %collective-permute-start.19 = (bf16[16,3584]{1,0:T(8,128)(2,1)S(1)}, bf16[16,3584]{1,0:T(8,128)(2,1)S(1)}, u32[]{:S(2)}, u32[]{:S(2)}) collective-permute-start(bf16[16,3584]{1,0:T(8,128)(2,1)S(1)} %get-tuple-element.149), channel_id=1, source_target_pairs={{0,10},{1,11},{2,8},{3,9},{4,14},{5,15},{6,12},{7,13},{8,2},{9,3},... | collective-permute-start | bytes 344072 | tf_op jit(solution)/shard_map/ppermute | solution.py:512
  57.0 7.4 %collective-permute-start.17 = (bf16[16,3584]{1,0:T(8,128)(2,1)S(1)}, bf16[16,3584]{1,0:T(8,128)(2,1)S(1)}, u32[]{:S(2)}, u32[]{:S(2)}) collective-permute-start(bf16[16,3584]{1,0:T(8,128)(2,1)S(1)} %get-tuple-element.149), channel_id=1, source_target_pairs={{0,8},{1,9},{2,10},{3,11},{4,12},{5,13},{6,14},{7,15},{8,0},{9,1},... | collective-permute-start | bytes 344072 | tf_op jit(solution)/shard_map/ppermute | solution.py:512
  64.5 1.6 %collective-permute-start.21 = (bf16[32,3584]{1,0:T(8,128)(2,1)S(1)}, bf16[32,3584]{1,0:T(8,128)(2,1)S(1)}, u32[]{:S(2)}, u32[]{:S(2)}) collective-permute-start(bf16[32,3584]{1,0:T(8,128)(2,1)S(1)} %total.9.um_ref.base_ref), channel_id=1, source_target_pairs={{0,1},{1,0},{2,3},{3,2},{4,5},{5,4},{6,7},{7,6},{8,9},{9,8},{10,11... | collective-permute-start | bytes 688136 | tf_op jit(solution)/shard_map/ppermute | solution.py:469
  68.1 1.6 %collective-permute-start.22 = (bf16[32,3584]{1,0:T(8,128)(2,1)S(1)}, bf16[32,3584]{1,0:T(8,128)(2,1)S(1)}, u32[]{:S(2)}, u32[]{:S(2)}) collective-permute-start(bf16[32,3584]{1,0:T(8,128)(2,1)S(1)} %get-tuple-element.158), channel_id=1, source_target_pairs={{0,1},{1,0},{2,3},{3,2},{4,5},{5,4},{6,7},{7,6},{8,9},{9,8},{10,11... | collective-permute-start | bytes 688136 | tf_op jit(solution)/shard_map/ppermute | solution.py:469
  68.4 9.6 %collective-permute-start.26 = (bf16[64,3584]{1,0:T(8,128)(2,1)S(1)}, bf16[64,3584]{1,0:T(8,128)(2,1)S(1)}, u32[]{:S(2)}, u32[]{:S(2)}) collective-permute-start(bf16[64,3584]{1,0:T(8,128)(2,1)S(1)} %stack.114), channel_id=1, source_target_pairs={{0,1},{1,0},{2,3},{3,2},{4,20},{5,21},{6,22},{7,23},{8,24},{9,25},... | collective-permute-start | bytes 1376264 | tf_op jit(solution)/shard_map/ppermute | solution.py:512
  70.1 7.7 %collective-permute-start.23 = (bf16[32,3584]{1,0:T(8,128)(2,1)S(1)}, bf16[32,3584]{1,0:T(8,128)(2,1)S(1)}, u32[]{:S(2)}, u32[]{:S(2)}) collective-permute-start(bf16[32,3584]{1,0:T(8,128)(2,1)S(1)} %hold.10.refs_0_), channel_id=1, source_target_pairs={{0,2},{1,3},{2,0},{3,1},{4,6},{5,7},{6,4},{7,5},{8,10},{9,11},{10,... | collective-permute-start | bytes 688136 | tf_op jit(solution)/shard_map/ppermute | solution.py:472
  71.5 16.8 %collective-permute-start.25 = (bf16[32,3584]{1,0:T(8,128)(2,1)S(1)}, bf16[32,3584]{1,0:T(8,128)(2,1)S(1)}, u32[]{:S(2)}, u32[]{:S(2)}) collective-permute-start(bf16[32,3584]{1,0:T(8,128)(2,1)S(1)} %get-tuple-element.161.refs_0_), channel_id=1, source_target_pairs={{0,12},{1,13},{2,14},{3,15},{4,8},{5,9},{6,10},{7,11},{8,4},{9,5},... | collective-permute-start | bytes 688136 | tf_op jit(solution)/shard_map/ppermute | solution.py:512
  77.9 10.4 %collective-permute-start.24 = (bf16[32,3584]{1,0:T(8,128)(2,1)S(1)}, bf16[32,3584]{1,0:T(8,128)(2,1)S(1)}, u32[]{:S(2)}, u32[]{:S(2)}) collective-permute-start(bf16[32,3584]{1,0:T(8,128)(2,1)S(1)} %total.10.um_ref.base_ref), channel_id=1, source_target_pairs={{0,1},{1,0},{2,3},{3,2},{4,5},{5,4},{6,7},{7,6},{8,9},{9,8},{10,11... | collective-permute-start | bytes 688136 | tf_op jit(solution)/shard_map/ppermute | solution.py:469
  88.3 4.0 %collective-permute-start.29 = (bf16[64,3584]{1,0:T(8,128)(2,1)S(1)}, bf16[64,3584]{1,0:T(8,128)(2,1)S(1)}, u32[]{:S(2)}, u32[]{:S(2)}) collective-permute-start(bf16[64,3584]{1,0:T(8,128)(2,1)S(1)} %collective-permute-done.26.p1), channel_id=1, source_target_pairs={{0,1},{1,0},{2,3},{3,2},{4,5},{5,4},{6,7},{7,6},{8,9},{9,8},{10,11... | collective-permute-start | bytes 1376264 | tf_op jit(solution)/shard_map/ppermute | solution.py:469
  90.2 1.7 %collective-permute-start.27 = (bf16[32,3584]{1,0:T(8,128)(2,1)S(1)}, bf16[32,3584]{1,0:T(8,128)(2,1)S(1)}, u32[]{:S(2)}, u32[]{:S(2)}) collective-permute-start(bf16[32,3584]{1,0:T(8,128)(2,1)S(1)} %get-tuple-element.168), channel_id=1, source_target_pairs={{0,1},{1,0},{2,3},{3,2},{4,5},{5,4},{6,7},{7,6},{8,9},{9,8},{10,11... | collective-permute-start | bytes 688136 | tf_op jit(solution)/shard_map/ppermute | solution.py:469
  90.8 1.5 %collective-permute-start.28 = (bf16[32,3584]{1,0:T(8,128)(2,1)S(1)}, bf16[32,3584]{1,0:T(8,128)(2,1)S(1)}, u32[]{:S(2)}, u32[]{:S(2)}) collective-permute-start(bf16[32,3584]{1,0:T(8,128)(2,1)S(1)} %collective-permute-done.20.refs_1_.p0), channel_id=1, source_target_pairs={{0,1},{1,0},{2,3},{3,2},{4,5},{5,4},{6,7},{7,6},{8,9},{9,8},{10,11... | collective-permute-start | bytes 688136 | tf_op jit(solution)/shard_map/ppermute | solution.py:469
  90.9 9.6 %collective-permute-start.36 = (bf16[64,3584]{1,0:T(8,128)(2,1)S(1)}, bf16[64,3584]{1,0:T(8,128)(2,1)S(1)}, u32[]{:S(2)}, u32[]{:S(2)}) collective-permute-start(bf16[64,3584]{1,0:T(8,128)(2,1)S(1)} %stack.115), channel_id=1, source_target_pairs={{0,1},{1,0},{2,3},{3,2},{4,5},{5,4},{6,7},{7,6},{8,24},{9,25},{10,... | collective-permute-start | bytes 1376264 | tf_op jit(solution)/shard_map/ppermute | solution.py:512
  92.3 1.8 %collective-permute-start.31 = (bf16[32,3584]{1,0:T(8,128)(2,1)S(1)}, bf16[32,3584]{1,0:T(8,128)(2,1)S(1)}, u32[]{:S(2)}, u32[]{:S(2)}) collective-permute-start(bf16[32,3584]{1,0:T(8,128)(2,1)S(1)} %get-tuple-element.173.early_ref.refs_4_), channel_id=1, source_target_pairs={{0,1},{1,0},{2,3},{3,2},{4,8},{5,9},{6,10},{7,11},{8,4},{9,5},{10,... | collective-permute-start | bytes 688136 | tf_op jit(solution)/shard_map/ppermute | solution.py:512
  92.8 7.6 %collective-permute-start.30 = (bf16[32,3584]{1,0:T(8,128)(2,1)S(1)}, bf16[32,3584]{1,0:T(8,128)(2,1)S(1)}, u32[]{:S(2)}, u32[]{:S(2)}) collective-permute-start(bf16[32,3584]{1,0:T(8,128)(2,1)S(1)} %hold.11.refs_0_), channel_id=1, source_target_pairs={{0,2},{1,3},{2,0},{3,1},{4,6},{5,7},{6,4},{7,5},{8,10},{9,11},{10,... | collective-permute-start | bytes 688136 | tf_op jit(solution)/shard_map/ppermute | solution.py:472
  100.5 6.0 %collective-permute-start.38 = (bf16[64,3584]{1,0:T(8,128)(2,1)S(1)}, bf16[64,3584]{1,0:T(8,128)(2,1)S(1)}, u32[]{:S(2)}, u32[]{:S(2)}) collective-permute-start(bf16[64,3584]{1,0:T(8,128)(2,1)S(1)} %collective-permute-done.36.q1.refs_9_), channel_id=1, source_target_pairs={{0,1},{1,0},{2,3},{3,2},{4,5},{5,4},{6,7},{7,6},{8,9},{9,8},{10,11... | collective-permute-start | bytes 1376264 | tf_op jit(solution)/shard_map/ppermute | solution.py:469
  100.6 4.6 %collective-permute-start.37 = (bf16[32,3584]{1,0:T(8,128)(2,1)S(1)}, bf16[32,3584]{1,0:T(8,128)(2,1)S(1)}, u32[]{:S(2)}, u32[]{:S(2)}) collective-permute-start(bf16[32,3584]{1,0:T(8,128)(2,1)S(1)} %collective-permute-done.25.refs_1_.q0.refs_8_), channel_id=1, source_target_pairs={{0,1},{1,0},{2,3},{3,2},{4,5},{5,4},{6,7},{7,6},{8,9},{9,8},{10,11... | collective-permute-start | bytes 688136 | tf_op jit(solution)/shard_map/ppermute | solution.py:469
  101.2 13.4 %collective-permute-start.33 = (bf16[32,3584]{1,0:T(8,128)(2,1)S(1)}, bf16[32,3584]{1,0:T(8,128)(2,1)S(1)}, u32[]{:S(2)}, u32[]{:S(2)}) collective-permute-start(bf16[32,3584]{1,0:T(8,128)(2,1)S(1)} %get-tuple-element.179), channel_id=1, source_target_pairs={{8,0},{9,1},{10,2},{11,3},{20,4},{21,5},{22,6},{23,7},{24,16},{25,... | collective-permute-start | bytes 688136 | tf_op jit(solution)/shard_map/ppermute | solution.py:512
  102.5 23.7 %collective-permute-start.35 = (bf16[32,3584]{1,0:T(8,128)(2,1)S(1)}, bf16[32,3584]{1,0:T(8,128)(2,1)S(1)}, u32[]{:S(2)}, u32[]{:S(2)}) collective-permute-start(bf16[32,3584]{1,0:T(8,128)(2,1)S(1)} %get-tuple-element.180), channel_id=1, source_target_pairs={{24,0},{25,1},{26,2},{27,3},{20,4},{21,5},{22,6},{23,7},{8,16},{9,... | collective-permute-start | bytes 688136 | tf_op jit(solution)/shard_map/ppermute | solution.py:512
  103.8 27.0 %collective-permute-start.34 = (bf16[32,3584]{1,0:T(8,128)(2,1)S(1)}, bf16[32,3584]{1,0:T(8,128)(2,1)S(1)}, u32[]{:S(2)}, u32[]{:S(2)}) collective-permute-start(bf16[32,3584]{1,0:T(8,128)(2,1)S(1)} %total.11.mine_ref), channel_id=1, source_target_pairs={{20,0},{21,1},{22,2},{23,3},{4,16},{5,17},{6,18},{7,19}} | collective-permute-start | bytes 688136 | tf_op jit(solution)/shard_map/ppermute | solution.py:512
  105.2 25.7 %collective-permute-start.32 = (bf16[32,3584]{1,0:T(8,128)(2,1)S(1)}, bf16[32,3584]{1,0:T(8,128)(2,1)S(1)}, u32[]{:S(2)}, u32[]{:S(2)}) collective-permute-start(bf16[32,3584]{1,0:T(8,128)(2,1)S(1)} %total.11.mine_ref), channel_id=1, source_target_pairs={{4,0},{5,1},{6,2},{7,3},{20,16},{21,17},{22,18},{23,19}} | collective-permute-start | bytes 688136 | tf_op jit(solution)/shard_map/ppermute | solution.py:512
  130.9 2.9 %collective-permute-start.39 = (bf16[128,3584]{1,0:T(8,128)(2,1)S(1)}, bf16[128,3584]{1,0:T(8,128)(2,1)S(1)}, u32[]{:S(2)}, u32[]{:S(2)}) collective-permute-start(bf16[128,3584]{1,0:T(8,128)(2,1)S(1)} %stack.116.refs_0_), channel_id=1, source_target_pairs={{0,1},{1,0},{2,3},{3,2},{4,5},{5,4},{6,7},{7,6},{8,9},{9,8},{10,11... | collective-permute-start | bytes 2752520 | tf_op jit(solution)/shard_map/ppermute | solution.py:469
  131.0 2.8 %collective-permute-start.40 = (bf16[32,3584]{1,0:T(8,128)(2,1)S(1)}, bf16[32,3584]{1,0:T(8,128)(2,1)S(1)}, u32[]{:S(2)}, u32[]{:S(2)}) collective-permute-start(bf16[32,3584]{1,0:T(8,128)(2,1)S(1)} %collective-permute-done.31.arrived_ref.refs_2_), channel_id=1, source_target_pairs={{0,1},{1,0},{2,3},{3,2},{4,5},{5,4},{6,7},{7,6},{8,9},{9,8},{10,11... | collective-permute-start | bytes 688136 | tf_op jit(solution)/shard_map/ppermute | solution.py:469
